TPU v7x, 32 devices: a whole 2x2x4 slice. The times are simulated.
32 devices in a mesh: gx: 8 (over z, core), gy: 4 (over y, x).
Axes of the slice: x: 2, y: 2, z: 4, core: 2. Of those that a mesh axis runs over, the one named last changes fastest.
Arguments:
- rhs_leaf: float32 [8, 4, 8, 512], P('gx', 'gy'), may hold values from -6 to 6
- leaf_inv: float32 [8, 4, 4, 128, 128], P('gx', 'gy'), may hold values from -0.5 to 0.5
- leaf_sub: float32 [8, 4, 3, 128, 128], P('gx', 'gy'), may hold values from -0.375 to 0.375
- sep_rhs: float32 [8, 4, 8, 96], P('gx', 'gy'), may hold values from -6 to 6
- interface: int32 [8, 4, 4, 128], P('gx', 'gy'), may hold values from 0 to 511, as said below
- coupling: float32 [8, 4, 4, 128, 512], P('gx', 'gy'), may hold values from -0.125 to 0.125
- factor_one: float32 [8, 4, 16, 512], P('gx', 'gy'), may hold values from -0.25 to 0.25
- factor_two: float32 [8, 4, 16, 256], P('gx', 'gy'), may hold values from -0.375 to 0.375
- factor_three: float32 [8, 4, 32, 256], P('gx', 'gy'), may hold values from -0.375 to 0.375
- factor_four: float32 [8, 4, 32, 128], P('gx', 'gy'), may hold values from -0.5 to 0.5
- link_two: float32 [8, 4, 16, 128], P('gx', 'gy'), may hold values from -0.375 to 0.375
- link_three: float32 [8, 4, 32, 128], P('gx', 'gy'), may hold values from -0.25 to 0.25
- link_four: float32 [8, 4, 32, 128], P('gx', 'gy'), may hold values from -0.25 to 0.25
Outputs:
- leaf_solution: float32 [8, 4, 8, 512], P('gx', 'gy')
- sep_solution: float32 [8, 4, 8, 96], P('gx', 'gy')
Inputs may be any that keep to these rules, and one draw needn't show every extreme that they name: interface[a, c, k-1, n] is a position of a level-k separator, below S_k, and S_k - 1 is reached at every level; positions may repeat within a leaf.
All inputs are finite; a program needn't handle non-finite values.
Results may differ from a plain program's by a relative error of at most 0.00014.
Values sent between devices are 32-bit elements; how exact they have to be, the bound alone decides.
No kernel may reach another device: no remote copies, remote signals or barrier semaphores. Data moves between devices by JAX's collectives and lax.ppermute only.
A program may use at most 64 MiB of HBM per device.

v0:
```python
import jax
import jax.numpy as jnp
from jax import lax
from jax.sharding import PartitionSpec as P

PRECISE = lax.Precision.HIGHEST


def from_partner(value, axis, distance):
    return lax.ppermute(value, axis, [(i, i ^ 1 << distance) for i in range(lax.axis_size(axis))])


def taken_lists(gy_bits, gx_bits):
    first = list(range(gy_bits + gx_bits))
    second = [bit_number for bit_number in first if bit_number != gy_bits + gx_bits - 1]
    third = [bit_number for bit_number in second if bit_number != gy_bits - 1]
    fourth = [bit_number for bit_number in third if bit_number != gy_bits + gx_bits - 2]
    return [first, second, third, fourth]


def rank_in_group(device_index, taken):
    group_rank = jnp.zeros((), jnp.int32)
    for bit_number in sorted(taken, reverse=True):
        group_rank = group_rank * 2 + (device_index >> bit_number & 1)
    return group_rank


def group_total(values, section, taken):
    if section == 0:
        return lax.psum(values, ("gx", "gy"))
    for bit_number in sorted(taken, reverse=True):
        values = values + from_partner(values, ("gx", "gy"), bit_number)
    return values


def leaf_forward(right_side, inverse_blocks, lower_blocks):
    block_size = inverse_blocks.shape[1]
    results = []
    earlier = None
    for counter in range(inverse_blocks.shape[0]):
        current = right_side[:, counter * block_size : (counter + 1) * block_size]
        if counter > 0:
            current = current - jnp.dot(earlier, lower_blocks[counter - 1], precision=PRECISE)
        earlier = jnp.dot(current, inverse_blocks[counter], precision=PRECISE)
        results.append(earlier)
    return jnp.concatenate(results, axis=1)


def leaf_backward(leaf_work, inverse_blocks, lower_blocks):
    block_size = inverse_blocks.shape[1]
    block_count = inverse_blocks.shape[0]
    contract_last = (((1,), (1,)), ((), ()))
    results = [None] * block_count
    later = None
    for counter in reversed(range(block_count)):
        current = leaf_work[:, counter * block_size : (counter + 1) * block_size]
        if counter < block_count - 1:
            current = current - lax.dot_general(
                later, lower_blocks[counter], contract_last, precision=PRECISE
            )
        later = lax.dot_general(current, inverse_blocks[counter], contract_last, precision=PRECISE)
        results[counter] = later
    return jnp.concatenate(results, axis=1)


def local(
    rhs_leaf,
    leaf_inv,
    leaf_sub,
    sep_rhs,
    interface,
    coupling,
    factor_one,
    factor_two,
    factor_three,
    factor_four,
    link_two,
    link_three,
    link_four,
):
    contract_last = (((1,), (1,)), ((), ()))
    gy_bits = lax.axis_size("gy").bit_length() - 1
    gx_bits = lax.axis_size("gx").bit_length() - 1
    sections = taken_lists(gy_bits, gx_bits)
    device_index = lax.axis_index(("gx", "gy"))
    factors = (factor_one[0, 0], factor_two[0, 0], factor_three[0, 0], factor_four[0, 0])
    link_mats = (link_two[0, 0], link_three[0, 0], link_four[0, 0])
    places = interface[0, 0]
    couplings = coupling[0, 0]
    own_rhs = sep_rhs[0, 0]
    inverse_blocks = leaf_inv[0, 0]
    lower_blocks = leaf_sub[0, 0]
    forward = leaf_forward(rhs_leaf[0, 0], inverse_blocks, lower_blocks)
    rhs_count = forward.shape[0]
    offsets = [0]
    for section in range(3):
        offsets.append(offsets[-1] + factors[section].shape[0])
    ranks = [rank_in_group(device_index, taken) for taken in sections]
    own_z = [None] * 4
    for section in (3, 2, 1, 0):
        own_rows, sep_width = factors[section].shape
        partials_in = lax.dot_general(forward, couplings[section], contract_last, precision=PRECISE)
        if section < 3:
            partials_in = partials_in + jnp.dot(
                own_z[section + 1], link_mats[section], precision=PRECISE
            )
        contribution = jnp.zeros((rhs_count, sep_width), jnp.float32)
        own_part = own_rhs[:, offsets[section] : offsets[section] + own_rows]
        contribution = lax.dynamic_update_slice(
            contribution, own_part, (jnp.zeros((), jnp.int32), ranks[section] * own_rows)
        )
        contribution = contribution.at[:, places[section]].add(-partials_in)
        summed = group_total(contribution, section, sections[section])
        own_z[section] = lax.dot_general(summed, factors[section], contract_last, precision=PRECISE)
    full_sep = [None] * 4
    own_x = []
    for section in range(4):
        own_rows = factors[section].shape[0]
        update = own_z[section]
        if section > 0:
            picked = full_sep[section - 1][:, places[section - 1]]
            update = update - lax.dot_general(
                picked, link_mats[section - 1], contract_last, precision=PRECISE
            )
        partial_value = jnp.dot(update, factors[section], precision=PRECISE)
        full_sep[section] = group_total(partial_value, section, sections[section])
        own_x.append(
            lax.dynamic_slice_in_dim(full_sep[section], ranks[section] * own_rows, own_rows, 1)
        )
    leaf_work = forward
    for section in range(4):
        picked = full_sep[section][:, places[section]]
        leaf_work = leaf_work - jnp.dot(picked, couplings[section], precision=PRECISE)
    leaf_solution = leaf_backward(leaf_work, inverse_blocks, lower_blocks)
    sep_solution = jnp.concatenate(own_x, axis=1)
    return (leaf_solution[None, None], sep_solution[None, None])


def solution(mesh):
    in_specs = (
        P("gx", "gy", None, None),
        P("gx", "gy", None, None, None),
        P("gx", "gy", None, None, None),
        P("gx", "gy", None, None),
        P("gx", "gy", None, None),
        P("gx", "gy", None, None, None),
        P("gx", "gy", None, None),
        P("gx", "gy", None, None),
        P("gx", "gy", None, None),
        P("gx", "gy", None, None),
        P("gx", "gy", None, None),
        P("gx", "gy", None, None),
        P("gx", "gy", None, None),
    )
    out_specs = (P("gx", "gy", None, None), P("gx", "gy", None, None))
    return jax.shard_map(local, mesh=mesh, in_specs=in_specs, out_specs=out_specs, check_vma=False)
```

profile of v0, /device:TPU:0, one launch (start us, length us, event | category | flops | bytes accessed | tf_op | source)
XLA Modules:
  0.0 170.0 jit_solution(12722022767741505163)
XLA Ops:
  0.7 0.9 copy.15
  1.6 0.8 fusion.96
  2.4 1.0 fusion.57
  3.4 1.0 convolution_subtract_fusion.7
  4.4 1.0 fusion.50
  5.4 1.0 convolution_subtract_fusion.6
  6.6 1.0 convolution_subtract_fusion.5
  7.8 1.2 fusion.8
  9.2 1.3 scatter_fusion
  10.6 0.5 collective-permute-start
  11.1 0.9 collective-permute-done
  12.0 2.9 %collective-permute-start.1 = (f32[8,128]{0,1:T(8,128)S(1)}, f32[8,128]{0,1:T(8,128)S(1)}, u32[]{:S(2)}, u32[]{:S(2)}) collective-permute-start(f32[8,128]{0,1:T(8,128)S(1)} %add.187), channel_id=1, source_target_pairs={{0,1},{1,0},{2,3},{3,2},{4,5},{5,4},{6,7},{7,6},{8,9},{9,8},{10,11... | collective-permute-start | bytes 12296 | tf_op jit(solution)/shard_map/ppermute | solution.py:10
  14.9 0.3 fusion.14
  15.2 2.1 %collective-permute-done.1 = f32[8,128]{0,1:T(8,128)S(1)} collective-permute-done((f32[8,128]{0,1:T(8,128)S(1)}, f32[8,128]{0,1:T(8,128)S(1)}, u32[]{:S(2)}, u32[]{:S(2)}) %collective-permute-start.1) | collective-permute-done | bytes 4128 | tf_op jit(solution)/shard_map/ppermute | solution.py:10
  17.8 1.3 scatter_fusion.1
  19.1 2.0 %collective-permute-start.2 = (f32[8,256]{0,1:T(8,128)S(1)}, f32[8,256]{0,1:T(8,128)S(1)}, u32[]{:S(2)}, u32[]{:S(2)}) collective-permute-start(f32[8,256]{0,1:T(8,128)S(1)} %scatter_fusion.1), channel_id=1, source_target_pairs={{0,8},{1,9},{2,10},{3,11},{4,12},{5,13},{6,14},{7,15},{8,0},{9,1},... | collective-permute-start | bytes 24584 | tf_op jit(solution)/shard_map/ppermute | solution.py:10
  21.1 3.1 %collective-permute-done.2 = f32[8,256]{0,1:T(8,128)S(1)} collective-permute-done((f32[8,256]{0,1:T(8,128)S(1)}, f32[8,256]{0,1:T(8,128)S(1)}, u32[]{:S(2)}, u32[]{:S(2)}) %collective-permute-start.2) | collective-permute-done | bytes 8224 | tf_op jit(solution)/shard_map/ppermute | solution.py:10
  24.4 0.3 fusion.17
  24.6 1.1 collective-permute-done.3
  25.7 1.8 %collective-permute-start.4 = (f32[8,256]{0,1:T(8,128)S(1)}, f32[8,256]{0,1:T(8,128)S(1)}, u32[]{:S(2)}, u32[]{:S(2)}) collective-permute-start(f32[8,256]{0,1:T(8,128)S(1)} %add.191), channel_id=1, source_target_pairs={{0,1},{1,0},{2,3},{3,2},{4,5},{5,4},{6,7},{7,6},{8,9},{9,8},{10,11... | collective-permute-start | bytes 24584 | tf_op jit(solution)/shard_map/ppermute | solution.py:10
  27.6 3.7 %collective-permute-done.4 = f32[8,256]{0,1:T(8,128)S(1)} collective-permute-done((f32[8,256]{0,1:T(8,128)S(1)}, f32[8,256]{0,1:T(8,128)S(1)}, u32[]{:S(2)}, u32[]{:S(2)}) %collective-permute-start.4) | collective-permute-done | bytes 8224 | tf_op jit(solution)/shard_map/ppermute | solution.py:10
  31.4 0.3 fusion.32
  32.0 1.3 scatter_fusion.2
  33.3 1.9 %collective-permute-start.5 = (f32[8,256]{0,1:T(8,128)S(1)}, f32[8,256]{0,1:T(8,128)S(1)}, u32[]{:S(2)}, u32[]{:S(2)}) collective-permute-start(f32[8,256]{0,1:T(8,128)S(1)} %scatter_fusion.2), channel_id=1, source_target_pairs={{0,8},{1,9},{2,10},{3,11},{4,12},{5,13},{6,14},{7,15},{8,0},{9,1},... | collective-permute-start | bytes 24584 | tf_op jit(solution)/shard_map/ppermute | solution.py:10
  35.2 3.1 %collective-permute-done.5 = f32[8,256]{0,1:T(8,128)S(1)} collective-permute-done((f32[8,256]{0,1:T(8,128)S(1)}, f32[8,256]{0,1:T(8,128)S(1)}, u32[]{:S(2)}, u32[]{:S(2)}) %collective-permute-start.5) | collective-permute-done | bytes 8224 | tf_op jit(solution)/shard_map/ppermute | solution.py:10
  38.4 1.3 collective-permute-done.6
  39.8 1.8 %collective-permute-start.7 = (f32[8,256]{0,1:T(8,128)S(1)}, f32[8,256]{0,1:T(8,128)S(1)}, u32[]{:S(2)}, u32[]{:S(2)}) collective-permute-start(f32[8,256]{0,1:T(8,128)S(1)} %add.195), channel_id=1, source_target_pairs={{0,2},{1,3},{2,0},{3,1},{4,6},{5,7},{6,4},{7,5},{8,10},{9,11},{10,... | collective-permute-start | bytes 24584 | tf_op jit(solution)/shard_map/ppermute | solution.py:10
  41.6 0.3 fusion.20
  42.0 3.5 %collective-permute-done.7 = f32[8,256]{0,1:T(8,128)S(1)} collective-permute-done((f32[8,256]{0,1:T(8,128)S(1)}, f32[8,256]{0,1:T(8,128)S(1)}, u32[]{:S(2)}, u32[]{:S(2)}) %collective-permute-start.7) | collective-permute-done | bytes 8224 | tf_op jit(solution)/shard_map/ppermute | solution.py:10
  45.4 1.8 %collective-permute-start.8 = (f32[8,256]{0,1:T(8,128)S(1)}, f32[8,256]{0,1:T(8,128)S(1)}, u32[]{:S(2)}, u32[]{:S(2)}) collective-permute-start(f32[8,256]{0,1:T(8,128)S(1)} %add.196), channel_id=1, source_target_pairs={{0,1},{1,0},{2,3},{3,2},{4,5},{5,4},{6,7},{7,6},{8,9},{9,8},{10,11... | collective-permute-start | bytes 24584 | tf_op jit(solution)/shard_map/ppermute | solution.py:10
  47.2 3.2 %collective-permute-done.8 = f32[8,256]{0,1:T(8,128)S(1)} collective-permute-done((f32[8,256]{0,1:T(8,128)S(1)}, f32[8,256]{0,1:T(8,128)S(1)}, u32[]{:S(2)}, u32[]{:S(2)}) %collective-permute-start.8) | collective-permute-done | bytes 8224 | tf_op jit(solution)/shard_map/ppermute | solution.py:10
  50.5 0.3 fusion.30
  50.8 0.3 fusion.1
  51.1 1.4 scatter_fusion.3
  52.5 43.5 %psum.14 = f32[8,512]{0,1:T(8,128)S(1)} all-reduce(f32[8,512]{0,1:T(8,128)S(1)} %scatter_fusion.3), channel_id=1, replica_groups=mesh['gx'=8,'gy'=4] {'gx','gy'}, use_global_device_ids=true, to_apply=%region_4.0 | all-reduce | flops 4096 | bytes 32768 | tf_op jit(solution)/shard_map/psum | solution.py:30
  96.0 0.6 fusion.77
  96.7 39.4 %psum.15 = f32[8,512]{1,0:T(8,128)S(1)} all-reduce(f32[8,512]{1,0:T(8,128)S(1)} %fusion.75), channel_id=1, replica_groups=mesh['gx'=8,'gy'=4] {'gx','gy'}, use_global_device_ids=true, to_apply=%region_5.0 | all-reduce | flops 4096 | bytes 32768 | tf_op jit(solution)/shard_map/psum | solution.py:30
  136.3 0.7 gather_fusion
  137.3 0.5 collective-permute-start.9
  137.8 3.2 %collective-permute-done.9 = f32[8,256]{1,0:T(8,128)S(1)} collective-permute-done((f32[8,256]{1,0:T(8,128)S(1)}, f32[8,256]{1,0:T(8,128)S(1)}, u32[]{:S(2)}, u32[]{:S(2)}) %collective-permute-start.9) | collective-permute-done | bytes 8224 | tf_op jit(solution)/shard_map/ppermute | solution.py:10
  141.0 1.2 collective-permute-done.10
  142.2 2.3 %collective-permute-start.11 = (f32[8,256]{1,0:T(8,128)S(1)}, f32[8,256]{1,0:T(8,128)S(1)}, u32[]{:S(2)}, u32[]{:S(2)}) collective-permute-start(f32[8,256]{1,0:T(8,128)S(1)} %add.200), channel_id=1, source_target_pairs={{0,2},{1,3},{2,0},{3,1},{4,6},{5,7},{6,4},{7,5},{8,10},{9,11},{10,... | collective-permute-start | bytes 24584 | tf_op jit(solution)/shard_map/ppermute | solution.py:10
  144.5 1.6 collective-permute-done.11
  146.1 2.0 %collective-permute-start.12 = (f32[8,256]{1,0:T(8,128)S(1)}, f32[8,256]{1,0:T(8,128)S(1)}, u32[]{:S(2)}, u32[]{:S(2)}) collective-permute-start(f32[8,256]{1,0:T(8,128)S(1)} %add.201), channel_id=1, source_target_pairs={{0,1},{1,0},{2,3},{3,2},{4,5},{5,4},{6,7},{7,6},{8,9},{9,8},{10,11... | collective-permute-start | bytes 24584 | tf_op jit(solution)/shard_map/ppermute | solution.py:10
  148.1 1.6 collective-permute-done.12
  149.9 0.7 gather_fusion.1
  150.9 0.5 collective-permute-start.13
  151.4 0.3 convolution_subtract_fusion.1
  151.7 2.9 %collective-permute-done.13 = f32[8,256]{1,0:T(8,128)S(1)} collective-permute-done((f32[8,256]{1,0:T(8,128)S(1)}, f32[8,256]{1,0:T(8,128)S(1)}, u32[]{:S(2)}, u32[]{:S(2)}) %collective-permute-start.13) | collective-permute-done | bytes 8224 | tf_op jit(solution)/shard_map/ppermute | solution.py:10
  154.7 1.1 collective-permute-done.14
  155.8 2.0 %collective-permute-start.15 = (f32[8,256]{1,0:T(8,128)S(1)}, f32[8,256]{1,0:T(8,128)S(1)}, u32[]{:S(2)}, u32[]{:S(2)}) collective-permute-start(f32[8,256]{1,0:T(8,128)S(1)} %add.204), channel_id=1, source_target_pairs={{0,1},{1,0},{2,3},{3,2},{4,5},{5,4},{6,7},{7,6},{8,9},{9,8},{10,11... | collective-permute-start | bytes 24584 | tf_op jit(solution)/shard_map/ppermute | solution.py:10
  157.8 1.6 collective-permute-done.15
  159.5 0.7 gather_fusion.2
  160.6 0.3 fusion.12
  160.9 0.9 collective-permute-done.16
  161.8 2.0 %collective-permute-start.17 = (f32[8,128]{1,0:T(8,128)S(1)}, f32[8,128]{1,0:T(8,128)S(1)}, u32[]{:S(2)}, u32[]{:S(2)}) collective-permute-start(f32[8,128]{1,0:T(8,128)S(1)} %add.206), channel_id=1, source_target_pairs={{0,1},{1,0},{2,3},{3,2},{4,5},{5,4},{6,7},{7,6},{8,9},{9,8},{10,11... | collective-permute-start | bytes 12296 | tf_op jit(solution)/shard_map/ppermute | solution.py:10
  163.8 1.5 collective-permute-done.17
  165.5 0.6 gather_fusion.3
  166.2 0.3 fusion.9
  166.5 0.3 fusion.3
  166.9 0.5 copy-done.3
  167.8 0.2 fusion.45
  168.7 0.7 maximum_bitcast_fusion
  169.3 0.7 maximum_bitcast_fusion.1
  (78 shorter events, 4.9 us)
Async XLA Ops:
  0.6 95.4 %copy-start = (f32[1,1,16,512]{3,2,1,0:T(8,128)S(1)}, f32[1,1,16,512]{3,2,1,0:T(8,128)}, u32[]{:S(2)}) copy-start(f32[1,1,16,512]{3,2,1,0:T(8,128)} %param.19) | copy-start | bytes 98308
  0.6 5.8 %copy-start.2 = (f32[1,1,4,128,128]{4,3,2,1,0:T(8,128)S(1)}, f32[1,1,4,128,128]{4,3,2,1,0:T(8,128)}, u32[]{:S(2)}) copy-start(f32[1,1,4,128,128]{4,3,2,1,0:T(8,128)} %param.14) | copy-start | bytes 786436
  0.7 14.2 %copy-start.1 = (f32[1,1,4,128,512]{4,3,2,1,0:T(8,128)S(1)}, f32[1,1,4,128,512]{4,3,2,1,0:T(8,128)}, u32[]{:S(2)}) copy-start(f32[1,1,4,128,512]{4,3,2,1,0:T(8,128)} %param.18) | copy-start | bytes 3145732
  10.6 1.4 collective-permute-start
  12.0 5.3 %copy-start.6 = (f32[1,1,32,128]{3,2,1,0:T(8,128)S(1)}, f32[1,1,32,128]{3,2,1,0:T(8,128)}, u32[]{:S(2)}) copy-start(f32[1,1,32,128]{3,2,1,0:T(8,128)} %param.22) | copy-start | bytes 49156
  12.0 5.3 %collective-permute-start.1 = (f32[8,128]{0,1:T(8,128)S(1)}, f32[8,128]{0,1:T(8,128)S(1)}, u32[]{:S(2)}, u32[]{:S(2)}) collective-permute-start(f32[8,128]{0,1:T(8,128)S(1)} %add.187), channel_id=1, source_target_pairs={{0,1},{1,0},{2,3},{3,2},{4,5},{5,4},{6,7},{7,6},{8,9},{9,8},{10,11... | collective-permute-start | bytes 12296 | tf_op jit(solution)/shard_map/ppermute | solution.py:10
  15.2 2.4 %copy-start.8 = (f32[1,1,32,128]{3,2,1,0:T(8,128)S(1)}, f32[1,1,32,128]{3,2,1,0:T(8,128)}, u32[]{:S(2)}) copy-start(f32[1,1,32,128]{3,2,1,0:T(8,128)} %param.25) | copy-start | bytes 49156
  19.1 5.1 %collective-permute-start.2 = (f32[8,256]{0,1:T(8,128)S(1)}, f32[8,256]{0,1:T(8,128)S(1)}, u32[]{:S(2)}, u32[]{:S(2)}) collective-permute-start(f32[8,256]{0,1:T(8,128)S(1)} %scatter_fusion.1), channel_id=1, source_target_pairs={{0,8},{1,9},{2,10},{3,11},{4,12},{5,13},{6,14},{7,15},{8,0},{9,1},... | collective-permute-start | bytes 24584 | tf_op jit(solution)/shard_map/ppermute | solution.py:10
  24.3 1.4 collective-permute-start.3
  25.7 5.6 %collective-permute-start.4 = (f32[8,256]{0,1:T(8,128)S(1)}, f32[8,256]{0,1:T(8,128)S(1)}, u32[]{:S(2)}, u32[]{:S(2)}) collective-permute-start(f32[8,256]{0,1:T(8,128)S(1)} %add.191), channel_id=1, source_target_pairs={{0,1},{1,0},{2,3},{3,2},{4,5},{5,4},{6,7},{7,6},{8,9},{9,8},{10,11... | collective-permute-start | bytes 24584 | tf_op jit(solution)/shard_map/ppermute | solution.py:10
  27.6 3.8 %copy-start.4 = (f32[1,1,32,256]{3,2,1,0:T(8,128)S(1)}, f32[1,1,32,256]{3,2,1,0:T(8,128)}, u32[]{:S(2)}) copy-start(f32[1,1,32,256]{3,2,1,0:T(8,128)} %param.21) | copy-start | bytes 98308
  27.6 4.1 %copy-start.7 = (f32[1,1,32,128]{3,2,1,0:T(8,128)S(1)}, f32[1,1,32,128]{3,2,1,0:T(8,128)}, u32[]{:S(2)}) copy-start(f32[1,1,32,128]{3,2,1,0:T(8,128)} %param.24) | copy-start | bytes 49156
  33.3 5.0 %collective-permute-start.5 = (f32[8,256]{0,1:T(8,128)S(1)}, f32[8,256]{0,1:T(8,128)S(1)}, u32[]{:S(2)}, u32[]{:S(2)}) collective-permute-start(f32[8,256]{0,1:T(8,128)S(1)} %scatter_fusion.2), channel_id=1, source_target_pairs={{0,8},{1,9},{2,10},{3,11},{4,12},{5,13},{6,14},{7,15},{8,0},{9,1},... | collective-permute-start | bytes 24584 | tf_op jit(solution)/shard_map/ppermute | solution.py:10
  38.3 1.4 collective-permute-start.6
  39.8 5.6 %collective-permute-start.7 = (f32[8,256]{0,1:T(8,128)S(1)}, f32[8,256]{0,1:T(8,128)S(1)}, u32[]{:S(2)}, u32[]{:S(2)}) collective-permute-start(f32[8,256]{0,1:T(8,128)S(1)} %add.195), channel_id=1, source_target_pairs={{0,2},{1,3},{2,0},{3,1},{4,6},{5,7},{6,4},{7,5},{8,10},{9,11},{10,... | collective-permute-start | bytes 24584 | tf_op jit(solution)/shard_map/ppermute | solution.py:10
  45.4 5.1 %copy-start.5 = (f32[1,1,16,256]{3,2,1,0:T(8,128)S(1)}, f32[1,1,16,256]{3,2,1,0:T(8,128)}, u32[]{:S(2)}) copy-start(f32[1,1,16,256]{3,2,1,0:T(8,128)} %param.20) | copy-start | bytes 49156
  45.4 5.0 %collective-permute-start.8 = (f32[8,256]{0,1:T(8,128)S(1)}, f32[8,256]{0,1:T(8,128)S(1)}, u32[]{:S(2)}, u32[]{:S(2)}) collective-permute-start(f32[8,256]{0,1:T(8,128)S(1)} %add.196), channel_id=1, source_target_pairs={{0,1},{1,0},{2,3},{3,2},{4,5},{5,4},{6,7},{7,6},{8,9},{9,8},{10,11... | collective-permute-start | bytes 24584 | tf_op jit(solution)/shard_map/ppermute | solution.py:10
  47.2 3.6 %copy-start.9 = (f32[1,1,16,128]{3,2,1,0:T(8,128)S(1)}, f32[1,1,16,128]{3,2,1,0:T(8,128)}, u32[]{:S(2)}) copy-start(f32[1,1,16,128]{3,2,1,0:T(8,128)} %param.23) | copy-start | bytes 24580
  137.3 3.7 %collective-permute-start.9 = (f32[8,256]{1,0:T(8,128)S(1)}, f32[8,256]{1,0:T(8,128)S(1)}, u32[]{:S(2)}, u32[]{:S(2)}) collective-permute-start(f32[8,256]{1,0:T(8,128)S(1)} %fusion.82), channel_id=1, source_target_pairs={{0,8},{1,9},{2,10},{3,11},{4,12},{5,13},{6,14},{7,15},{8,0},{9,1},... | collective-permute-start | bytes 24584 | tf_op jit(solution)/shard_map/ppermute | solution.py:10
  141.0 1.2 collective-permute-start.10
  142.2 3.9 %collective-permute-start.11 = (f32[8,256]{1,0:T(8,128)S(1)}, f32[8,256]{1,0:T(8,128)S(1)}, u32[]{:S(2)}, u32[]{:S(2)}) collective-permute-start(f32[8,256]{1,0:T(8,128)S(1)} %add.200), channel_id=1, source_target_pairs={{0,2},{1,3},{2,0},{3,1},{4,6},{5,7},{6,4},{7,5},{8,10},{9,11},{10,... | collective-permute-start | bytes 24584 | tf_op jit(solution)/shard_map/ppermute | solution.py:10
  146.1 3.7 %collective-permute-start.12 = (f32[8,256]{1,0:T(8,128)S(1)}, f32[8,256]{1,0:T(8,128)S(1)}, u32[]{:S(2)}, u32[]{:S(2)}) collective-permute-start(f32[8,256]{1,0:T(8,128)S(1)} %add.201), channel_id=1, source_target_pairs={{0,1},{1,0},{2,3},{3,2},{4,5},{5,4},{6,7},{7,6},{8,9},{9,8},{10,11... | collective-permute-start | bytes 24584 | tf_op jit(solution)/shard_map/ppermute | solution.py:10
  150.9 3.7 %collective-permute-start.13 = (f32[8,256]{1,0:T(8,128)S(1)}, f32[8,256]{1,0:T(8,128)S(1)}, u32[]{:S(2)}, u32[]{:S(2)}) collective-permute-start(f32[8,256]{1,0:T(8,128)S(1)} %fusion.79), channel_id=1, source_target_pairs={{0,8},{1,9},{2,10},{3,11},{4,12},{5,13},{6,14},{7,15},{8,0},{9,1},... | collective-permute-start | bytes 24584 | tf_op jit(solution)/shard_map/ppermute | solution.py:10
  154.6 1.2 collective-permute-start.14
  155.8 3.7 %collective-permute-start.15 = (f32[8,256]{1,0:T(8,128)S(1)}, f32[8,256]{1,0:T(8,128)S(1)}, u32[]{:S(2)}, u32[]{:S(2)}) collective-permute-start(f32[8,256]{1,0:T(8,128)S(1)} %add.204), channel_id=1, source_target_pairs={{0,1},{1,0},{2,3},{3,2},{4,5},{5,4},{6,7},{7,6},{8,9},{9,8},{10,11... | collective-permute-start | bytes 24584 | tf_op jit(solution)/shard_map/ppermute | solution.py:10
  160.6 1.2 collective-permute-start.16
  161.8 3.6 %collective-permute-start.17 = (f32[8,128]{1,0:T(8,128)S(1)}, f32[8,128]{1,0:T(8,128)S(1)}, u32[]{:S(2)}, u32[]{:S(2)}) collective-permute-start(f32[8,128]{1,0:T(8,128)S(1)} %add.206), channel_id=1, source_target_pairs={{0,1},{1,0},{2,3},{3,2},{4,5},{5,4},{6,7},{7,6},{8,9},{9,8},{10,11... | collective-permute-start | bytes 12296 | tf_op jit(solution)/shard_map/ppermute | solution.py:10
  166.4 0.9 copy-start.3
where the time goes:
time: 171 us; the launch traced here: 170 us
  blocking collectives  82.9 us (48%)
  waiting for transfers between devices  37.7 us (22%)
  starting transfers between devices  22.2 us (13%)
  matrix products  13.4 us (8%)
  other arithmetic  7.61 us (4%)
  local copies, waits for them, and re-layouts  5.19 us (3%)
    psum x2, blocking collectives, group_total(): return lax.psum(values, ('gx', 'gy'))  82.9 us
    ppermute x18, waiting for transfers between devices, from_partner(): lax.ppermute(value, axis, [(i, i ^ 1 << distance) for i in range(lax.axis...  37.7 us
    ppermute x18, starting transfers between devices, from_partner(): lax.ppermute(value, axis, [(i, i ^ 1 << distance) for i in range(lax.axis...  22.2 us
    scatter-add x4, other arithmetic, local(): contribution = contribution.at[:, places[section]].add(-partials_in)  5.3 us
  transfers between devices with their start and end apart: 18, of which 18 were waited for; matrix products, arithmetic and copies ran while one was open for 1% of the time, Pallas kernels for 0%

commit v1 on v0

--- a/solution.py
+++ b/solution.py
@@ -1,9 +1,16 @@
+import functools
+
 import jax
 import jax.numpy as jnp
 from jax import lax
+from jax.experimental import pallas as pl
+from jax.experimental.pallas import tpu as pltpu
 from jax.sharding import PartitionSpec as P
 
 PRECISE = lax.Precision.HIGHEST
+LANES = 128
+GATHER_BYTES = 8 * 2**20
+VMEM_BYTES = 24 * 2**20
 
 
 def from_partner(value, axis, distance):
@@ -63,7 +70,7 @@
     return jnp.concatenate(results, axis=1)
 
 
-def local(
+def level_by_level(
     rhs_leaf,
     leaf_inv,
     leaf_sub,
@@ -136,6 +143,287 @@
     return (leaf_solution[None, None], sep_solution[None, None])
 
 
+def halves(value):
+    high = value.astype(jnp.bfloat16)
+    low = (value - high.astype(jnp.float32)).astype(jnp.bfloat16)
+    return high, low
+
+
+def few_rows(value):
+    high = value.astype(jnp.bfloat16).astype(jnp.float32)
+    return jnp.concatenate([high, value - high], axis=0).astype(jnp.bfloat16)
+
+
+def times(left, right, transposed):
+    dims = (((1,), (1 if transposed else 0,)), ((), ()))
+    stacked = few_rows(left)
+    total = None
+    for piece in right:
+        term = lax.dot_general(stacked, piece, dims, preferred_element_type=jnp.float32)
+        total = term if total is None else total + term
+    rows = left.shape[0]
+    return total[:rows] + total[rows:]
+
+
+def one_hot(positions, height):
+    rows = lax.broadcasted_iota(jnp.int32, (height, positions.shape[1]), 0)
+    return (rows == positions).astype(jnp.float32).astype(jnp.bfloat16)
+
+
+def wide(ref, start, rows, chunks):
+    pieces = [ref[start + chunk * rows : start + (chunk + 1) * rows, :] for chunk in range(chunks)]
+    return pieces[0] if chunks == 1 else jnp.concatenate(pieces, axis=1)
+
+
+def vmem_call(body, outs, *operands):
+    out_shape = [jax.ShapeDtypeStruct(shape, dtype) for shape, dtype in outs]
+    return pl.pallas_call(
+        body,
+        out_shape=out_shape,
+        in_specs=[pl.BlockSpec(memory_space=pltpu.VMEM)] * len(operands),
+        out_specs=[pl.BlockSpec(memory_space=pltpu.VMEM)] * len(outs),
+        compiler_params=pltpu.CompilerParams(vmem_limit_bytes=VMEM_BYTES),
+    )(*operands)
+
+
+def packed_layout(factors, link_mats):
+    starts = {}
+    at = 0
+    for name, rows in (
+        ("f0", factors[0].shape[0] * (factors[0].shape[1] // LANES)),
+        ("f1", factors[1].shape[0] * (factors[1].shape[1] // LANES)),
+        ("l1", link_mats[0].shape[0]),
+        ("places", 8),
+        ("f2", factors[2].shape[0] * (factors[2].shape[1] // LANES)),
+        ("l2", link_mats[1].shape[0]),
+        ("f3", factors[3].shape[0] * (factors[3].shape[1] // LANES)),
+        ("l3", link_mats[2].shape[0]),
+    ):
+        starts[name] = at
+        at += rows
+    return starts, at
+
+
+def pack_body(starts, f0, f1, f2, f3, l1, l2, l3, places, out):
+    for name, ref in (("f0", f0), ("f1", f1), ("f2", f2), ("f3", f3)):
+        rows, width = ref.shape[2:]
+        for chunk in range(width // LANES):
+            at = starts[name] + chunk * rows
+            out[at : at + rows, :] = ref[0, 0, :, chunk * LANES : (chunk + 1) * LANES]
+    for name, ref in (("l1", l1), ("l2", l2), ("l3", l3)):
+        out[starts[name] : starts[name] + ref.shape[2], :] = ref[0, 0]
+    numbers = places[0, 0].astype(jnp.float32)
+    out[starts["places"] : starts["places"] + 8, :] = jnp.concatenate([numbers, numbers], axis=0)
+
+
+def own_targets(sizes, owned, taken):
+    device_index = lax.axis_index("gx") * lax.axis_size("gy") + lax.axis_index("gy")
+    columns = lax.broadcasted_iota(jnp.int32, (1, sum(owned)), 1)
+    target = columns
+    before = 0
+    level_start = 0
+    for section in range(4):
+        rank = jnp.int32(0)
+        for bit_number in sorted(taken[section], reverse=True):
+            rank = rank * 2 + ((device_index >> bit_number) & 1)
+        here = columns - before + (level_start + rank * owned[section])
+        target = jnp.where(columns >= before, here, target)
+        before += owned[section]
+        level_start += sizes[section]
+    return target
+
+
+def forward_body(sizes, owned, taken, rhs, inverse, lower, sep_rhs, places, coupling, forward, sums):
+    count, block = inverse.shape[2], inverse.shape[3]
+    earlier = None
+    for counter in range(count):
+        current = rhs[0, 0, :, counter * block : (counter + 1) * block]
+        if counter > 0:
+            current = current - times(earlier, halves(lower[0, 0, counter - 1]), False)
+        earlier = times(current, halves(inverse[0, 0, counter]), False)
+        forward[:, counter * block : (counter + 1) * block] = earlier
+    whole = forward[...]
+    own = times(sep_rhs[0, 0], [one_hot(own_targets(sizes, owned, taken), sum(sizes))], True)
+    at = 0
+    for section in range(4):
+        term = times(whole, halves(coupling[0, 0, section]), True)
+        spread = times(term, [one_hot(places[0, 0, section : section + 1, :], sizes[section])], True)
+        sums[:, at : at + sizes[section]] = own[:, at : at + sizes[section]] - spread
+        at += sizes[section]
+
+
+def gather_body(section, starts, rows, size, above, strides, *refs):
+    outs = refs[len(strides) :]
+    at = 0
+    for ref, (members, stride) in zip(refs, strides):
+        for member in range(members):
+            base = member * stride
+            factor = wide(ref, base + starts["f%d" % section], rows, size // LANES)
+            outs[0][at : at + rows, :], outs[1][at : at + rows, :] = halves(factor)
+            if section > 0:
+                begin = base + starts["l%d" % section]
+                link = ref[begin : begin + rows, :]
+                row = base + starts["places"] + section - 1
+                positions = ref[row : row + 1, :].astype(jnp.int32)
+                linked = times(link, [one_hot(positions, above)], True)
+                outs[2][at : at + rows, :], outs[3][at : at + rows, :] = halves(linked)
+            at += rows
+
+
+def eliminate_body(size, above, mine, theirs, f_high, f_low, m_high, m_low, sums, found):
+    width = mine.shape[1]
+    total = mine[...] + theirs[...]
+    solved = times(total[:, width - size :], [f_high[...], f_low[...]], True)
+    found[...] = solved
+    sums[:, : width - size] = total[:, : width - size]
+    rest = total[:, width - size - above : width - size]
+    sums[:, width - size - above :] = rest - times(solved, [m_high[...], m_low[...]], False)
+
+
+def top_body(mine, theirs, f_high, f_low, partial):
+    total = mine[...] + theirs[...]
+    pieces = [f_high[...], f_low[...]]
+    partial[...] = times(times(total, pieces, True), pieces, False)
+
+
+def backward_body(
+    sizes, owned, taken, mine, theirs, z1, z2, z3,
+    f1h, f1l, m1h, m1l, f2h, f2l, m2h, m2l, f3h, f3l, m3h, m3l,
+    forward, coupling, places, inverse, lower, leaf, sep,
+):
+    solved = [mine[...] + theirs[...]]
+    levels = (
+        (z1, f1h, f1l, m1h, m1l),
+        (z2, f2h, f2l, m2h, m2l),
+        (z3, f3h, f3l, m3h, m3l),
+    )
+    for found, f_high, f_low, m_high, m_low in levels:
+        update = found[...] - times(solved[-1], [m_high[...], m_low[...]], True)
+        solved.append(times(update, [f_high[...], f_low[...]], False))
+    everything = jnp.concatenate(solved, axis=1)
+    sep[0, 0] = times(everything, [one_hot(own_targets(sizes, owned, taken), sum(sizes))], False)
+    work = forward[...]
+    for section in range(4):
+        picked = times(solved[section], [one_hot(places[0, 0, section : section + 1, :], sizes[section])], False)
+        work = work - times(picked, halves(coupling[0, 0, section]), False)
+    count, block = inverse.shape[2], inverse.shape[3]
+    later = None
+    for counter in reversed(range(count)):
+        current = work[:, counter * block : (counter + 1) * block]
+        if counter < count - 1:
+            current = current - times(later, halves(lower[0, 0, counter]), True)
+        later = times(current, halves(inverse[0, 0, counter]), True)
+        leaf[0, 0, :, counter * block : (counter + 1) * block] = later
+
+
+def gathered(
+    rhs_leaf,
+    leaf_inv,
+    leaf_sub,
+    sep_rhs,
+    interface,
+    coupling,
+    factor_one,
+    factor_two,
+    factor_three,
+    factor_four,
+    link_two,
+    link_three,
+    link_four,
+):
+    gy_bits = lax.axis_size("gy").bit_length() - 1
+    gx_bits = lax.axis_size("gx").bit_length() - 1
+    taken = taken_lists(gy_bits, gx_bits)
+    factors = [array.reshape(array.shape[2:]) for array in (factor_one, factor_two, factor_three, factor_four)]
+    links = [array.reshape(array.shape[2:]) for array in (link_two, link_three, link_four)]
+    sizes = tuple(factor.shape[1] for factor in factors)
+    owned = tuple(factor.shape[0] for factor in factors)
+    starts, height = packed_layout(factors, links)
+    heights = {3: height, 2: starts["f3"], 1: starts["f2"]}
+    axes = ("gx", "gy")
+    core = gy_bits
+    rhs_count = rhs_leaf.shape[2]
+
+    (packed,) = vmem_call(
+        functools.partial(pack_body, starts),
+        [((height, LANES), jnp.float32)],
+        factor_one, factor_two, factor_three, factor_four, link_two, link_three, link_four, interface,
+    )
+    held = [packed]
+    counts = [1]
+    both = [packed, from_partner(packed, axes, core)]
+    strides = [(1, height), (1, height)]
+
+    def widen(bit_number, rows):
+        message = [
+            block.reshape(members, -1, LANES)[:, :rows].reshape(members * rows, LANES)
+            for block, members in zip(held, counts)
+        ]
+        message = message[0] if len(message) == 1 else jnp.concatenate(message, axis=0)
+        arrived = from_partner(message, axes, bit_number)
+        members = sum(counts)
+        held.append(arrived)
+        counts.append(members)
+        both.extend([arrived, from_partner(arrived, axes, core)])
+        strides.extend([(members, rows)] * 2)
+
+    def level(section):
+        rows, size = factors[section].shape
+        above = sizes[section - 1] if section > 0 else 0
+        members = sum(count for count, _ in strides)
+        outs = [((members * rows, size), jnp.bfloat16)] * 2
+        if section > 0:
+            outs = outs + [((members * rows, above), jnp.bfloat16)] * 2
+        body = functools.partial(gather_body, section, starts, rows, size, above, tuple(strides))
+        return vmem_call(body, outs, *both)
+
+    forward, sums = vmem_call(
+        functools.partial(forward_body, sizes, owned, taken),
+        [((rhs_count, rhs_leaf.shape[3]), jnp.float32), ((rhs_count, sum(sizes)), jnp.float32)],
+        rhs_leaf, leaf_inv, leaf_sub, sep_rhs, interface, coupling,
+    )
+
+    inner = [bit_number for bit_number in taken[3] if bit_number != core]
+    steps = {3: inner, 2: [gy_bits + gx_bits - 2], 1: [gy_bits - 1], 0: [gy_bits + gx_bits - 1]}
+    sums = sums + from_partner(sums, axes, core)
+    tables = [None] * 4
+    found = [None] * 4
+    for section in (3, 2, 1):
+        for position, bit_number in enumerate(steps[section]):
+            widen(bit_number, heights[section])
+            theirs = from_partner(sums, axes, bit_number)
+            if position < len(steps[section]) - 1:
+                sums = sums + theirs
+        tables[section] = level(section)
+        size, above = sizes[section], sizes[section - 1]
+        sums, found[section] = vmem_call(
+            functools.partial(eliminate_body, size, above),
+            [((rhs_count, sums.shape[1] - size), jnp.float32), ((rhs_count, size), jnp.float32)],
+            sums, theirs, *tables[section],
+        )
+    tables[0] = level(0)
+    theirs = from_partner(sums, axes, steps[0][0])
+    (partial,) = vmem_call(top_body, [((rhs_count, sizes[0]), jnp.float32)], sums, theirs, *tables[0])
+    theirs = from_partner(partial, axes, steps[0][0])
+    leaf, sep = vmem_call(
+        functools.partial(backward_body, sizes, owned, taken),
+        [(rhs_leaf.shape, jnp.float32), (sep_rhs.shape, jnp.float32)],
+        partial, theirs, *found[1:], *tables[1], *tables[2], *tables[3],
+        forward, coupling, interface, leaf_inv, leaf_sub,
+    )
+    return (leaf, sep)
+
+
+def local(*arrays):
+    gathered_bytes = 0
+    bits = lax.axis_size("gy").bit_length() + lax.axis_size("gx").bit_length() - 2
+    for level, array in enumerate(arrays[6:10]):
+        gathered_bytes += array.size * 4 << (bits - level)
+    if gathered_bytes > GATHER_BYTES:
+        return level_by_level(*arrays)
+    return gathered(*arrays)
+
+
 def solution(mesh):
     in_specs = (
         P("gx", "gy", None, None),

time: 171 us -> 57.4 us (0.34)
  blocking collectives: 82.9 us -> 0 us
  matrix products: 13.4 us -> 0 us
  waiting for transfers between devices: 37.7 us -> 24.5 us
  Pallas kernels: 0 us -> 8.71 us
  other arithmetic: 7.61 us -> 0.04 us
  starting transfers between devices: 22.2 us -> 16.9 us
    psum x2 -> x0, blocking collectives: 82.9 us -> none  [group_total(): return lax.psum(values, ('gx', 'gy'))]
    dot_general x36 -> x0, matrix products: 13.4 us -> none  [the longest x3 3.04 us: leaf_forward(): jnp.dot(earlier, lower_blocks[counter - 1], precision=PRECISE)]
    ppermute x18 -> x13, waiting for transfers between devices: 37.7 us -> 24.5 us  [from_partner(): lax.ppermute(value, axis, [(i, i ^ 1 << distance) for i in range(lax.axis...]
    pallas_call x0 -> x11, Pallas kernels: none -> 8.71 us  [vmem_call(): pl.pallas_call(body, out_shape=out_shape, in_specs=[pl.BlockSpec(memory_s...]
    ppermute x18 -> x13, starting transfers between devices: 22.2 us -> 16.9 us  [from_partner(): lax.ppermute(value, axis, [(i, i ^ 1 << distance) for i in range(lax.axis...]
    scatter-add x4 -> x0, other arithmetic: 5.3 us -> none  [local(): contribution = contribution.at[:, places[section]].add(-partials_in)]
    unnamed x21 -> x28, local copies, waits for them, and re-layouts: 1.41 us -> 5.79 us
    gather x4 -> x0, local copies, waits for them, and re-layouts: 2.59 us -> none  [local(): picked = full_sep[section][:, places[section]]]
  transfers between devices with their start and end apart: 18 -> 13, of which waited for: 18 -> 9; matrix products, arithmetic and copies ran while one was open for 1% -> 0% of each run, Pallas kernels for 0% -> 7%
where the time goes in v1:
time: 57.4 us; the launch traced here: 56.8 us
  waiting for transfers between devices  24.5 us (43%)
  starting transfers between devices  16.9 us (29%)
  Pallas kernels  8.71 us (15%)
  local copies, waits for them, and re-layouts  5.83 us (10%)
  between operations  0.8 us (1%)
    ppermute x13, waiting for transfers between devices, from_partner(): lax.ppermute(value, axis, [(i, i ^ 1 << distance) for i in range(lax.axis...  24.5 us
    ppermute x13, starting transfers between devices, from_partner(): lax.ppermute(value, axis, [(i, i ^ 1 << distance) for i in range(lax.axis...  16.9 us
    pallas_call x11, Pallas kernels, vmem_call(): pl.pallas_call(body, out_shape=out_shape, in_specs=[pl.BlockSpec(memory_s...  8.71 us
    unnamed x28, local copies, waits for them, and re-layouts  5.79 us
  transfers between devices with their start and end apart: 13, of which 9 were waited for; matrix products, arithmetic and copies ran while one was open for 0% of the time, Pallas kernels for 7%

profile of v1, /device:TPU:0, one launch (start us, length us, event | category | flops | bytes accessed | tf_op | source)
XLA Modules:
  0.0 56.8 jit_solution(11931555259945330148)
XLA Ops:
  0.6 0.0 copy-start.3
  0.6 0.7 %copy-done.3 = f32[1,1,16,512]{3,2,1,0:T(8,128)S(1)} copy-done((f32[1,1,16,512]{3,2,1,0:T(8,128)S(1)}, f32[1,1,16,512]{3,2,1,0:T(8,128)}, u32[]{:S(2)}) %copy-start.3) | copy-done | bytes 32792
  1.4 0.0 copy-start.4
  1.4 0.8 %copy-done.4 = f32[1,1,32,256]{3,2,1,0:T(8,128)S(1)} copy-done((f32[1,1,32,256]{3,2,1,0:T(8,128)S(1)}, f32[1,1,32,256]{3,2,1,0:T(8,128)}, u32[]{:S(2)}) %copy-start.4) | copy-done | bytes 32792
  2.2 0.0 copy-start.5
  2.2 0.7 %copy-done.5 = s32[1,1,4,128]{3,2,1,0:T(4,128)S(1)} copy-done((s32[1,1,4,128]{3,2,1,0:T(4,128)S(1)}, s32[1,1,4,128]{3,2,1,0:T(4,128)}, u32[]{:S(2)}) %copy-start.5) | copy-done | bytes 2072
  2.8 0.0 copy-start.8
  2.8 0.7 %copy-done.8 = f32[1,1,16,256]{3,2,1,0:T(8,128)S(1)} copy-done((f32[1,1,16,256]{3,2,1,0:T(8,128)S(1)}, f32[1,1,16,256]{3,2,1,0:T(8,128)}, u32[]{:S(2)}) %copy-start.8) | copy-done | bytes 16408
  3.6 0.0 copy-start.9
  3.6 0.7 %copy-done.9 = f32[1,1,32,128]{3,2,1,0:T(8,128)S(1)} copy-done((f32[1,1,32,128]{3,2,1,0:T(8,128)S(1)}, f32[1,1,32,128]{3,2,1,0:T(8,128)}, u32[]{:S(2)}) %copy-start.9) | copy-done | bytes 16408
  4.3 0.0 copy-start.10
  4.3 0.7 %copy-done.10 = f32[1,1,32,128]{3,2,1,0:T(8,128)S(1)} copy-done((f32[1,1,32,128]{3,2,1,0:T(8,128)S(1)}, f32[1,1,32,128]{3,2,1,0:T(8,128)}, u32[]{:S(2)}) %copy-start.10) | copy-done | bytes 16408
  5.0 0.0 copy-start.11
  5.0 0.7 %copy-done.11 = f32[1,1,32,128]{3,2,1,0:T(8,128)S(1)} copy-done((f32[1,1,32,128]{3,2,1,0:T(8,128)S(1)}, f32[1,1,32,128]{3,2,1,0:T(8,128)}, u32[]{:S(2)}) %copy-start.11) | copy-done | bytes 16408
  5.7 0.0 copy-start.12
  5.7 0.7 %copy-done.12 = f32[1,1,16,128]{3,2,1,0:T(8,128)S(1)} copy-done((f32[1,1,16,128]{3,2,1,0:T(8,128)S(1)}, f32[1,1,16,128]{3,2,1,0:T(8,128)}, u32[]{:S(2)}) %copy-start.12) | copy-done | bytes 8216
  6.4 0.0 copy-start
  6.4 3.0 %collective-permute-start.3 = (f32[280,128]{1,0:T(8,128)S(1)}, f32[280,128]{1,0:T(8,128)S(1)}, u32[]{:S(2)}, u32[]{:S(2)}) collective-permute-start(f32[280,128]{1,0:T(8,128)S(1)} %shard_map.141.refs_0_), channel_id=1, source_target_pairs={{0,1},{1,0},{2,3},{3,2},{4,5},{5,4},{6,7},{7,6},{8,9},{9,8},{10,11... | collective-permute-start | bytes 430088 | tf_op jit(solution)/shard_map/ppermute | solution.py:17
  9.4 3.7 %collective-permute-done.3.refs_2_ = f32[280,128]{1,0:T(8,128)S(1)} collective-permute-done((f32[280,128]{1,0:T(8,128)S(1)}, f32[280,128]{1,0:T(8,128)S(1)}, u32[]{:S(2)}, u32[]{:S(2)}) %collective-permute-start.3) | collective-permute-done | bytes 143392 | tf_op jit(solution)/shard_map/ppermute | solution.py:17
  13.2 1.9 %collective-permute-start.6 = (f32[432,128]{1,0:T(8,128)S(1)}, f32[432,128]{1,0:T(8,128)S(1)}, u32[]{:S(2)}, u32[]{:S(2)}) collective-permute-start(f32[432,128]{1,0:T(8,128)S(1)} %pad_maximum_fusion.1), channel_id=1, source_target_pairs={{0,8},{1,9},{2,10},{3,11},{4,12},{5,13},{6,14},{7,15},{8,0},{9,1},... | collective-permute-start | bytes 663560 | tf_op jit(solution)/shard_map/ppermute | solution.py:17
  15.1 4.8 %collective-permute-done.6.refs_4_ = f32[432,128]{1,0:T(8,128)S(1)} collective-permute-done((f32[432,128]{1,0:T(8,128)S(1)}, f32[432,128]{1,0:T(8,128)S(1)}, u32[]{:S(2)}, u32[]{:S(2)}) %collective-permute-start.6) | collective-permute-done | bytes 221216 | tf_op jit(solution)/shard_map/ppermute | solution.py:17
  19.9 0.0 copy-start.1
  19.9 0.0 copy-start.2
  19.9 0.0 copy-start.6
  19.9 0.0 copy-start.7
  20.0 0.0 copy-start.13
  20.0 1.5 %collective-permute-start.9 = (f32[480,128]{1,0:T(8,128)S(1)}, f32[480,128]{1,0:T(8,128)S(1)}, u32[]{:S(2)}, u32[]{:S(2)}) collective-permute-start(f32[480,128]{1,0:T(8,128)S(1)} %pad_maximum_fusion), channel_id=1, source_target_pairs={{0,2},{1,3},{2,0},{3,1},{4,6},{5,7},{6,4},{7,5},{8,10},{9,11},{10,... | collective-permute-start | bytes 737288 | tf_op jit(solution)/shard_map/ppermute | solution.py:17
  21.5 0.0 collective-permute-start.7
  21.5 4.8 %collective-permute-done.9.refs_6_ = f32[480,128]{1,0:T(8,128)S(1)} collective-permute-done((f32[480,128]{1,0:T(8,128)S(1)}, f32[480,128]{1,0:T(8,128)S(1)}, u32[]{:S(2)}, u32[]{:S(2)}) %collective-permute-start.9) | collective-permute-done | bytes 245792 | tf_op jit(solution)/shard_map/ppermute | solution.py:17
  26.3 0.0 collective-permute-start.10
  26.3 0.5 collective-permute-start.2
  26.8 0.0 collective-permute-start.4
  26.8 0.0 copy-done
  26.8 0.0 copy-done.1
  26.8 0.0 copy-done.2
  26.8 0.0 copy-done.6
  26.8 0.0 copy-done.7
  26.8 0.0 copy-done.13
  26.8 2.1 %shard_map.140 = (f32[8,512]{1,0:T(8,128)S(1)}, f32[8,1152]{1,0:T(8,128)S(1)}) custom-call(f32[1,1,8,512]{3,2,1,0:T(8,128)S(1)} %copy-done.7, f32[1,1,4,128,128]{4,3,2,1,0:T(8,128)S(1)} %copy-done.1, f32[1,1,3,128,128]{4,3,2,1,0:T(8,128)S(1)} %copy-done.2, f32[1,1,8,96]{3,2,1,0:T(8,128)S(1)} %copy-done.13, s32[1,1,4,128]{3,2,1,0:T(4,128)S(1)} %copy-done.6, ...), custom_call_target="tpu_custom_call" | custom-call | tf_op jit(solution)/shard_map/pallas_call | solution.py:180
  28.9 0.5 collective-permute-start
  29.4 0.9 %collective-permute-done = f32[8,1152]{1,0:T(8,128)S(1)} collective-permute-done((f32[8,1152]{1,0:T(8,128)S(1)}, f32[8,1152]{1,0:T(8,128)S(1)}, u32[]{:S(2)}, u32[]{:S(2)}) %collective-permute-start) | collective-permute-done | bytes 36896 | tf_op jit(solution)/shard_map/ppermute | solution.py:17
  30.3 1.4 %collective-permute-start.1 = (f32[8,1152]{1,0:T(8,128)S(1)}, f32[8,1152]{1,0:T(8,128)S(1)}, u32[]{:S(2)}, u32[]{:S(2)}) collective-permute-start(f32[8,1152]{1,0:T(8,128)S(1)} %add.3.mine), channel_id=1, source_target_pairs={{0,1},{1,0},{2,3},{3,2},{4,5},{5,4},{6,7},{7,6},{8,9},{9,8},{10,11... | collective-permute-start | bytes 110600 | tf_op jit(solution)/shard_map/ppermute | solution.py:17
  31.7 0.0 collective-permute-done.2.refs_1_
  31.7 0.0 collective-permute-done.4.refs_3_
  31.7 0.2 shard_map.142
  32.0 2.3 %collective-permute-done.1.theirs = f32[8,1152]{1,0:T(8,128)S(1)} collective-permute-done((f32[8,1152]{1,0:T(8,128)S(1)}, f32[8,1152]{1,0:T(8,128)S(1)}, u32[]{:S(2)}, u32[]{:S(2)}) %collective-permute-start.1) | collective-permute-done | bytes 36896 | tf_op jit(solution)/shard_map/ppermute | solution.py:17
  34.3 0.3 shard_map.143
  34.6 1.5 %collective-permute-start.5 = (f32[8,1024]{1,0:T(8,128)S(1)}, f32[8,1024]{1,0:T(8,128)S(1)}, u32[]{:S(2)}, u32[]{:S(2)}) collective-permute-start(f32[8,1024]{1,0:T(8,128)S(1)} %get-tuple-element.29.mine), channel_id=1, source_target_pairs={{0,8},{1,9},{2,10},{3,11},{4,12},{5,13},{6,14},{7,15},{8,0},{9,1},... | collective-permute-start | bytes 98312 | tf_op jit(solution)/shard_map/ppermute | solution.py:17
  36.1 0.0 collective-permute-done.7.refs_5_
  36.1 0.3 shard_map.144
  36.4 2.1 %collective-permute-done.5.theirs = f32[8,1024]{1,0:T(8,128)S(1)} collective-permute-done((f32[8,1024]{1,0:T(8,128)S(1)}, f32[8,1024]{1,0:T(8,128)S(1)}, u32[]{:S(2)}, u32[]{:S(2)}) %collective-permute-start.5) | collective-permute-done | bytes 32800 | tf_op jit(solution)/shard_map/ppermute | solution.py:17
  38.5 0.4 shard_map.145
  38.9 1.4 %collective-permute-start.8 = (f32[8,768]{1,0:T(8,128)S(1)}, f32[8,768]{1,0:T(8,128)S(1)}, u32[]{:S(2)}, u32[]{:S(2)}) collective-permute-start(f32[8,768]{1,0:T(8,128)S(1)} %get-tuple-element.34.mine), channel_id=1, source_target_pairs={{0,2},{1,3},{2,0},{3,1},{4,6},{5,7},{6,4},{7,5},{8,10},{9,11},{10,... | collective-permute-start | bytes 73736 | tf_op jit(solution)/shard_map/ppermute | solution.py:17
  40.3 0.0 collective-permute-done.10.refs_7_
  40.3 0.8 %shard_map.146 = (bf16[256,256]{1,0:T(8,128)(2,1)S(1)}, bf16[256,256]{1,0:T(8,128)(2,1)S(1)}, bf16[256,512]{1,0:T(8,128)(2,1)S(1)}, bf16[256,512]{1,0:T(8,128)(2,1)S(1)}) custom-call(f32[280,128]{1,0:T(8,128)S(1)} %shard_map.141.refs_0_, f32[280,128]{1,0:T(8,128)S(1)} %collective-permute-done.2.refs_1_, f32[280,128]{1,0:T(8,128)S(1)} %collective-permute-done.3.refs_2_, ...), custom_call_target="tpu_custom_call" | custom-call | tf_op jit(solution)/shard_map/pallas_call | solution.py:180
  41.1 1.6 %collective-permute-done.8.theirs = f32[8,768]{1,0:T(8,128)S(1)} collective-permute-done((f32[8,768]{1,0:T(8,128)S(1)}, f32[8,768]{1,0:T(8,128)S(1)}, u32[]{:S(2)}, u32[]{:S(2)}) %collective-permute-start.8) | collective-permute-done | bytes 24608 | tf_op jit(solution)/shard_map/ppermute | solution.py:17
  42.7 0.5 shard_map.147
  43.2 2.5 %collective-permute-start.11 = (f32[8,512]{1,0:T(8,128)S(1)}, f32[8,512]{1,0:T(8,128)S(1)}, u32[]{:S(2)}, u32[]{:S(2)}) collective-permute-start(f32[8,512]{1,0:T(8,128)S(1)} %get-tuple-element.39.mine), channel_id=1, source_target_pairs={{0,16},{1,17},{2,18},{3,19},{4,20},{5,21},{6,22},{7,23},{8,24},{9,... | collective-permute-start | bytes 49160 | tf_op jit(solution)/shard_map/ppermute | solution.py:17
  45.7 0.1 shard_map.148
  45.8 2.2 %collective-permute-done.11.theirs = f32[8,512]{1,0:T(8,128)S(1)} collective-permute-done((f32[8,512]{1,0:T(8,128)S(1)}, f32[8,512]{1,0:T(8,128)S(1)}, u32[]{:S(2)}, u32[]{:S(2)}) %collective-permute-start.11) | collective-permute-done | bytes 16416 | tf_op jit(solution)/shard_map/ppermute | solution.py:17
  48.0 0.5 shard_map.149.mine
  48.5 2.5 %collective-permute-start.12 = (f32[8,512]{1,0:T(8,128)S(1)}, f32[8,512]{1,0:T(8,128)S(1)}, u32[]{:S(2)}, u32[]{:S(2)}) collective-permute-start(f32[8,512]{1,0:T(8,128)S(1)} %shard_map.149.mine), channel_id=1, source_target_pairs={{0,16},{1,17},{2,18},{3,19},{4,20},{5,21},{6,22},{7,23},{8,24},{9,... | collective-permute-start | bytes 49160 | tf_op jit(solution)/shard_map/ppermute | solution.py:17
  51.1 2.1 %collective-permute-done.12.theirs = f32[8,512]{1,0:T(8,128)S(1)} collective-permute-done((f32[8,512]{1,0:T(8,128)S(1)}, f32[8,512]{1,0:T(8,128)S(1)}, u32[]{:S(2)}, u32[]{:S(2)}) %collective-permute-start.12) | collective-permute-done | bytes 16416 | tf_op jit(solution)/shard_map/ppermute | solution.py:17
  53.2 3.6 %shard_map.150 = (f32[1,1,8,512]{3,2,1,0:T(8,128)}, f32[1,1,8,96]{3,2,1,0:T(8,128)}) custom-call(f32[8,512]{1,0:T(8,128)S(1)} %shard_map.149.mine, f32[8,512]{1,0:T(8,128)S(1)} %collective-permute-done.12.theirs, f32[8,256]{1,0:T(8,128)S(1)} %get-tuple-element.42.z1, f32[8,256]{1,0:T(8,128)S(1)} %get-tuple-element.43.z2, f32[8,128]{1,0:T(8,128)S(1)} %get-tuple-element.44.z3, ...), custom_call_target="tpu_custom_call" | custom-call | tf_op jit(solution)/shard_map/pallas_call | solution.py:180
  (9 shorter events, 0.1 us)
Async XLA Ops:
  0.6 0.8 %copy-start.3 = (f32[1,1,16,512]{3,2,1,0:T(8,128)S(1)}, f32[1,1,16,512]{3,2,1,0:T(8,128)}, u32[]{:S(2)}) copy-start(f32[1,1,16,512]{3,2,1,0:T(8,128)} %f0.1) | copy-start | bytes 98308
  1.4 0.8 %copy-start.4 = (f32[1,1,32,256]{3,2,1,0:T(8,128)S(1)}, f32[1,1,32,256]{3,2,1,0:T(8,128)}, u32[]{:S(2)}) copy-start(f32[1,1,32,256]{3,2,1,0:T(8,128)} %f2.1) | copy-start | bytes 98308
  2.2 0.7 %copy-start.5 = (s32[1,1,4,128]{3,2,1,0:T(4,128)S(1)}, s32[1,1,4,128]{3,2,1,0:T(4,128)}, u32[]{:S(2)}) copy-start(s32[1,1,4,128]{3,2,1,0:T(4,128)} %places.5) | copy-start | bytes 6148
  2.8 0.7 %copy-start.8 = (f32[1,1,16,256]{3,2,1,0:T(8,128)S(1)}, f32[1,1,16,256]{3,2,1,0:T(8,128)}, u32[]{:S(2)}) copy-start(f32[1,1,16,256]{3,2,1,0:T(8,128)} %f1.1) | copy-start | bytes 49156
  3.6 0.7 %copy-start.9 = (f32[1,1,32,128]{3,2,1,0:T(8,128)S(1)}, f32[1,1,32,128]{3,2,1,0:T(8,128)}, u32[]{:S(2)}) copy-start(f32[1,1,32,128]{3,2,1,0:T(8,128)} %f3.1) | copy-start | bytes 49156
  4.3 0.7 %copy-start.10 = (f32[1,1,32,128]{3,2,1,0:T(8,128)S(1)}, f32[1,1,32,128]{3,2,1,0:T(8,128)}, u32[]{:S(2)}) copy-start(f32[1,1,32,128]{3,2,1,0:T(8,128)} %l2.1) | copy-start | bytes 49156
  5.0 0.7 %copy-start.11 = (f32[1,1,32,128]{3,2,1,0:T(8,128)S(1)}, f32[1,1,32,128]{3,2,1,0:T(8,128)}, u32[]{:S(2)}) copy-start(f32[1,1,32,128]{3,2,1,0:T(8,128)} %l3.1) | copy-start | bytes 49156
  5.7 0.7 %copy-start.12 = (f32[1,1,16,128]{3,2,1,0:T(8,128)S(1)}, f32[1,1,16,128]{3,2,1,0:T(8,128)}, u32[]{:S(2)}) copy-start(f32[1,1,16,128]{3,2,1,0:T(8,128)} %l1.1) | copy-start | bytes 24580
  6.4 20.4 %copy-start = (f32[1,1,4,128,512]{4,3,2,1,0:T(8,128)S(1)}, f32[1,1,4,128,512]{4,3,2,1,0:T(8,128)}, u32[]{:S(2)}) copy-start(f32[1,1,4,128,512]{4,3,2,1,0:T(8,128)} %coupling.3) | copy-start | bytes 3145732
  6.4 6.8 %collective-permute-start.3 = (f32[280,128]{1,0:T(8,128)S(1)}, f32[280,128]{1,0:T(8,128)S(1)}, u32[]{:S(2)}, u32[]{:S(2)}) collective-permute-start(f32[280,128]{1,0:T(8,128)S(1)} %shard_map.141.refs_0_), channel_id=1, source_target_pairs={{0,1},{1,0},{2,3},{3,2},{4,5},{5,4},{6,7},{7,6},{8,9},{9,8},{10,11... | collective-permute-start | bytes 430088 | tf_op jit(solution)/shard_map/ppermute | solution.py:17
  13.2 6.7 %collective-permute-start.6 = (f32[432,128]{1,0:T(8,128)S(1)}, f32[432,128]{1,0:T(8,128)S(1)}, u32[]{:S(2)}, u32[]{:S(2)}) collective-permute-start(f32[432,128]{1,0:T(8,128)S(1)} %pad_maximum_fusion.1), channel_id=1, source_target_pairs={{0,8},{1,9},{2,10},{3,11},{4,12},{5,13},{6,14},{7,15},{8,0},{9,1},... | collective-permute-start | bytes 663560 | tf_op jit(solution)/shard_map/ppermute | solution.py:17
  19.9 6.9 %copy-start.1 = (f32[1,1,4,128,128]{4,3,2,1,0:T(8,128)S(1)}, f32[1,1,4,128,128]{4,3,2,1,0:T(8,128)}, u32[]{:S(2)}) copy-start(f32[1,1,4,128,128]{4,3,2,1,0:T(8,128)} %inverse.3) | copy-start | bytes 786436
  19.9 6.9 %copy-start.2 = (f32[1,1,3,128,128]{4,3,2,1,0:T(8,128)S(1)}, f32[1,1,3,128,128]{4,3,2,1,0:T(8,128)}, u32[]{:S(2)}) copy-start(f32[1,1,3,128,128]{4,3,2,1,0:T(8,128)} %lower.3) | copy-start | bytes 589828
  19.9 6.9 %copy-start.6 = (s32[1,1,4,128]{3,2,1,0:T(4,128)S(1)}, s32[1,1,4,128]{3,2,1,0:T(4,128)}, u32[]{:S(2)}) copy-start(s32[1,1,4,128]{3,2,1,0:T(4,128)} %places.5) | copy-start | bytes 6148
  19.9 6.9 %copy-start.7 = (f32[1,1,8,512]{3,2,1,0:T(8,128)S(1)}, f32[1,1,8,512]{3,2,1,0:T(8,128)}, u32[]{:S(2)}) copy-start(f32[1,1,8,512]{3,2,1,0:T(8,128)} %rhs.1) | copy-start | bytes 49156
  20.0 6.9 %copy-start.13 = (f32[1,1,8,96]{3,2,1,0:T(8,128)S(1)}, f32[1,1,8,96]{3,2,1,0:T(8,128)}, u32[]{:S(2)}) copy-start(f32[1,1,8,96]{3,2,1,0:T(8,128)} %sep_rhs.1) | copy-start | bytes 9220
  20.0 6.3 %collective-permute-start.9 = (f32[480,128]{1,0:T(8,128)S(1)}, f32[480,128]{1,0:T(8,128)S(1)}, u32[]{:S(2)}, u32[]{:S(2)}) collective-permute-start(f32[480,128]{1,0:T(8,128)S(1)} %pad_maximum_fusion), channel_id=1, source_target_pairs={{0,2},{1,3},{2,0},{3,1},{4,6},{5,7},{6,4},{7,5},{8,10},{9,11},{10,... | collective-permute-start | bytes 737288 | tf_op jit(solution)/shard_map/ppermute | solution.py:17
  21.5 14.6 %collective-permute-start.7 = (f32[432,128]{1,0:T(8,128)S(1)}, f32[432,128]{1,0:T(8,128)S(1)}, u32[]{:S(2)}, u32[]{:S(2)}) collective-permute-start(f32[432,128]{1,0:T(8,128)S(1)} %collective-permute-done.6.refs_4_), channel_id=1, source_target_pairs={{0,4},{1,5},{2,6},{3,7},{4,0},{5,1},{6,2},{7,3},{8,12},{9,13},{10,... | collective-permute-start | bytes 663560 | tf_op jit(solution)/shard_map/ppermute | solution.py:17
  26.3 14.1 %collective-permute-start.10 = (f32[480,128]{1,0:T(8,128)S(1)}, f32[480,128]{1,0:T(8,128)S(1)}, u32[]{:S(2)}, u32[]{:S(2)}) collective-permute-start(f32[480,128]{1,0:T(8,128)S(1)} %collective-permute-done.9.refs_6_), channel_id=1, source_target_pairs={{0,4},{1,5},{2,6},{3,7},{4,0},{5,1},{6,2},{7,3},{8,12},{9,13},{10,... | collective-permute-start | bytes 737288 | tf_op jit(solution)/shard_map/ppermute | solution.py:17
  26.3 5.4 %collective-permute-start.2 = (f32[280,128]{1,0:T(8,128)S(1)}, f32[280,128]{1,0:T(8,128)S(1)}, u32[]{:S(2)}, u32[]{:S(2)}) collective-permute-start(f32[280,128]{1,0:T(8,128)S(1)} %shard_map.141.refs_0_), channel_id=1, source_target_pairs={{0,4},{1,5},{2,6},{3,7},{4,0},{5,1},{6,2},{7,3},{8,12},{9,13},{10,... | collective-permute-start | bytes 430088 | tf_op jit(solution)/shard_map/ppermute | solution.py:17
  26.8 4.9 %collective-permute-start.4 = (f32[280,128]{1,0:T(8,128)S(1)}, f32[280,128]{1,0:T(8,128)S(1)}, u32[]{:S(2)}, u32[]{:S(2)}) collective-permute-start(f32[280,128]{1,0:T(8,128)S(1)} %collective-permute-done.3.refs_2_), channel_id=1, source_target_pairs={{0,4},{1,5},{2,6},{3,7},{4,0},{5,1},{6,2},{7,3},{8,12},{9,13},{10,... | collective-permute-start | bytes 430088 | tf_op jit(solution)/shard_map/ppermute | solution.py:17
  28.9 1.4 %collective-permute-start = (f32[8,1152]{1,0:T(8,128)S(1)}, f32[8,1152]{1,0:T(8,128)S(1)}, u32[]{:S(2)}, u32[]{:S(2)}) collective-permute-start(f32[8,1152]{1,0:T(8,128)S(1)} %get-tuple-element.24), channel_id=1, source_target_pairs={{0,4},{1,5},{2,6},{3,7},{4,0},{5,1},{6,2},{7,3},{8,12},{9,13},{10,... | collective-permute-start | bytes 110600 | tf_op jit(solution)/shard_map/ppermute | solution.py:17
  30.3 4.0 %collective-permute-start.1 = (f32[8,1152]{1,0:T(8,128)S(1)}, f32[8,1152]{1,0:T(8,128)S(1)}, u32[]{:S(2)}, u32[]{:S(2)}) collective-permute-start(f32[8,1152]{1,0:T(8,128)S(1)} %add.3.mine), channel_id=1, source_target_pairs={{0,1},{1,0},{2,3},{3,2},{4,5},{5,4},{6,7},{7,6},{8,9},{9,8},{10,11... | collective-permute-start | bytes 110600 | tf_op jit(solution)/shard_map/ppermute | solution.py:17
  34.6 3.9 %collective-permute-start.5 = (f32[8,1024]{1,0:T(8,128)S(1)}, f32[8,1024]{1,0:T(8,128)S(1)}, u32[]{:S(2)}, u32[]{:S(2)}) collective-permute-start(f32[8,1024]{1,0:T(8,128)S(1)} %get-tuple-element.29.mine), channel_id=1, source_target_pairs={{0,8},{1,9},{2,10},{3,11},{4,12},{5,13},{6,14},{7,15},{8,0},{9,1},... | collective-permute-start | bytes 98312 | tf_op jit(solution)/shard_map/ppermute | solution.py:17
  38.9 3.8 %collective-permute-start.8 = (f32[8,768]{1,0:T(8,128)S(1)}, f32[8,768]{1,0:T(8,128)S(1)}, u32[]{:S(2)}, u32[]{:S(2)}) collective-permute-start(f32[8,768]{1,0:T(8,128)S(1)} %get-tuple-element.34.mine), channel_id=1, source_target_pairs={{0,2},{1,3},{2,0},{3,1},{4,6},{5,7},{6,4},{7,5},{8,10},{9,11},{10,... | collective-permute-start | bytes 73736 | tf_op jit(solution)/shard_map/ppermute | solution.py:17
  43.2 4.8 %collective-permute-start.11 = (f32[8,512]{1,0:T(8,128)S(1)}, f32[8,512]{1,0:T(8,128)S(1)}, u32[]{:S(2)}, u32[]{:S(2)}) collective-permute-start(f32[8,512]{1,0:T(8,128)S(1)} %get-tuple-element.39.mine), channel_id=1, source_target_pairs={{0,16},{1,17},{2,18},{3,19},{4,20},{5,21},{6,22},{7,23},{8,24},{9,... | collective-permute-start | bytes 49160 | tf_op jit(solution)/shard_map/ppermute | solution.py:17
  48.5 4.7 %collective-permute-start.12 = (f32[8,512]{1,0:T(8,128)S(1)}, f32[8,512]{1,0:T(8,128)S(1)}, u32[]{:S(2)}, u32[]{:S(2)}) collective-permute-start(f32[8,512]{1,0:T(8,128)S(1)} %shard_map.149.mine), channel_id=1, source_target_pairs={{0,16},{1,17},{2,18},{3,19},{4,20},{5,21},{6,22},{7,23},{8,24},{9,... | collective-permute-start | bytes 49160 | tf_op jit(solution)/shard_map/ppermute | solution.py:17

commit v2 on v1

--- a/solution.py
+++ b/solution.py
@@ -11,6 +11,8 @@
 LANES = 128
 GATHER_BYTES = 8 * 2**20
 VMEM_BYTES = 24 * 2**20
+WHOLE_VMEM_BYTES = 60 * 2**20
+BYTES_A_MICROSECOND = 3_690_000
 
 
 def from_partner(value, axis, distance):
@@ -165,6 +167,17 @@
     return total[:rows] + total[rows:]
 
 
+def wide_times(left, right):
+    left = jnp.concatenate(halves(left), axis=1)
+    right_high, right_low = halves(right)
+    right = jnp.concatenate(
+        [jnp.concatenate([right_high] * 2, axis=1), jnp.concatenate([right_low] * 2, axis=1)], axis=0
+    )
+    total = lax.dot_general(left, right, (((1,), (1,)), ((), ())), preferred_element_type=jnp.float32)
+    width = right.shape[0] // 2
+    return total[:, :width] + total[:, width:]
+
+
 def one_hot(positions, height):
     rows = lax.broadcasted_iota(jnp.int32, (height, positions.shape[1]), 0)
     return (rows == positions).astype(jnp.float32).astype(jnp.bfloat16)
@@ -175,15 +188,24 @@
     return pieces[0] if chunks == 1 else jnp.concatenate(pieces, axis=1)
 
 
-def vmem_call(body, outs, *operands):
+def vmem_call(body, outs, *operands, microseconds, after=(), space=pltpu.VMEM, scratch=(), limit=VMEM_BYTES):
     out_shape = [jax.ShapeDtypeStruct(shape, dtype) for shape, dtype in outs]
+
+    def kernel(*refs):
+        body(*refs[: len(operands)], *refs[len(operands) + len(after) :])
+
     return pl.pallas_call(
-        body,
+        kernel,
         out_shape=out_shape,
-        in_specs=[pl.BlockSpec(memory_space=pltpu.VMEM)] * len(operands),
+        in_specs=[pl.BlockSpec(memory_space=space)] * len(operands)
+        + [pl.BlockSpec(memory_space=pl.ANY)] * len(after),
         out_specs=[pl.BlockSpec(memory_space=pltpu.VMEM)] * len(outs),
-        compiler_params=pltpu.CompilerParams(vmem_limit_bytes=VMEM_BYTES),
-    )(*operands)
+        scratch_shapes=scratch,
+        cost_estimate=pl.CostEstimate(
+            flops=0, bytes_accessed=int(microseconds * BYTES_A_MICROSECOND), transcendentals=0
+        ),
+        compiler_params=pltpu.CompilerParams(vmem_limit_bytes=limit),
+    )(*operands, *after)
 
 
 def packed_layout(factors, link_mats):
@@ -204,16 +226,26 @@
     return starts, at
 
 
-def pack_body(starts, f0, f1, f2, f3, l1, l2, l3, places, out):
+def pack_body(starts, f0, f1, f2, f3, l1, l2, l3, places, out, numbers, semaphores):
+    moves = [(places.at[0, 0], numbers)]
     for name, ref in (("f0", f0), ("f1", f1), ("f2", f2), ("f3", f3)):
         rows, width = ref.shape[2:]
         for chunk in range(width // LANES):
             at = starts[name] + chunk * rows
-            out[at : at + rows, :] = ref[0, 0, :, chunk * LANES : (chunk + 1) * LANES]
+            moves.append((ref.at[0, 0, :, pl.ds(chunk * LANES, LANES)], out.at[pl.ds(at, rows), :]))
     for name, ref in (("l1", l1), ("l2", l2), ("l3", l3)):
-        out[starts[name] : starts[name] + ref.shape[2], :] = ref[0, 0]
-    numbers = places[0, 0].astype(jnp.float32)
-    out[starts["places"] : starts["places"] + 8, :] = jnp.concatenate([numbers, numbers], axis=0)
+        moves.append((ref.at[0, 0], out.at[pl.ds(starts[name], ref.shape[2]), :]))
+    copies = [
+        pltpu.make_async_copy(source, target, semaphores.at[number])
+        for number, (source, target) in enumerate(moves)
+    ]
+    for copy in copies:
+        copy.start()
+    copies[0].wait()
+    positions = numbers[...].astype(jnp.float32)
+    out[starts["places"] : starts["places"] + 8, :] = jnp.concatenate([positions, positions], axis=0)
+    for copy in copies[1:]:
+        copy.wait()
 
 
 def own_targets(sizes, owned, taken):
@@ -270,14 +302,22 @@
             at += rows
 
 
-def eliminate_body(size, above, mine, theirs, f_high, f_low, m_high, m_low, sums, found):
+def eliminate_body(size, above, tables, mine, theirs, *refs):
+    sums, found = refs[4 * tables :]
     width = mine.shape[1]
     total = mine[...] + theirs[...]
-    solved = times(total[:, width - size :], [f_high[...], f_low[...]], True)
-    found[...] = solved
-    sums[:, : width - size] = total[:, : width - size]
+    right_side = total[:, width - size :]
     rest = total[:, width - size - above : width - size]
-    sums[:, width - size - above :] = rest - times(solved, [m_high[...], m_low[...]], False)
+    at = 0
+    for table in range(tables):
+        f_high, f_low, m_high, m_low = refs[4 * table : 4 * table + 4]
+        solved = times(right_side, [f_high[...], f_low[...]], True)
+        found[:, at : at + solved.shape[1]] = solved
+        rest = rest - times(solved, [m_high[...], m_low[...]], False)
+        at += solved.shape[1]
+    if width > size + above:
+        sums[:, : width - size - above] = total[:, : width - size - above]
+    sums[:, width - size - above :] = rest
 
 
 def top_body(mine, theirs, f_high, f_low, partial):
@@ -286,34 +326,76 @@
     partial[...] = times(times(total, pieces, True), pieces, False)
 
 
+def join_body(prefix, counts, *refs):
+    copy = refs[len(counts)]
+    copy[...] = refs[len(counts) - 1][...]
+    if prefix == 0:
+        return
+    message = refs[len(counts) + 1]
+    at = 0
+    for ref, members in zip(refs, counts):
+        stride = ref.shape[0] // members
+        for member in range(members):
+            message[at : at + prefix, :] = ref[member * stride : member * stride + prefix, :]
+            at += prefix
+
+
+def add_body(mine, theirs, out):
+    out[...] = mine[...] + theirs[...]
+
+
+def fold_body(tables, found, *refs):
+    solved, n_high, n_low = refs[4 * tables :]
+    dims = (((0,), (0,)), ((), ()))
+    known = folded = None
+    at = 0
+    for table in range(tables):
+        f_high, f_low, m_high, m_low = refs[4 * table : 4 * table + 4]
+        rows = f_high.shape[0]
+        pieces = [f_high[...], f_low[...]]
+        term = times(found[:, at : at + rows], pieces, False)
+        known = term if known is None else known + term
+        for link in (m_high[...], m_low[...]):
+            for piece in pieces:
+                term = lax.dot_general(link, piece, dims, preferred_element_type=jnp.float32)
+                folded = term if folded is None else folded + term
+        at += rows
+    solved[...] = known
+    n_high[...], n_low[...] = halves(folded)
+
+
+def leaf_body(sections, forward, coupling, inverse, lower, base, d_high, d_low):
+    count, block = inverse.shape[2], inverse.shape[3]
+    rhs_count = forward.shape[0]
+    rows = [coupling[0, 0, section] for section in sections]
+    rows = jnp.concatenate([forward[...]] + rows, axis=0)
+    later = None
+    for counter in reversed(range(count)):
+        current = rows[:, counter * block : (counter + 1) * block]
+        if counter < count - 1:
+            current = current - wide_times(later, lower[0, 0, counter])
+        later = wide_times(current, inverse[0, 0, counter])
+        columns = slice(counter * block, (counter + 1) * block)
+        base[:, columns] = later[:rhs_count]
+        d_high[:, columns], d_low[:, columns] = halves(later[rhs_count:])
+
+
 def backward_body(
-    sizes, owned, taken, mine, theirs, z1, z2, z3,
-    f1h, f1l, m1h, m1l, f2h, f2l, m2h, m2l, f3h, f3l, m3h, m3l,
-    forward, coupling, places, inverse, lower, leaf, sep,
+    sizes, owned, taken, mine, theirs, u1, n1h, n1l, u2, n2h, n2l, u3, n3h, n3l,
+    base, d1h, d1l, d2h, d2l, places, leaf, sep,
 ):
     solved = [mine[...] + theirs[...]]
-    levels = (
-        (z1, f1h, f1l, m1h, m1l),
-        (z2, f2h, f2l, m2h, m2l),
-        (z3, f3h, f3l, m3h, m3l),
-    )
-    for found, f_high, f_low, m_high, m_low in levels:
-        update = found[...] - times(solved[-1], [m_high[...], m_low[...]], True)
-        solved.append(times(update, [f_high[...], f_low[...]], False))
+    for known, n_high, n_low in ((u1, n1h, n1l), (u2, n2h, n2l), (u3, n3h, n3l)):
+        solved.append(known[...] - times(solved[-1], [n_high[...], n_low[...]], False))
+    picked = [
+        times(solved[section], [one_hot(places[0, 0, section : section + 1, :], sizes[section])], False)
+        for section in range(4)
+    ]
+    first = times(jnp.concatenate(picked[:2], axis=1), [d1h[...], d1l[...]], False)
+    second = times(jnp.concatenate(picked[2:], axis=1), [d2h[...], d2l[...]], False)
+    leaf[0, 0] = base[...] - first - second
     everything = jnp.concatenate(solved, axis=1)
     sep[0, 0] = times(everything, [one_hot(own_targets(sizes, owned, taken), sum(sizes))], False)
-    work = forward[...]
-    for section in range(4):
-        picked = times(solved[section], [one_hot(places[0, 0, section : section + 1, :], sizes[section])], False)
-        work = work - times(picked, halves(coupling[0, 0, section]), False)
-    count, block = inverse.shape[2], inverse.shape[3]
-    later = None
-    for counter in reversed(range(count)):
-        current = work[:, counter * block : (counter + 1) * block]
-        if counter < count - 1:
-            current = current - times(later, halves(lower[0, 0, counter]), True)
-        later = times(current, halves(inverse[0, 0, counter]), True)
-        leaf[0, 0, :, counter * block : (counter + 1) * block] = later
 
 
 def gathered(
@@ -343,73 +425,107 @@
     axes = ("gx", "gy")
     core = gy_bits
     rhs_count = rhs_leaf.shape[2]
+    copies = 1 + sum(size // LANES for size in sizes) + len(links)
 
     (packed,) = vmem_call(
         functools.partial(pack_body, starts),
         [((height, LANES), jnp.float32)],
         factor_one, factor_two, factor_three, factor_four, link_two, link_three, link_four, interface,
+        microseconds=1.0, space=pltpu.HBM, limit=WHOLE_VMEM_BYTES,
+        scratch=(pltpu.VMEM(interface.shape[2:], jnp.int32), pltpu.SemaphoreType.DMA((copies,))),
     )
     held = [packed]
     counts = [1]
     both = [packed, from_partner(packed, axes, core)]
     strides = [(1, height), (1, height)]
 
-    def widen(bit_number, rows):
-        message = [
-            block.reshape(members, -1, LANES)[:, :rows].reshape(members * rows, LANES)
-            for block, members in zip(held, counts)
-        ]
-        message = message[0] if len(message) == 1 else jnp.concatenate(message, axis=0)
-        arrived = from_partner(message, axes, bit_number)
-        members = sum(counts)
+    def arrive(arrived, stride, prefix, after):
         held.append(arrived)
-        counts.append(members)
-        both.extend([arrived, from_partner(arrived, axes, core)])
-        strides.extend([(members, rows)] * 2)
-
-    def level(section):
+        counts.append(arrived.shape[0] // stride)
+        outs = [(arrived.shape, jnp.float32)]
+        if prefix:
+            outs.append(((sum(counts) * prefix, LANES), jnp.float32))
+        copy, *message = vmem_call(
+            functools.partial(join_body, prefix, tuple(counts)), outs, *held, after=after, microseconds=0.1
+        )
+        held[-1] = copy
+        both.extend([copy, from_partner(copy, axes, core)])
+        strides.extend([(counts[-1], stride)] * 2)
+        return message
+
+    def level(section, first, last, after=()):
         rows, size = factors[section].shape
         above = sizes[section - 1] if section > 0 else 0
-        members = sum(count for count, _ in strides)
+        members = sum(count for count, _ in strides[first:last])
         outs = [((members * rows, size), jnp.bfloat16)] * 2
         if section > 0:
             outs = outs + [((members * rows, above), jnp.bfloat16)] * 2
-        body = functools.partial(gather_body, section, starts, rows, size, above, tuple(strides))
-        return vmem_call(body, outs, *both)
-
+        body = functools.partial(gather_body, section, starts, rows, size, above, tuple(strides[first:last]))
+        return vmem_call(body, outs, *both[first:last], microseconds=0.4, after=after)
+
+    inner = [bit_number for bit_number in taken[3] if bit_number != core]
+    steps = [(bit_number, 3) for bit_number in inner]
+    steps += [(gy_bits + gx_bits - 2, 2), (gy_bits - 1, 1)]
+    moving = from_partner(packed, axes, steps[0][0])
     forward, sums = vmem_call(
         functools.partial(forward_body, sizes, owned, taken),
         [((rhs_count, rhs_leaf.shape[3]), jnp.float32), ((rhs_count, sum(sizes)), jnp.float32)],
-        rhs_leaf, leaf_inv, leaf_sub, sep_rhs, interface, coupling,
-    )
-
-    inner = [bit_number for bit_number in taken[3] if bit_number != core]
-    steps = {3: inner, 2: [gy_bits + gx_bits - 2], 1: [gy_bits - 1], 0: [gy_bits + gx_bits - 1]}
-    sums = sums + from_partner(sums, axes, core)
-    tables = [None] * 4
-    found = [None] * 4
-    for section in (3, 2, 1):
-        for position, bit_number in enumerate(steps[section]):
-            widen(bit_number, heights[section])
-            theirs = from_partner(sums, axes, bit_number)
-            if position < len(steps[section]) - 1:
-                sums = sums + theirs
-        tables[section] = level(section)
+        rhs_leaf, leaf_inv, leaf_sub, sep_rhs, interface, coupling, microseconds=2.0,
+    )
+    (sums,) = vmem_call(
+        add_body, [((rhs_count, sum(sizes)), jnp.float32)], sums, from_partner(sums, axes, core), microseconds=0.1
+    )
+    folded = [None] * 4
+    late = ()
+    for number, (bit_number, section) in enumerate(steps):
+        theirs = from_partner(sums, axes, bit_number)
+        following = steps[number + 1] if number + 1 < len(steps) else (None, None)
+        prefix = heights[following[1]] if following[1] else 0
+        known = len(both)
+        message = arrive(moving, heights[section], prefix, (sums,))
+        if message:
+            moving = from_partner(message[0], axes, following[0])
+        if following[1] == section:
+            sums = sums + theirs
+            continue
+        if section == 1:
+            tables = [level(section, 0, known, (sums,)), level(section, known, len(both))]
+        else:
+            tables = [level(section, 0, len(both))]
         size, above = sizes[section], sizes[section - 1]
-        sums, found[section] = vmem_call(
-            functools.partial(eliminate_body, size, above),
+        flat = [array for table in tables for array in table]
+        sums, found = vmem_call(
+            functools.partial(eliminate_body, size, above, len(tables)),
             [((rhs_count, sums.shape[1] - size), jnp.float32), ((rhs_count, size), jnp.float32)],
-            sums, theirs, *tables[section],
+            sums, theirs, *flat, microseconds=0.4, after=late,
         )
-    tables[0] = level(0)
-    theirs = from_partner(sums, axes, steps[0][0])
-    (partial,) = vmem_call(top_body, [((rhs_count, sizes[0]), jnp.float32)], sums, theirs, *tables[0])
-    theirs = from_partner(partial, axes, steps[0][0])
+        folded[section] = vmem_call(
+            functools.partial(fold_body, len(tables)),
+            [((rhs_count, size), jnp.float32)] + [((above, size), jnp.bfloat16)] * 2,
+            found, *flat, microseconds=0.5,
+        )
+        late = tuple(folded[section][:1])
+    last = gy_bits + gx_bits - 1
+    solves = [
+        vmem_call(
+            functools.partial(leaf_body, sections),
+            [((rhs_count, rhs_leaf.shape[3]), jnp.float32)] + [((2 * LANES, rhs_leaf.shape[3]), jnp.bfloat16)] * 2,
+            forward, coupling, leaf_inv, leaf_sub, microseconds=1.0, after=(before,),
+        )
+        for sections, before in (((0, 1), sums), ((2, 3), sums))
+    ]
+    table = level(0, 0, len(both))
+    theirs = from_partner(sums, axes, last)
+    (partial,) = vmem_call(
+        top_body, [((rhs_count, sizes[0]), jnp.float32)],
+        sums, theirs, *table, microseconds=0.5, after=(solves[0][0],),
+    )
+    theirs = from_partner(partial, axes, last)
     leaf, sep = vmem_call(
         functools.partial(backward_body, sizes, owned, taken),
         [(rhs_leaf.shape, jnp.float32), (sep_rhs.shape, jnp.float32)],
-        partial, theirs, *found[1:], *tables[1], *tables[2], *tables[3],
-        forward, coupling, interface, leaf_inv, leaf_sub,
+        partial, theirs, *folded[1], *folded[2], *folded[3], *solves[0], *solves[1][1:], interface,
+        microseconds=2.0,
     )
     return (leaf, sep)
 

time: 57.4 us -> 42 us (0.73)
  waiting for transfers between devices: 24.5 us -> 10.7 us
  local copies, waits for them, and re-layouts: 5.83 us -> 2.18 us
  Pallas kernels: 8.71 us -> 12.3 us
  starting transfers between devices: 16.9 us -> 15.8 us
    ppermute x13, waiting for transfers between devices: 24.5 us -> 10.7 us  [from_partner(): lax.ppermute(value, axis, [(i, i ^ 1 << distance) for i in range(lax.axis...]
    unnamed x28 -> x18, local copies, waits for them, and re-layouts: 5.79 us -> 2.18 us
    pallas_call x11 -> x21, Pallas kernels: 8.71 us -> 12.3 us  [vmem_call(): pl.pallas_call(kernel, out_shape=out_shape, in_specs=[pl.BlockSpec(memory...]
    ppermute x13, starting transfers between devices: 16.9 us -> 15.8 us  [from_partner(): lax.ppermute(value, axis, [(i, i ^ 1 << distance) for i in range(lax.axis...]
  transfers between devices with their start and end apart: 13 -> 13, of which waited for: 9 -> 9; matrix products, arithmetic and copies ran while one was open for 0% -> 0% of each run, Pallas kernels for 7% -> 20%
where the time goes in v2:
time: 42 us; the launch traced here: 41.7 us
  starting transfers between devices  15.8 us (38%)
  Pallas kernels  12.3 us (29%)
  waiting for transfers between devices  10.7 us (25%)
  local copies, waits for them, and re-layouts  2.18 us (5%)
  between operations  0.83 us (2%)
    ppermute x13, starting transfers between devices, from_partner(): lax.ppermute(value, axis, [(i, i ^ 1 << distance) for i in range(lax.axis...  15.8 us
    pallas_call x21, Pallas kernels, vmem_call(): pl.pallas_call(kernel, out_shape=out_shape, in_specs=[pl.BlockSpec(memory...  12.3 us
    ppermute x13, waiting for transfers between devices, from_partner(): lax.ppermute(value, axis, [(i, i ^ 1 << distance) for i in range(lax.axis...  10.7 us
    unnamed x18, local copies, waits for them, and re-layouts  2.18 us
  transfers between devices with their start and end apart: 13, of which 9 were waited for; matrix products, arithmetic and copies ran while one was open for 0% of the time, Pallas kernels for 20%

profile of v2, /device:TPU:0, one launch (start us, length us, event | category | flops | bytes accessed | tf_op | source)
XLA Modules:
  0.0 41.7 jit_solution(8207308668864008920)
XLA Ops:
  0.6 0.0 copy-start.6
  0.6 0.0 copy-start.3
  0.7 0.0 copy-start.8
  0.7 0.0 copy-start.7
  0.7 1.6 %shard_map.142.refs_0_ = f32[280,128]{1,0:T(8,128)} custom-call(f32[1,1,16,512]{3,2,1,0:T(8,128)} %refs_0_.3, f32[1,1,16,256]{3,2,1,0:T(8,128)} %refs_1_.5, f32[1,1,32,256]{3,2,1,0:T(8,128)} %refs_2_.5, f32[1,1,32,128]{3,2,1,0:T(8,128)} %refs_3_.5, f32[1,1,16,128]{3,2,1,0:T(8,128)} %refs_4_.3, f32[1,1,32,128]{3,2,1,0:T(8,128)} %refs_5_.3, ...), custom_call_target="tpu_custom_call" | custom-call | bytes 3690000 | tf_op jit(solution)/shard_map/pallas_call | solution.py:197
  2.3 3.0 %collective-permute-start.3 = (f32[280,128]{1,0:T(8,128)}, f32[280,128]{1,0:T(8,128)S(1)}, u32[]{:S(2)}, u32[]{:S(2)}) collective-permute-start(f32[280,128]{1,0:T(8,128)} %shard_map.142.refs_0_), channel_id=1, source_target_pairs={{0,1},{1,0},{2,3},{3,2},{4,5},{5,4},{6,7},{7,6},{8,9},{9,8},{10,11... | collective-permute-start | bytes 430088 | tf_op jit(solution)/shard_map/ppermute | solution.py:19
  5.3 0.0 copy-done.6
  5.3 0.0 copy-done.3
  5.3 0.0 copy-done.8
  5.3 0.0 copy-done.7
  5.3 0.0 copy-start
  5.3 1.2 %copy-done = f32[1,1,4,128,512]{4,3,2,1,0:T(8,128)S(1)} copy-done((f32[1,1,4,128,512]{4,3,2,1,0:T(8,128)S(1)}, f32[1,1,4,128,512]{4,3,2,1,0:T(8,128)}, u32[]{:S(2)}) %copy-start) | copy-done | bytes 1048600
  6.6 0.0 copy-start.4
  6.6 0.9 %copy-done.4 = f32[1,1,3,128,128]{4,3,2,1,0:T(8,128)S(1)} copy-done((f32[1,1,3,128,128]{4,3,2,1,0:T(8,128)S(1)}, f32[1,1,3,128,128]{4,3,2,1,0:T(8,128)}, u32[]{:S(2)}) %copy-start.4) | copy-done | bytes 196632
  7.5 0.0 copy-start.2
  7.5 2.1 %shard_map.140 = (f32[8,512]{1,0:T(8,128)S(1)}, f32[8,1152]{1,0:T(8,128)S(1)}) custom-call(f32[1,1,8,512]{3,2,1,0:T(8,128)S(1)} %copy-done.7, f32[1,1,4,128,128]{4,3,2,1,0:T(8,128)S(1)} %copy-done.3, f32[1,1,3,128,128]{4,3,2,1,0:T(8,128)S(1)} %copy-done.4, f32[1,1,8,96]{3,2,1,0:T(8,128)S(1)} %copy-done.8, s32[1,1,4,128]{3,2,1,0:T(4,128)S(1)} %copy-done.6, ...), custom_call_target="tpu_custom_call" | custom-call | bytes 7380000 | tf_op jit(solution)/shard_map/pallas_call | solution.py:197
  9.6 0.0 collective-permute-start
  9.6 1.2 %collective-permute-done.refs_1_ = f32[8,1152]{1,0:T(8,128)S(1)} collective-permute-done((f32[8,1152]{1,0:T(8,128)S(1)}, f32[8,1152]{1,0:T(8,128)S(1)}, u32[]{:S(2)}, u32[]{:S(2)}) %collective-permute-start) | collective-permute-done | bytes 36896 | tf_op jit(solution)/shard_map/ppermute | solution.py:19
  10.8 0.0 collective-permute-done.3.refs_1_
  10.8 0.0 copy-done.2
  10.9 1.6 %collective-permute-start.6 = (f32[432,128]{1,0:T(8,128)S(1)}, f32[432,128]{1,0:T(8,128)S(1)}, u32[]{:S(2)}, u32[]{:S(2)}) collective-permute-start(f32[432,128]{1,0:T(8,128)S(1)} %get-tuple-element.53), channel_id=1, source_target_pairs={{0,8},{1,9},{2,10},{3,11},{4,12},{5,13},{6,14},{7,15},{8,0},{9,1},... | collective-permute-start | bytes 663560 | tf_op jit(solution)/shard_map/ppermute | solution.py:19
  12.5 0.0 collective-permute-start.2
  12.5 0.5 %collective-permute-start.4 = (f32[280,128]{1,0:T(8,128)S(1)}, f32[280,128]{1,0:T(8,128)S(1)}, u32[]{:S(2)}, u32[]{:S(2)}) collective-permute-start(f32[280,128]{1,0:T(8,128)S(1)} %get-tuple-element.47.refs_2_.refs_1_), channel_id=1, source_target_pairs={{0,4},{1,5},{2,6},{3,7},{4,0},{5,1},{6,2},{7,3},{8,12},{9,13},{10,... | collective-permute-start | bytes 430088 | tf_op jit(solution)/shard_map/ppermute | solution.py:19
  13.0 0.5 %collective-permute-start.1 = (f32[8,1152]{1,0:T(8,128)S(1)}, f32[8,1152]{1,0:T(8,128)S(1)}, u32[]{:S(2)}, u32[]{:S(2)}) collective-permute-start(f32[8,1152]{1,0:T(8,128)S(1)} %shard_map.141.refs_2_.refs_0_), channel_id=1, source_target_pairs={{0,1},{1,0},{2,3},{3,2},{4,5},{5,4},{6,7},{7,6},{8,9},{9,8},{10,11... | collective-permute-start | bytes 110600 | tf_op jit(solution)/shard_map/ppermute | solution.py:19
  13.5 0.3 collective-permute-done.2.refs_1_
  13.9 0.2 collective-permute-done.4.refs_3_
  14.1 0.2 shard_map.144
  14.3 2.7 %collective-permute-done.1.refs_1_ = f32[8,1152]{1,0:T(8,128)S(1)} collective-permute-done((f32[8,1152]{1,0:T(8,128)S(1)}, f32[8,1152]{1,0:T(8,128)S(1)}, u32[]{:S(2)}, u32[]{:S(2)}) %collective-permute-start.1) | collective-permute-done | bytes 36896 | tf_op jit(solution)/shard_map/ppermute | solution.py:19
  17.0 0.3 shard_map.145
  17.3 1.1 %collective-permute-done.6.refs_2_ = f32[432,128]{1,0:T(8,128)S(1)} collective-permute-done((f32[432,128]{1,0:T(8,128)S(1)}, f32[432,128]{1,0:T(8,128)S(1)}, u32[]{:S(2)}, u32[]{:S(2)}) %collective-permute-start.6) | collective-permute-done | bytes 221216 | tf_op jit(solution)/shard_map/ppermute | solution.py:19
  18.4 1.6 %collective-permute-start.9 = (f32[480,128]{1,0:T(8,128)S(1)}, f32[480,128]{1,0:T(8,128)S(1)}, u32[]{:S(2)}, u32[]{:S(2)}) collective-permute-start(f32[480,128]{1,0:T(8,128)S(1)} %get-tuple-element.66), channel_id=1, source_target_pairs={{0,2},{1,3},{2,0},{3,1},{4,6},{5,7},{6,4},{7,5},{8,10},{9,11},{10,... | collective-permute-start | bytes 737288 | tf_op jit(solution)/shard_map/ppermute | solution.py:19
  20.0 0.0 collective-permute-start.7
  20.0 1.6 %collective-permute-start.5 = (f32[8,1024]{1,0:T(8,128)S(1)}, f32[8,1024]{1,0:T(8,128)S(1)}, u32[]{:S(2)}, u32[]{:S(2)}) collective-permute-start(f32[8,1024]{1,0:T(8,128)S(1)} %get-tuple-element.52.refs_3_.refs_0_), channel_id=1, source_target_pairs={{0,8},{1,9},{2,10},{3,11},{4,12},{5,13},{6,14},{7,15},{8,0},{9,1},... | collective-permute-start | bytes 98312 | tf_op jit(solution)/shard_map/ppermute | solution.py:19
  21.6 0.3 shard_map.148
  21.9 0.0 collective-permute-done.7.refs_5_
  21.9 0.3 shard_map.147
  22.2 1.7 %collective-permute-done.5.refs_1_ = f32[8,1024]{1,0:T(8,128)S(1)} collective-permute-done((f32[8,1024]{1,0:T(8,128)S(1)}, f32[8,1024]{1,0:T(8,128)S(1)}, u32[]{:S(2)}, u32[]{:S(2)}) %collective-permute-start.5) | collective-permute-done | bytes 32800 | tf_op jit(solution)/shard_map/ppermute | solution.py:19
  24.0 0.4 shard_map.149
  24.3 1.4 %collective-permute-done.9.refs_3_ = f32[480,128]{1,0:T(8,128)S(1)} collective-permute-done((f32[480,128]{1,0:T(8,128)S(1)}, f32[480,128]{1,0:T(8,128)S(1)}, u32[]{:S(2)}, u32[]{:S(2)}) %collective-permute-start.9) | collective-permute-done | bytes 245792 | tf_op jit(solution)/shard_map/ppermute | solution.py:19
  25.7 0.1 collective-permute-start.10
  25.8 1.6 %collective-permute-start.8 = (f32[8,768]{1,0:T(8,128)S(1)}, f32[8,768]{1,0:T(8,128)S(1)}, u32[]{:S(2)}, u32[]{:S(2)}) collective-permute-start(f32[8,768]{1,0:T(8,128)S(1)} %get-tuple-element.61.refs_6_.refs_4_.refs_0_), channel_id=1, source_target_pairs={{0,2},{1,3},{2,0},{3,1},{4,6},{5,7},{6,4},{7,5},{8,10},{9,11},{10,... | collective-permute-start | bytes 73736 | tf_op jit(solution)/shard_map/ppermute | solution.py:19
  27.4 0.4 shard_map.153
  27.7 0.0 copy-start.1
  27.8 0.4 %shard_map.150 = (bf16[128,256]{1,0:T(8,128)(2,1)S(1)}, bf16[128,256]{1,0:T(8,128)(2,1)S(1)}, bf16[128,512]{1,0:T(8,128)(2,1)S(1)}, bf16[128,512]{1,0:T(8,128)(2,1)S(1)}) custom-call(f32[280,128]{1,0:T(8,128)S(1)} %copy-done.2, f32[280,128]{1,0:T(8,128)S(1)} %collective-permute-done.2.refs_1_, f32[280,128]{1,0:T(8,128)S(1)} %get-tuple-element.47.refs_2_.refs_1_, ...), custom_call_target="tpu_custom_call" | custom-call | bytes 1476000 | tf_op jit(solution)/shard_map/pallas_call | solution.py:197
  28.2 0.0 collective-permute-done.10.refs_1_.refs_7_
  28.2 0.4 %shard_map.152 = (bf16[128,256]{1,0:T(8,128)(2,1)S(1)}, bf16[128,256]{1,0:T(8,128)(2,1)S(1)}, bf16[128,512]{1,0:T(8,128)(2,1)S(1)}, bf16[128,512]{1,0:T(8,128)(2,1)S(1)}) custom-call(f32[480,128]{1,0:T(8,128)S(1)} %shard_map.151.refs_0_.refs_6_, f32[480,128]{1,0:T(8,128)S(1)} %collective-permute-done.10.refs_1_.refs_7_), custom_call_target="tpu_custom_call" | custom-call | bytes 1476000 | tf_op jit(solution)/shard_map/pallas_call | solution.py:197
  28.7 1.0 %collective-permute-done.8.refs_1_ = f32[8,768]{1,0:T(8,128)S(1)} collective-permute-done((f32[8,768]{1,0:T(8,128)S(1)}, f32[8,768]{1,0:T(8,128)S(1)}, u32[]{:S(2)}, u32[]{:S(2)}) %collective-permute-start.8) | collective-permute-done | bytes 24608 | tf_op jit(solution)/shard_map/ppermute | solution.py:19
  29.7 0.0 copy-start.5
  29.7 0.4 shard_map.154
  30.1 2.7 %collective-permute-start.11 = (f32[8,512]{1,0:T(8,128)S(1)}, f32[8,512]{1,0:T(8,128)S(1)}, u32[]{:S(2)}, u32[]{:S(2)}) collective-permute-start(f32[8,512]{1,0:T(8,128)S(1)} %get-tuple-element.73.refs_4_.refs_0_), channel_id=1, source_target_pairs={{0,16},{1,17},{2,18},{3,19},{4,20},{5,21},{6,22},{7,23},{8,24},{9,... | collective-permute-start | bytes 49160 | tf_op jit(solution)/shard_map/ppermute | solution.py:19
  32.8 0.0 copy-done.1
  32.8 0.0 copy-done.5
  32.8 1.0 %shard_map.156 = (f32[8,512]{1,0:T(8,128)S(1)}, bf16[256,512]{1,0:T(8,128)(2,1)S(1)}, bf16[256,512]{1,0:T(8,128)(2,1)S(1)}) custom-call(f32[8,512]{1,0:T(8,128)S(1)} %get-tuple-element.76.refs_0_, f32[1,1,4,128,512]{4,3,2,1,0:T(8,128)S(1)} %copy-done.1, f32[1,1,4,128,128]{4,3,2,1,0:T(8,128)S(1)} %copy-done.3, f32[1,1,3,128,128]{4,3,2,1,0:T(8,128)S(1)} %copy-done.5, ...), custom_call_target="tpu_custom_call" | custom-call | bytes 3690000 | tf_op jit(solution)/shard_map/pallas_call | solution.py:197
  33.8 0.1 shard_map.155
  33.8 1.0 %collective-permute-done.11.refs_1_ = f32[8,512]{1,0:T(8,128)S(1)} collective-permute-done((f32[8,512]{1,0:T(8,128)S(1)}, f32[8,512]{1,0:T(8,128)S(1)}, u32[]{:S(2)}, u32[]{:S(2)}) %collective-permute-start.11) | collective-permute-done | bytes 16416 | tf_op jit(solution)/shard_map/ppermute | solution.py:19
  34.8 0.5 %shard_map.157.refs_0_ = f32[8,512]{1,0:T(8,128)S(1)} custom-call(f32[8,512]{1,0:T(8,128)S(1)} %get-tuple-element.73.refs_4_.refs_0_, f32[8,512]{1,0:T(8,128)S(1)} %collective-permute-done.11.refs_1_, bf16[256,512]{1,0:T(8,128)(2,1)S(1)} %get-tuple-element.74.refs_2_, bf16[256,512]{1,0:T(8,128)(2,1)S(1)} %get-tuple-element.75.refs_3_, ...), custom_call_target="tpu_custom_call" | custom-call | bytes 1845000 | tf_op jit(solution)/shard_map/pallas_call | solution.py:197
  35.3 2.6 %collective-permute-start.12 = (f32[8,512]{1,0:T(8,128)S(1)}, f32[8,512]{1,0:T(8,128)S(1)}, u32[]{:S(2)}, u32[]{:S(2)}) collective-permute-start(f32[8,512]{1,0:T(8,128)S(1)} %shard_map.157.refs_0_), channel_id=1, source_target_pairs={{0,16},{1,17},{2,18},{3,19},{4,20},{5,21},{6,22},{7,23},{8,24},{9,... | collective-permute-start | bytes 49160 | tf_op jit(solution)/shard_map/ppermute | solution.py:19
  37.9 1.5 %shard_map.159 = (f32[8,512]{1,0:T(8,128)}, bf16[256,512]{1,0:T(8,128)(2,1)S(1)}, bf16[256,512]{1,0:T(8,128)(2,1)S(1)}) custom-call(f32[8,512]{1,0:T(8,128)S(1)} %get-tuple-element.76.refs_0_, f32[1,1,4,128,512]{4,3,2,1,0:T(8,128)S(1)} %copy-done.1, f32[1,1,4,128,128]{4,3,2,1,0:T(8,128)S(1)} %copy-done.3, f32[1,1,3,128,128]{4,3,2,1,0:T(8,128)S(1)} %copy-done.5, ...), custom_call_target="tpu_custom_call" | custom-call | bytes 3690000 | tf_op jit(solution)/shard_map/pallas_call | solution.py:197
  39.5 0.8 %shard_map.158 = (f32[8,256]{1,0:T(8,128)S(1)}, bf16[512,256]{1,0:T(8,128)(2,1)S(1)}, bf16[512,256]{1,0:T(8,128)(2,1)S(1)}) custom-call(f32[8,256]{1,0:T(8,128)S(1)} %get-tuple-element.78.refs_0_, bf16[128,256]{1,0:T(8,128)(2,1)S(1)} %get-tuple-element.62.refs_2_.refs_1_, bf16[128,256]{1,0:T(8,128)(2,1)S(1)} %get-tuple-element.63.refs_3_.refs_2_, ...), custom_call_target="tpu_custom_call" | custom-call | bytes 1845000 | tf_op jit(solution)/shard_map/pallas_call | solution.py:197
  40.2 0.0 collective-permute-done.12.refs_1_
  40.2 1.5 %shard_map.160 = (f32[1,1,8,512]{3,2,1,0:T(8,128)}, f32[1,1,8,96]{3,2,1,0:T(8,128)}) custom-call(f32[8,512]{1,0:T(8,128)S(1)} %shard_map.157.refs_0_, f32[8,512]{1,0:T(8,128)S(1)} %collective-permute-done.12.refs_1_, f32[8,256]{1,0:T(8,128)S(1)} %get-tuple-element.79.refs_2_, bf16[512,256]{1,0:T(8,128)(2,1)S(1)} %get-tuple-element.80.refs_3_, ...), custom_call_target="tpu_custom_call" | custom-call | bytes 7380000 | tf_op jit(solution)/shard_map/pallas_call | solution.py:197
  (4 shorter events, 0.1 us)
Async XLA Ops:
  0.6 4.7 %copy-start.6 = (s32[1,1,4,128]{3,2,1,0:T(4,128)S(1)}, s32[1,1,4,128]{3,2,1,0:T(4,128)}, u32[]{:S(2)}) copy-start(s32[1,1,4,128]{3,2,1,0:T(4,128)} %refs_16_.1) | copy-start | bytes 6148
  0.6 4.7 %copy-start.3 = (f32[1,1,4,128,128]{4,3,2,1,0:T(8,128)S(1)}, f32[1,1,4,128,128]{4,3,2,1,0:T(8,128)}, u32[]{:S(2)}) copy-start(f32[1,1,4,128,128]{4,3,2,1,0:T(8,128)} %refs_2_.7) | copy-start | bytes 786436
  0.7 4.7 %copy-start.8 = (f32[1,1,8,96]{3,2,1,0:T(8,128)S(1)}, f32[1,1,8,96]{3,2,1,0:T(8,128)}, u32[]{:S(2)}) copy-start(f32[1,1,8,96]{3,2,1,0:T(8,128)} %refs_3_.4) | copy-start | bytes 9220
  0.7 4.7 %copy-start.7 = (f32[1,1,8,512]{3,2,1,0:T(8,128)S(1)}, f32[1,1,8,512]{3,2,1,0:T(8,128)}, u32[]{:S(2)}) copy-start(f32[1,1,8,512]{3,2,1,0:T(8,128)} %refs_0_.2) | copy-start | bytes 49156
  2.3 8.5 %collective-permute-start.3 = (f32[280,128]{1,0:T(8,128)}, f32[280,128]{1,0:T(8,128)S(1)}, u32[]{:S(2)}, u32[]{:S(2)}) collective-permute-start(f32[280,128]{1,0:T(8,128)} %shard_map.142.refs_0_), channel_id=1, source_target_pairs={{0,1},{1,0},{2,3},{3,2},{4,5},{5,4},{6,7},{7,6},{8,9},{9,8},{10,11... | collective-permute-start | bytes 430088 | tf_op jit(solution)/shard_map/ppermute | solution.py:19
  5.3 1.2 %copy-start = (f32[1,1,4,128,512]{4,3,2,1,0:T(8,128)S(1)}, f32[1,1,4,128,512]{4,3,2,1,0:T(8,128)}, u32[]{:S(2)}) copy-start(f32[1,1,4,128,512]{4,3,2,1,0:T(8,128)} %refs_1_.7) | copy-start | bytes 3145732
  6.6 0.9 %copy-start.4 = (f32[1,1,3,128,128]{4,3,2,1,0:T(8,128)S(1)}, f32[1,1,3,128,128]{4,3,2,1,0:T(8,128)}, u32[]{:S(2)}) copy-start(f32[1,1,3,128,128]{4,3,2,1,0:T(8,128)} %refs_3_.7) | copy-start | bytes 589828
  7.5 3.3 %copy-start.2 = (f32[280,128]{1,0:T(8,128)S(1)}, f32[280,128]{1,0:T(8,128)}, u32[]{:S(2)}) copy-start(f32[280,128]{1,0:T(8,128)} %shard_map.142.refs_0_) | copy-start | bytes 430084
  9.6 1.2 %collective-permute-start = (f32[8,1152]{1,0:T(8,128)S(1)}, f32[8,1152]{1,0:T(8,128)S(1)}, u32[]{:S(2)}, u32[]{:S(2)}) collective-permute-start(f32[8,1152]{1,0:T(8,128)S(1)} %get-tuple-element.46.refs_0_), channel_id=1, source_target_pairs={{0,4},{1,5},{2,6},{3,7},{4,0},{5,1},{6,2},{7,3},{8,12},{9,13},{10,... | collective-permute-start | bytes 110600 | tf_op jit(solution)/shard_map/ppermute | solution.py:19
  10.9 7.6 %collective-permute-start.6 = (f32[432,128]{1,0:T(8,128)S(1)}, f32[432,128]{1,0:T(8,128)S(1)}, u32[]{:S(2)}, u32[]{:S(2)}) collective-permute-start(f32[432,128]{1,0:T(8,128)S(1)} %get-tuple-element.53), channel_id=1, source_target_pairs={{0,8},{1,9},{2,10},{3,11},{4,12},{5,13},{6,14},{7,15},{8,0},{9,1},... | collective-permute-start | bytes 663560 | tf_op jit(solution)/shard_map/ppermute | solution.py:19
  12.5 1.4 %collective-permute-start.2 = (f32[280,128]{1,0:T(8,128)S(1)}, f32[280,128]{1,0:T(8,128)S(1)}, u32[]{:S(2)}, u32[]{:S(2)}) collective-permute-start(f32[280,128]{1,0:T(8,128)S(1)} %copy-done.2), channel_id=1, source_target_pairs={{0,4},{1,5},{2,6},{3,7},{4,0},{5,1},{6,2},{7,3},{8,12},{9,13},{10,... | collective-permute-start | bytes 430088 | tf_op jit(solution)/shard_map/ppermute | solution.py:19
  12.5 1.6 %collective-permute-start.4 = (f32[280,128]{1,0:T(8,128)S(1)}, f32[280,128]{1,0:T(8,128)S(1)}, u32[]{:S(2)}, u32[]{:S(2)}) collective-permute-start(f32[280,128]{1,0:T(8,128)S(1)} %get-tuple-element.47.refs_2_.refs_1_), channel_id=1, source_target_pairs={{0,4},{1,5},{2,6},{3,7},{4,0},{5,1},{6,2},{7,3},{8,12},{9,13},{10,... | collective-permute-start | bytes 430088 | tf_op jit(solution)/shard_map/ppermute | solution.py:19
  13.0 4.0 %collective-permute-start.1 = (f32[8,1152]{1,0:T(8,128)S(1)}, f32[8,1152]{1,0:T(8,128)S(1)}, u32[]{:S(2)}, u32[]{:S(2)}) collective-permute-start(f32[8,1152]{1,0:T(8,128)S(1)} %shard_map.141.refs_2_.refs_0_), channel_id=1, source_target_pairs={{0,1},{1,0},{2,3},{3,2},{4,5},{5,4},{6,7},{7,6},{8,9},{9,8},{10,11... | collective-permute-start | bytes 110600 | tf_op jit(solution)/shard_map/ppermute | solution.py:19
  18.4 7.3 %collective-permute-start.9 = (f32[480,128]{1,0:T(8,128)S(1)}, f32[480,128]{1,0:T(8,128)S(1)}, u32[]{:S(2)}, u32[]{:S(2)}) collective-permute-start(f32[480,128]{1,0:T(8,128)S(1)} %get-tuple-element.66), channel_id=1, source_target_pairs={{0,2},{1,3},{2,0},{3,1},{4,6},{5,7},{6,4},{7,5},{8,10},{9,11},{10,... | collective-permute-start | bytes 737288 | tf_op jit(solution)/shard_map/ppermute | solution.py:19
  20.0 1.9 %collective-permute-start.7 = (f32[432,128]{1,0:T(8,128)S(1)}, f32[432,128]{1,0:T(8,128)S(1)}, u32[]{:S(2)}, u32[]{:S(2)}) collective-permute-start(f32[432,128]{1,0:T(8,128)S(1)} %get-tuple-element.54.refs_4_.refs_2_), channel_id=1, source_target_pairs={{0,4},{1,5},{2,6},{3,7},{4,0},{5,1},{6,2},{7,3},{8,12},{9,13},{10,... | collective-permute-start | bytes 663560 | tf_op jit(solution)/shard_map/ppermute | solution.py:19
  20.0 3.9 %collective-permute-start.5 = (f32[8,1024]{1,0:T(8,128)S(1)}, f32[8,1024]{1,0:T(8,128)S(1)}, u32[]{:S(2)}, u32[]{:S(2)}) collective-permute-start(f32[8,1024]{1,0:T(8,128)S(1)} %get-tuple-element.52.refs_3_.refs_0_), channel_id=1, source_target_pairs={{0,8},{1,9},{2,10},{3,11},{4,12},{5,13},{6,14},{7,15},{8,0},{9,1},... | collective-permute-start | bytes 98312 | tf_op jit(solution)/shard_map/ppermute | solution.py:19
  25.7 2.5 %collective-permute-start.10 = (f32[480,128]{1,0:T(8,128)S(1)}, f32[480,128]{1,0:T(8,128)S(1)}, u32[]{:S(2)}, u32[]{:S(2)}) collective-permute-start(f32[480,128]{1,0:T(8,128)S(1)} %shard_map.151.refs_0_.refs_6_), channel_id=1, source_target_pairs={{0,4},{1,5},{2,6},{3,7},{4,0},{5,1},{6,2},{7,3},{8,12},{9,13},{10,... | collective-permute-start | bytes 737288 | tf_op jit(solution)/shard_map/ppermute | solution.py:19
  25.8 3.9 %collective-permute-start.8 = (f32[8,768]{1,0:T(8,128)S(1)}, f32[8,768]{1,0:T(8,128)S(1)}, u32[]{:S(2)}, u32[]{:S(2)}) collective-permute-start(f32[8,768]{1,0:T(8,128)S(1)} %get-tuple-element.61.refs_6_.refs_4_.refs_0_), channel_id=1, source_target_pairs={{0,2},{1,3},{2,0},{3,1},{4,6},{5,7},{6,4},{7,5},{8,10},{9,11},{10,... | collective-permute-start | bytes 73736 | tf_op jit(solution)/shard_map/ppermute | solution.py:19
  27.7 5.0 %copy-start.1 = (f32[1,1,4,128,512]{4,3,2,1,0:T(8,128)S(1)}, f32[1,1,4,128,512]{4,3,2,1,0:T(8,128)}, u32[]{:S(2)}) copy-start(f32[1,1,4,128,512]{4,3,2,1,0:T(8,128)} %refs_1_.7) | copy-start | bytes 3145732
  29.7 3.1 %copy-start.5 = (f32[1,1,3,128,128]{4,3,2,1,0:T(8,128)S(1)}, f32[1,1,3,128,128]{4,3,2,1,0:T(8,128)}, u32[]{:S(2)}) copy-start(f32[1,1,3,128,128]{4,3,2,1,0:T(8,128)} %refs_3_.7) | copy-start | bytes 589828
  30.1 4.7 %collective-permute-start.11 = (f32[8,512]{1,0:T(8,128)S(1)}, f32[8,512]{1,0:T(8,128)S(1)}, u32[]{:S(2)}, u32[]{:S(2)}) collective-permute-start(f32[8,512]{1,0:T(8,128)S(1)} %get-tuple-element.73.refs_4_.refs_0_), channel_id=1, source_target_pairs={{0,16},{1,17},{2,18},{3,19},{4,20},{5,21},{6,22},{7,23},{8,24},{9,... | collective-permute-start | bytes 49160 | tf_op jit(solution)/shard_map/ppermute | solution.py:19
  35.3 4.9 %collective-permute-start.12 = (f32[8,512]{1,0:T(8,128)S(1)}, f32[8,512]{1,0:T(8,128)S(1)}, u32[]{:S(2)}, u32[]{:S(2)}) collective-permute-start(f32[8,512]{1,0:T(8,128)S(1)} %shard_map.157.refs_0_), channel_id=1, source_target_pairs={{0,16},{1,17},{2,18},{3,19},{4,20},{5,21},{6,22},{7,23},{8,24},{9,... | collective-permute-start | bytes 49160 | tf_op jit(solution)/shard_map/ppermute | solution.py:19

commit v3 on v2

--- a/solution.py
+++ b/solution.py
@@ -12,7 +12,20 @@
 GATHER_BYTES = 8 * 2**20
 VMEM_BYTES = 24 * 2**20
 WHOLE_VMEM_BYTES = 60 * 2**20
-BYTES_A_MICROSECOND = 3_690_000
+FLOPS_A_MICROSECOND = 1_000_000_000
+ARRIVE_US = 0.1
+SOLVE_US = 2.0
+X2_US = 5.0
+NEAR_US = 5.0
+Y2_US = 5.0
+LAST_US = 0.1
+F1_US = 5.0
+F1C_US = 0.1
+SUM_US = 5.0
+TABLE_US = 0.4
+FOLD_US = 0.5
+LEAF_US = 1.0
+ELIM_US = 5.0
 
 
 def from_partner(value, axis, distance):
@@ -202,7 +215,7 @@
         out_specs=[pl.BlockSpec(memory_space=pltpu.VMEM)] * len(outs),
         scratch_shapes=scratch,
         cost_estimate=pl.CostEstimate(
-            flops=0, bytes_accessed=int(microseconds * BYTES_A_MICROSECOND), transcendentals=0
+            flops=int(microseconds * FLOPS_A_MICROSECOND), bytes_accessed=0, transcendentals=0
         ),
         compiler_params=pltpu.CompilerParams(vmem_limit_bytes=limit),
     )(*operands, *after)
@@ -210,30 +223,25 @@
 
 def packed_layout(factors, link_mats):
     starts = {}
+    sets = []
     at = 0
-    for name, rows in (
-        ("f0", factors[0].shape[0] * (factors[0].shape[1] // LANES)),
-        ("f1", factors[1].shape[0] * (factors[1].shape[1] // LANES)),
-        ("l1", link_mats[0].shape[0]),
-        ("places", 8),
-        ("f2", factors[2].shape[0] * (factors[2].shape[1] // LANES)),
-        ("l2", link_mats[1].shape[0]),
-        ("f3", factors[3].shape[0] * (factors[3].shape[1] // LANES)),
-        ("l3", link_mats[2].shape[0]),
-    ):
-        starts[name] = at
-        at += rows
-    return starts, at
-
-
-def pack_body(starts, f0, f1, f2, f3, l1, l2, l3, places, out, numbers, semaphores):
-    moves = [(places.at[0, 0], numbers)]
-    for name, ref in (("f0", f0), ("f1", f1), ("f2", f2), ("f3", f3)):
-        rows, width = ref.shape[2:]
-        for chunk in range(width // LANES):
-            at = starts[name] + chunk * rows
-            moves.append((ref.at[0, 0, :, pl.ds(chunk * LANES, LANES)], out.at[pl.ds(at, rows), :]))
-    for name, ref in (("l1", l1), ("l2", l2), ("l3", l3)):
+    for section, names in enumerate((("f0",), ("f1", "l1", "places"), ("f2", "l2"), ("f3", "l3"))):
+        begin = at
+        for name in names:
+            starts[name] = at
+            if name == "places":
+                at += 8
+            elif name[0] == "f":
+                at += factors[section].shape[0] * (factors[section].shape[1] // LANES)
+            else:
+                at += link_mats[section - 1].shape[0]
+        sets.append((begin, at))
+    return starts, tuple(sets), at
+
+
+def pack_body(starts, part, f0, f1, f2, f3, l1, l2, l3, places, out, tail, s0, s1, s2, numbers, semaphores):
+    moves = [(places.at[0, 0], numbers), (f0.at[0, 0], s0), (f1.at[0, 0], s1), (f2.at[0, 0], s2)]
+    for name, ref in (("f3", f3), ("l1", l1), ("l2", l2), ("l3", l3)):
         moves.append((ref.at[0, 0], out.at[pl.ds(starts[name], ref.shape[2]), :]))
     copies = [
         pltpu.make_async_copy(source, target, semaphores.at[number])
@@ -241,11 +249,18 @@
     ]
     for copy in copies:
         copy.start()
-    copies[0].wait()
+    for copy in copies[:4]:
+        copy.wait()
     positions = numbers[...].astype(jnp.float32)
     out[starts["places"] : starts["places"] + 8, :] = jnp.concatenate([positions, positions], axis=0)
-    for copy in copies[1:]:
+    for name, ref in (("f0", s0), ("f1", s1), ("f2", s2)):
+        rows, width = ref.shape
+        for chunk in range(width // LANES):
+            at = starts[name] + chunk * rows
+            out[at : at + rows, :] = ref[:, chunk * LANES : (chunk + 1) * LANES]
+    for copy in copies[4:]:
         copy.wait()
+    tail[...] = out[part[0] : part[1], :]
 
 
 def own_targets(sizes, owned, taken):
@@ -284,17 +299,16 @@
         at += sizes[section]
 
 
-def gather_body(section, starts, rows, size, above, strides, *refs):
-    outs = refs[len(strides) :]
+def gather_body(section, starts, rows, size, above, places, *refs):
+    outs = refs[len(places) :]
     at = 0
-    for ref, (members, stride) in zip(refs, strides):
-        for member in range(members):
-            base = member * stride
+    for ref, bases in zip(refs, places):
+        for base in bases:
             factor = wide(ref, base + starts["f%d" % section], rows, size // LANES)
             outs[0][at : at + rows, :], outs[1][at : at + rows, :] = halves(factor)
             if section > 0:
-                begin = base + starts["l%d" % section]
-                link = ref[begin : begin + rows, :]
+                place = base + starts["l%d" % section]
+                link = ref[place : place + rows, :]
                 row = base + starts["places"] + section - 1
                 positions = ref[row : row + 1, :].astype(jnp.int32)
                 linked = times(link, [one_hot(positions, above)], True)
@@ -320,24 +334,18 @@
     sums[:, width - size - above :] = rest
 
 
-def top_body(mine, theirs, f_high, f_low, partial):
-    total = mine[...] + theirs[...]
+def top_body(total, f_high, f_low, partial):
     pieces = [f_high[...], f_low[...]]
-    partial[...] = times(times(total, pieces, True), pieces, False)
-
-
-def join_body(prefix, counts, *refs):
-    copy = refs[len(counts)]
-    copy[...] = refs[len(counts) - 1][...]
-    if prefix == 0:
-        return
-    message = refs[len(counts) + 1]
-    at = 0
-    for ref, members in zip(refs, counts):
-        stride = ref.shape[0] // members
-        for member in range(members):
-            message[at : at + prefix, :] = ref[member * stride : member * stride + prefix, :]
-            at += prefix
+    partial[...] = times(times(total[...], pieces, True), pieces, False)
+
+
+def join_body(moves, *refs):
+    for number, start, at, rows in moves:
+        refs[-1][at : at + rows, :] = refs[number][start : start + rows, :]
+
+
+def copy_body(arrived, out):
+    out[...] = arrived[...]
 
 
 def add_body(mine, theirs, out):
@@ -420,111 +428,153 @@
     links = [array.reshape(array.shape[2:]) for array in (link_two, link_three, link_four)]
     sizes = tuple(factor.shape[1] for factor in factors)
     owned = tuple(factor.shape[0] for factor in factors)
-    starts, height = packed_layout(factors, links)
-    heights = {3: height, 2: starts["f3"], 1: starts["f2"]}
+    starts, sets, height = packed_layout(factors, links)
     axes = ("gx", "gy")
     core = gy_bits
     rhs_count = rhs_leaf.shape[2]
-    copies = 1 + sum(size // LANES for size in sizes) + len(links)
-
-    (packed,) = vmem_call(
-        functools.partial(pack_body, starts),
-        [((height, LANES), jnp.float32)],
+    total = sum(sizes)
+
+    part = (sets[1][0], sets[2][1])
+    packed, tail = vmem_call(
+        functools.partial(pack_body, starts, part),
+        [((height, LANES), jnp.float32), ((part[1] - part[0], LANES), jnp.float32)],
         factor_one, factor_two, factor_three, factor_four, link_two, link_three, link_four, interface,
         microseconds=1.0, space=pltpu.HBM, limit=WHOLE_VMEM_BYTES,
-        scratch=(pltpu.VMEM(interface.shape[2:], jnp.int32), pltpu.SemaphoreType.DMA((copies,))),
-    )
-    held = [packed]
-    counts = [1]
-    both = [packed, from_partner(packed, axes, core)]
-    strides = [(1, height), (1, height)]
-
-    def arrive(arrived, stride, prefix, after):
-        held.append(arrived)
-        counts.append(arrived.shape[0] // stride)
-        outs = [(arrived.shape, jnp.float32)]
-        if prefix:
-            outs.append(((sum(counts) * prefix, LANES), jnp.float32))
-        copy, *message = vmem_call(
-            functools.partial(join_body, prefix, tuple(counts)), outs, *held, after=after, microseconds=0.1
+        scratch=[pltpu.VMEM(factor.shape, jnp.float32) for factor in factors[:3]]
+        + [pltpu.VMEM(interface.shape[2:], jnp.int32), pltpu.SemaphoreType.DMA((8,))],
+    )
+
+    everything = (0, 1, 2, 3)
+    whole = ((0, everything),)
+    both = [(packed, whole), (from_partner(packed, axes, core), whole)]
+
+    def plan(wanted):
+        moves, members, at = [], [], 0
+        for number, (_, have) in enumerate(wanted):
+            for base, its_sets, travels in have:
+                first, last = sets[travels[0]][0], sets[travels[-1]][1]
+                moves.append((number, base + first, at, last - first))
+                members.append((at - first, travels))
+                at += last - first
+        return tuple(moves), tuple(members), at
+
+    def choose(buffers, *travels):
+        wanted = []
+        for array, members in buffers:
+            have = []
+            for base, its_sets in members:
+                fit = [run for run in travels if set(run) <= set(its_sets)]
+                if fit:
+                    have.append((base, its_sets, fit[0]))
+            if have:
+                wanted.append((array, tuple(have)))
+        return wanted
+
+    def message(wanted, after, microseconds=ARRIVE_US):
+        moves, members, rows = plan(wanted)
+        (out,) = vmem_call(
+            functools.partial(join_body, moves), [((rows, LANES), jnp.float32)],
+            *[array for array, _ in wanted], after=after, microseconds=microseconds,
         )
-        held[-1] = copy
-        both.extend([copy, from_partner(copy, axes, core)])
-        strides.extend([(counts[-1], stride)] * 2)
-        return message
-
-    def level(section, first, last, after=()):
+        return out, members
+
+    def arrive(arrived, members, after, microseconds=ARRIVE_US):
+        (copy,) = vmem_call(
+            copy_body, [(arrived.shape, jnp.float32)], arrived, after=after, microseconds=microseconds
+        )
+        both.extend([(copy, members), (from_partner(copy, axes, core), members)])
+        return copy, members
+
+    def level(section, buffers, after=()):
         rows, size = factors[section].shape
         above = sizes[section - 1] if section > 0 else 0
-        members = sum(count for count, _ in strides[first:last])
-        outs = [((members * rows, size), jnp.bfloat16)] * 2
+        chosen = choose(buffers, (section,))
+        places = tuple(tuple(base for base, _, _ in have) for _, have in chosen)
+        count = sum(len(bases) for bases in places)
+        outs = [((count * rows, size), jnp.bfloat16)] * 2
         if section > 0:
-            outs = outs + [((members * rows, above), jnp.bfloat16)] * 2
-        body = functools.partial(gather_body, section, starts, rows, size, above, tuple(strides[first:last]))
-        return vmem_call(body, outs, *both[first:last], microseconds=0.4, after=after)
-
-    inner = [bit_number for bit_number in taken[3] if bit_number != core]
-    steps = [(bit_number, 3) for bit_number in inner]
-    steps += [(gy_bits + gx_bits - 2, 2), (gy_bits - 1, 1)]
-    moving = from_partner(packed, axes, steps[0][0])
-    forward, sums = vmem_call(
-        functools.partial(forward_body, sizes, owned, taken),
-        [((rhs_count, rhs_leaf.shape[3]), jnp.float32), ((rhs_count, sum(sizes)), jnp.float32)],
-        rhs_leaf, leaf_inv, leaf_sub, sep_rhs, interface, coupling, microseconds=2.0,
-    )
-    (sums,) = vmem_call(
-        add_body, [((rhs_count, sum(sizes)), jnp.float32)], sums, from_partner(sums, axes, core), microseconds=0.1
-    )
-    folded = [None] * 4
-    late = ()
-    for number, (bit_number, section) in enumerate(steps):
-        theirs = from_partner(sums, axes, bit_number)
-        following = steps[number + 1] if number + 1 < len(steps) else (None, None)
-        prefix = heights[following[1]] if following[1] else 0
-        known = len(both)
-        message = arrive(moving, heights[section], prefix, (sums,))
-        if message:
-            moving = from_partner(message[0], axes, following[0])
-        if following[1] == section:
-            sums = sums + theirs
-            continue
-        if section == 1:
-            tables = [level(section, 0, known, (sums,)), level(section, known, len(both))]
-        else:
-            tables = [level(section, 0, len(both))]
+            outs = outs + [((count * rows, above), jnp.bfloat16)] * 2
+        body = functools.partial(gather_body, section, starts, rows, size, above, places)
+        return vmem_call(body, outs, *[array for array, _ in chosen], microseconds=TABLE_US, after=after)
+
+    def eliminate(section, sums, theirs, tables, after):
         size, above = sizes[section], sizes[section - 1]
         flat = [array for table in tables for array in table]
         sums, found = vmem_call(
             functools.partial(eliminate_body, size, above, len(tables)),
             [((rhs_count, sums.shape[1] - size), jnp.float32), ((rhs_count, size), jnp.float32)],
-            sums, theirs, *flat, microseconds=0.4, after=late,
+            sums, theirs, *flat, microseconds=ELIM_US, after=after,
         )
-        folded[section] = vmem_call(
+        folded = vmem_call(
             functools.partial(fold_body, len(tables)),
             [((rhs_count, size), jnp.float32)] + [((above, size), jnp.bfloat16)] * 2,
-            found, *flat, microseconds=0.5,
+            found, *flat, microseconds=FOLD_US,
         )
-        late = tuple(folded[section][:1])
-    last = gy_bits + gx_bits - 1
-    solves = [
-        vmem_call(
+        return sums, folded
+
+    def solve(sections, after):
+        return vmem_call(
             functools.partial(leaf_body, sections),
-            [((rhs_count, rhs_leaf.shape[3]), jnp.float32)] + [((2 * LANES, rhs_leaf.shape[3]), jnp.bfloat16)] * 2,
-            forward, coupling, leaf_inv, leaf_sub, microseconds=1.0, after=(before,),
+            [((rhs_count, rhs_leaf.shape[3]), jnp.float32)]
+            + [((len(sections) * LANES, rhs_leaf.shape[3]), jnp.bfloat16)] * 2,
+            forward, coupling, leaf_inv, leaf_sub, microseconds=LEAF_US, after=after,
         )
-        for sections, before in (((0, 1), sums), ((2, 3), sums))
-    ]
-    table = level(0, 0, len(both))
-    theirs = from_partner(sums, axes, last)
+
+    inner = min(taken[3]) if core == max(taken[3]) else max(taken[3])
+    third, second, first = gy_bits + gx_bits - 2, gy_bits - 1, gy_bits + gx_bits - 1
+
+    from_inner = from_partner(packed, axes, inner)
+    from_third = from_partner(tail, axes, third)
+    forward, sums = vmem_call(
+        functools.partial(forward_body, sizes, owned, taken),
+        [((rhs_count, rhs_leaf.shape[3]), jnp.float32), ((rhs_count, total), jnp.float32)],
+        rhs_leaf, leaf_inv, leaf_sub, sep_rhs, interface, coupling, microseconds=SOLVE_US,
+    )
+    others = from_partner(sums, axes, core)
+    by_third = arrive(from_third, ((-part[0], (1, 2)),), ())
+    (sums,) = vmem_call(
+        add_body, [((rhs_count, total), jnp.float32)], sums, others, microseconds=0.1, after=(by_third[0],)
+    )
+    theirs = from_partner(sums, axes, inner)
+    by_inner = arrive(from_inner, whole, (sums,))
+    following, two_at = message(choose([by_third], (1, 2)), (sums,))
+    two = from_partner(following, axes, inner)
+    following, near_at = message(choose([both[0], by_inner], (0, 1)), (sums,))
+    near = from_partner(following, axes, second)
+    table = level(3, both)
+    sums, folded_four = eliminate(3, sums, theirs, [table], ())
+
+    theirs = from_partner(sums, axes, third)
+    solved_first = solve((0, 1), (sums,))
+    by_two = arrive(two, two_at, (solved_first[0],), X2_US)
+    by_near = arrive(near, near_at, (solved_first[0],), NEAR_US)
+    following, last_at = message(choose([by_third, by_two], (1,)), (sums,), Y2_US)
+    last = from_partner(following, axes, second)
+    table = level(2, both)
+    sums, folded_three = eliminate(2, sums, theirs, [table], (folded_four[0],))
+
+    theirs = from_partner(sums, axes, second)
+    following, top_at = message(choose([both[0], by_inner, by_near], (0,)), (sums,), F1_US)
+    from_third = from_partner(following, axes, third)
+    early = len(both)
+    arrive(last, last_at, (sums,), LAST_US)
+    tables = [level(1, both[:early], (sums,)), level(1, both[early:], (sums,))]
+    sums, folded_two = eliminate(1, sums, theirs, tables, (folded_three[0],))
+
+    theirs = from_partner(sums, axes, first)
+    arrive(from_third, top_at, (sums,), F1C_US)
+    (sums,) = vmem_call(
+        add_body, [((rhs_count, sizes[0]), jnp.float32)], sums, theirs, microseconds=SUM_US
+    )
     (partial,) = vmem_call(
-        top_body, [((rhs_count, sizes[0]), jnp.float32)],
-        sums, theirs, *table, microseconds=0.5, after=(solves[0][0],),
-    )
-    theirs = from_partner(partial, axes, last)
+        top_body, [((rhs_count, sizes[0]), jnp.float32)], sums, *level(0, both, (sums,)), microseconds=0.5
+    )
+    theirs = from_partner(partial, axes, first)
+    solved_second = solve((2, 3), (partial,))
     leaf, sep = vmem_call(
         functools.partial(backward_body, sizes, owned, taken),
         [(rhs_leaf.shape, jnp.float32), (sep_rhs.shape, jnp.float32)],
-        partial, theirs, *folded[1], *folded[2], *folded[3], *solves[0], *solves[1][1:], interface,
+        partial, theirs, *folded_two, *folded_three, *folded_four, *solved_first, *solved_second[1:], interface,
         microseconds=2.0,
     )
     return (leaf, sep)
@@ -535,7 +585,9 @@
     bits = lax.axis_size("gy").bit_length() + lax.axis_size("gx").bit_length() - 2
     for level, array in enumerate(arrays[6:10]):
         gathered_bytes += array.size * 4 << (bits - level)
-    if gathered_bytes > GATHER_BYTES:
+    gy_bits = lax.axis_size("gy").bit_length() - 1
+    fourth = taken_lists(gy_bits, bits - gy_bits)[3]
+    if gathered_bytes > GATHER_BYTES or len(fourth) != 2 or gy_bits not in fourth:
         return level_by_level(*arrays)
     return gathered(*arrays)
 

time: 42 us -> 36.6 us (0.87)
  waiting for transfers between devices: 10.7 us -> 4 us
  starting transfers between devices: 15.8 us -> 19 us
  local copies, waits for them, and re-layouts: 2.18 us -> 0.03 us
    ppermute x13 -> x19, waiting for transfers between devices: 10.7 us -> 4 us  [from_partner(): lax.ppermute(value, axis, [(i, i ^ 1 << distance) for i in range(lax.axis...]
    ppermute x13 -> x19, starting transfers between devices: 15.8 us -> 19 us  [from_partner(): lax.ppermute(value, axis, [(i, i ^ 1 << distance) for i in range(lax.axis...]
    unnamed x18 -> x14, local copies, waits for them, and re-layouts: 2.18 us -> 0.03 us
    pallas_call x21 -> x29, Pallas kernels: 12.3 us -> 12.4 us  [vmem_call(): pl.pallas_call(kernel, out_shape=out_shape, in_specs=[pl.BlockSpec(memory...]
  transfers between devices with their start and end apart: 13 -> 19, of which waited for: 9 -> 7; matrix products, arithmetic and copies ran while one was open for 0% -> 0% of each run, Pallas kernels for 20% -> 24%
where the time goes in v3:
time: 36.6 us; the launch traced here: 36.3 us
  starting transfers between devices  19 us (52%)
  Pallas kernels  12.4 us (34%)
  waiting for transfers between devices  4 us (11%)
  between operations  0.91 us (2%)
    ppermute x19, starting transfers between devices, from_partner(): lax.ppermute(value, axis, [(i, i ^ 1 << distance) for i in range(lax.axis...  19 us
    pallas_call x29, Pallas kernels, vmem_call(): pl.pallas_call(kernel, out_shape=out_shape, in_specs=[pl.BlockSpec(memory...  12.4 us
    ppermute x19, waiting for transfers between devices, from_partner(): lax.ppermute(value, axis, [(i, i ^ 1 << distance) for i in range(lax.axis...  4 us
  transfers between devices with their start and end apart: 19, of which 7 were waited for; matrix products, arithmetic and copies ran while one was open for 0% of the time, Pallas kernels for 24%

profile of v3, /device:TPU:0, one launch (start us, length us, event | category | flops | bytes accessed | tf_op | source)
XLA Modules:
  0.0 36.3 jit_solution(10402692267112657640)
XLA Ops:
  0.6 0.0 copy-start.1
  0.6 0.0 copy-start.3
  0.7 0.0 copy-start.2
  0.7 0.0 copy-start.5
  0.7 1.7 %shard_map.141 = (f32[280,128]{1,0:T(8,128)}, f32[152,128]{1,0:T(8,128)}) custom-call(f32[1,1,16,512]{3,2,1,0:T(8,128)} %refs_0_.3, f32[1,1,16,256]{3,2,1,0:T(8,128)} %refs_1_.5, f32[1,1,32,256]{3,2,1,0:T(8,128)} %refs_2_.5, f32[1,1,32,128]{3,2,1,0:T(8,128)} %refs_3_.5, f32[1,1,16,128]{3,2,1,0:T(8,128)} %refs_4_.3, f32[1,1,32,128]{3,2,1,0:T(8,128)} %refs_5_.3, ...), custom_call_target="tpu_custom_call" | custom-call | flops 1000000000 | tf_op jit(solution)/shard_map/pallas_call | solution.py:210
  2.4 0.0 copy-start.6
  2.4 3.1 %collective-permute-start.1 = (f32[152,128]{1,0:T(8,128)}, f32[152,128]{1,0:T(8,128)S(1)}, u32[]{:S(2)}, u32[]{:S(2)}) collective-permute-start(f32[152,128]{1,0:T(8,128)} %get-tuple-element.45), channel_id=1, source_target_pairs={{0,8},{1,9},{2,10},{3,11},{4,12},{5,13},{6,14},{7,15},{8,0},{9,1},... | collective-permute-start | bytes 233480 | tf_op jit(solution)/shard_map/ppermute | solution.py:32
  5.5 1.5 %collective-permute-start.4 = (f32[280,128]{1,0:T(8,128)}, f32[280,128]{1,0:T(8,128)S(1)}, u32[]{:S(2)}, u32[]{:S(2)}) collective-permute-start(f32[280,128]{1,0:T(8,128)} %get-tuple-element.46.refs_0_), channel_id=1, source_target_pairs={{0,1},{1,0},{2,3},{3,2},{4,5},{5,4},{6,7},{7,6},{8,9},{9,8},{10,11... | collective-permute-start | bytes 430088 | tf_op jit(solution)/shard_map/ppermute | solution.py:32
  7.0 0.0 copy-done.1
  7.0 0.0 copy-done.4
  7.0 0.0 copy-done.6
  7.0 2.1 %shard_map.140 = (f32[8,512]{1,0:T(8,128)S(1)}, f32[8,1152]{1,0:T(8,128)S(1)}) custom-call(f32[1,1,8,512]{3,2,1,0:T(8,128)S(1)} %copy-done.4, f32[1,1,4,128,128]{4,3,2,1,0:T(8,128)S(1)} %copy-done.2, f32[1,1,3,128,128]{4,3,2,1,0:T(8,128)S(1)} %copy-done.3, f32[1,1,8,96]{3,2,1,0:T(8,128)S(1)} %copy-done.5, s32[1,1,4,128]{3,2,1,0:T(4,128)S(1)} %copy-done.6, ...), custom_call_target="tpu_custom_call" | custom-call | flops 2000000000 | tf_op jit(solution)/shard_map/pallas_call | solution.py:210
  9.1 0.0 collective-permute-start
  9.1 0.0 copy-done
  9.1 0.5 %collective-permute-start.3 = (f32[280,128]{1,0:T(8,128)S(1)}, f32[280,128]{1,0:T(8,128)S(1)}, u32[]{:S(2)}, u32[]{:S(2)}) collective-permute-start(f32[280,128]{1,0:T(8,128)S(1)} %copy-done), channel_id=1, source_target_pairs={{0,4},{1,5},{2,6},{3,7},{4,0},{5,1},{6,2},{7,3},{8,12},{9,13},{10,... | collective-permute-start | bytes 430088 | tf_op jit(solution)/shard_map/ppermute | solution.py:32
  9.6 0.0 collective-permute-done.1.refs_0_
  9.6 0.7 %collective-permute-done.refs_1_ = f32[8,1152]{1,0:T(8,128)S(1)} collective-permute-done((f32[8,1152]{1,0:T(8,128)S(1)}, f32[8,1152]{1,0:T(8,128)S(1)}, u32[]{:S(2)}, u32[]{:S(2)}) %collective-permute-start) | collective-permute-done | bytes 36896 | tf_op jit(solution)/shard_map/ppermute | solution.py:32
  10.3 0.6 %collective-permute-done.4.refs_0_ = f32[280,128]{1,0:T(8,128)S(1)} collective-permute-done((f32[280,128]{1,0:T(8,128)}, f32[280,128]{1,0:T(8,128)S(1)}, u32[]{:S(2)}, u32[]{:S(2)}) %collective-permute-start.4) | collective-permute-done | bytes 143392 | tf_op jit(solution)/shard_map/ppermute | solution.py:32
  10.9 0.1 collective-permute-start.5
  11.0 1.6 %collective-permute-start.2 = (f32[8,1152]{1,0:T(8,128)S(1)}, f32[8,1152]{1,0:T(8,128)S(1)}, u32[]{:S(2)}, u32[]{:S(2)}) collective-permute-start(f32[8,1152]{1,0:T(8,128)S(1)} %shard_map.143.refs_1_.refs_0_.refs_2_), channel_id=1, source_target_pairs={{0,1},{1,0},{2,3},{3,2},{4,5},{5,4},{6,7},{7,6},{8,9},{9,8},{10,11... | collective-permute-start | bytes 110600 | tf_op jit(solution)/shard_map/ppermute | solution.py:32
  12.6 0.2 collective-permute-start.7
  12.7 0.5 %collective-permute-start.8 = (f32[152,128]{1,0:T(8,128)S(1)}, f32[152,128]{1,0:T(8,128)S(1)}, u32[]{:S(2)}, u32[]{:S(2)}) collective-permute-start(f32[152,128]{1,0:T(8,128)S(1)} %shard_map.147), channel_id=1, source_target_pairs={{0,1},{1,0},{2,3},{3,2},{4,5},{5,4},{6,7},{7,6},{8,9},{9,8},{10,11... | collective-permute-start | bytes 233480 | tf_op jit(solution)/shard_map/ppermute | solution.py:32
  13.3 0.0 collective-permute-done.3.refs_1_
  13.3 1.6 %collective-permute-start.11 = (f32[240,128]{1,0:T(8,128)S(1)}, f32[240,128]{1,0:T(8,128)S(1)}, u32[]{:S(2)}, u32[]{:S(2)}) collective-permute-start(f32[240,128]{1,0:T(8,128)S(1)} %shard_map.153), channel_id=1, source_target_pairs={{0,2},{1,3},{2,0},{3,1},{4,6},{5,7},{6,4},{7,5},{8,10},{9,11},{10,... | collective-permute-start | bytes 368648 | tf_op jit(solution)/shard_map/ppermute | solution.py:32
  14.9 0.0 collective-permute-done.5.refs_3_.refs_5_
  14.9 0.2 shard_map.145
  15.1 0.0 collective-permute-done.2.refs_1_
  15.1 0.3 shard_map.146
  15.4 0.5 %collective-permute-start.6 = (f32[8,1024]{1,0:T(8,128)S(1)}, f32[8,1024]{1,0:T(8,128)S(1)}, u32[]{:S(2)}, u32[]{:S(2)}) collective-permute-start(f32[8,1024]{1,0:T(8,128)S(1)} %get-tuple-element.51.refs_4_.refs_0_.refs_2_), channel_id=1, source_target_pairs={{0,8},{1,9},{2,10},{3,11},{4,12},{5,13},{6,14},{7,15},{8,0},{9,1},... | collective-permute-start | bytes 98312 | tf_op jit(solution)/shard_map/ppermute | solution.py:32
  15.9 1.0 %shard_map.148 = (f32[8,512]{1,0:T(8,128)S(1)}, bf16[256,512]{1,0:T(8,128)(2,1)S(1)}, bf16[256,512]{1,0:T(8,128)(2,1)S(1)}) custom-call(f32[8,512]{1,0:T(8,128)S(1)} %get-tuple-element.52.refs_0_, f32[1,1,4,128,512]{4,3,2,1,0:T(8,128)S(1)} %copy-done.1, f32[1,1,4,128,128]{4,3,2,1,0:T(8,128)S(1)} %copy-done.2, f32[1,1,3,128,128]{4,3,2,1,0:T(8,128)S(1)} %copy-done.3, ...), custom_call_target="tpu_custom_call" | custom-call | flops 1000000000 | tf_op jit(solution)/shard_map/pallas_call | solution.py:210
  16.9 0.4 %collective-permute-done.8.refs_0_ = f32[152,128]{1,0:T(8,128)S(1)} collective-permute-done((f32[152,128]{1,0:T(8,128)S(1)}, f32[152,128]{1,0:T(8,128)S(1)}, u32[]{:S(2)}, u32[]{:S(2)}) %collective-permute-start.8) | collective-permute-done | bytes 77856 | tf_op jit(solution)/shard_map/ppermute | solution.py:32
  17.4 0.1 collective-permute-start.9
  17.4 1.6 %collective-permute-start.13 = (f32[112,128]{1,0:T(8,128)S(1)}, f32[112,128]{1,0:T(8,128)S(1)}, u32[]{:S(2)}, u32[]{:S(2)}) collective-permute-start(f32[112,128]{1,0:T(8,128)S(1)} %shard_map.156), channel_id=1, source_target_pairs={{0,2},{1,3},{2,0},{3,1},{4,6},{5,7},{6,4},{7,5},{8,10},{9,11},{10,... | collective-permute-start | bytes 172040 | tf_op jit(solution)/shard_map/ppermute | solution.py:32
  19.0 0.0 collective-permute-done.11.refs_0_
  19.0 0.2 collective-permute-start.12
  19.3 0.3 shard_map.151
  19.5 0.0 collective-permute-done.7.refs_3_
  19.6 0.0 collective-permute-done.9.refs_7_
  19.6 0.3 shard_map.150
  19.9 0.0 collective-permute-done.6.refs_1_
  19.9 0.4 %shard_map.152 = (f32[8,768]{1,0:T(8,128)S(1)}, f32[8,256]{1,0:T(8,128)S(1)}) custom-call(f32[8,1024]{1,0:T(8,128)S(1)} %get-tuple-element.51.refs_4_.refs_0_.refs_2_, f32[8,1024]{1,0:T(8,128)S(1)} %collective-permute-done.6.refs_1_, bf16[256,256]{1,0:T(8,128)(2,1)S(1)} %get-tuple-element.54.refs_2_.refs_1_, ...), custom_call_target="tpu_custom_call" | custom-call | flops 5000000000 | tf_op jit(solution)/shard_map/pallas_call | solution.py:210
  20.3 1.0 %collective-permute-start.10 = (f32[8,768]{1,0:T(8,128)S(1)}, f32[8,768]{1,0:T(8,128)S(1)}, u32[]{:S(2)}, u32[]{:S(2)}) collective-permute-start(f32[8,768]{1,0:T(8,128)S(1)} %get-tuple-element.60.refs_10_.refs_1_.refs_2_.refs_0_.refs_3_), channel_id=1, source_target_pairs={{0,2},{1,3},{2,0},{3,1},{4,6},{5,7},{6,4},{7,5},{8,10},{9,11},{10,... | collective-permute-start | bytes 73736 | tf_op jit(solution)/shard_map/ppermute | solution.py:32
  21.3 0.5 %collective-permute-done.13.refs_0_ = f32[112,128]{1,0:T(8,128)S(1)} collective-permute-done((f32[112,128]{1,0:T(8,128)S(1)}, f32[112,128]{1,0:T(8,128)S(1)}, u32[]{:S(2)}, u32[]{:S(2)}) %collective-permute-start.13) | collective-permute-done | bytes 57376 | tf_op jit(solution)/shard_map/ppermute | solution.py:32
  21.8 0.0 collective-permute-start.14
  21.8 0.4 shard_map.159
  22.1 1.2 %collective-permute-start.16 = (f32[256,128]{1,0:T(8,128)S(1)}, f32[256,128]{1,0:T(8,128)S(1)}, u32[]{:S(2)}, u32[]{:S(2)}) collective-permute-start(f32[256,128]{1,0:T(8,128)S(1)} %shard_map.162), channel_id=1, source_target_pairs={{0,8},{1,9},{2,10},{3,11},{4,12},{5,13},{6,14},{7,15},{8,0},{9,1},... | collective-permute-start | bytes 393224 | tf_op jit(solution)/shard_map/ppermute | solution.py:32
  23.4 0.0 collective-permute-done.12.refs_9_.refs_5_
  23.4 0.6 %shard_map.155 = (bf16[192,256]{1,0:T(8,128)(2,1)S(1)}, bf16[192,256]{1,0:T(8,128)(2,1)S(1)}, bf16[192,512]{1,0:T(8,128)(2,1)S(1)}, bf16[192,512]{1,0:T(8,128)(2,1)S(1)}) custom-call(f32[280,128]{1,0:T(8,128)S(1)} %copy-done, f32[280,128]{1,0:T(8,128)S(1)} %collective-permute-done.3.refs_1_, f32[152,128]{1,0:T(8,128)S(1)} %shard_map.142.refs_2_.refs_0_, ...), custom_call_target="tpu_custom_call" | custom-call | flops 400000000 | tf_op jit(solution)/shard_map/pallas_call | solution.py:210
  24.0 0.0 collective-permute-done.14.refs_1_
  24.0 0.3 shard_map.158
  24.3 0.0 collective-permute-done.10.refs_1_
  24.3 0.4 %shard_map.160 = (f32[8,512]{1,0:T(8,128)S(1)}, f32[8,256]{1,0:T(8,128)S(1)}) custom-call(f32[8,768]{1,0:T(8,128)S(1)} %get-tuple-element.60.refs_10_.refs_1_.refs_2_.refs_0_.refs_3_, f32[8,768]{1,0:T(8,128)S(1)} %collective-permute-done.10.refs_1_, bf16[192,256]{1,0:T(8,128)(2,1)S(1)} %get-tuple-element.61.refs_2_.refs_1_, ...), custom_call_target="tpu_custom_call" | custom-call | flops 5000000000 | tf_op jit(solution)/shard_map/pallas_call | solution.py:210
  24.7 2.7 %collective-permute-start.15 = (f32[8,512]{1,0:T(8,128)S(1)}, f32[8,512]{1,0:T(8,128)S(1)}, u32[]{:S(2)}, u32[]{:S(2)}) collective-permute-start(f32[8,512]{1,0:T(8,128)S(1)} %get-tuple-element.71.refs_0_.refs_1_), channel_id=1, source_target_pairs={{0,16},{1,17},{2,18},{3,19},{4,20},{5,21},{6,22},{7,23},{8,24},{9,... | collective-permute-start | bytes 49160 | tf_op jit(solution)/shard_map/ppermute | solution.py:32
  27.4 0.8 %shard_map.166 = (f32[8,256]{1,0:T(8,128)S(1)}, bf16[512,256]{1,0:T(8,128)(2,1)S(1)}, bf16[512,256]{1,0:T(8,128)(2,1)S(1)}) custom-call(f32[8,256]{1,0:T(8,128)S(1)} %get-tuple-element.74.refs_0_, bf16[192,256]{1,0:T(8,128)(2,1)S(1)} %get-tuple-element.61.refs_2_.refs_1_, bf16[192,256]{1,0:T(8,128)(2,1)S(1)} %get-tuple-element.62.refs_3_.refs_2_, ...), custom_call_target="tpu_custom_call" | custom-call | flops 500000000 | tf_op jit(solution)/shard_map/pallas_call | solution.py:210
  28.2 0.0 collective-permute-done.16.refs_0_
  28.2 0.1 collective-permute-start.17
  28.3 1.2 %collective-permute-done.15.refs_1_ = f32[8,512]{1,0:T(8,128)S(1)} collective-permute-done((f32[8,512]{1,0:T(8,128)S(1)}, f32[8,512]{1,0:T(8,128)S(1)}, u32[]{:S(2)}, u32[]{:S(2)}) %collective-permute-start.15) | collective-permute-done | bytes 16416 | tf_op jit(solution)/shard_map/ppermute | solution.py:32
  29.5 0.2 collective-permute-done.17.refs_7_
  29.6 0.1 shard_map.164
  29.7 0.5 %shard_map.165.refs_4_.refs_0_ = f32[8,512]{1,0:T(8,128)S(1)} custom-call(f32[8,512]{1,0:T(8,128)S(1)} %shard_map.161.refs_8_.refs_0_, bf16[256,512]{1,0:T(8,128)(2,1)S(1)} %get-tuple-element.72.refs_1_, bf16[256,512]{1,0:T(8,128)(2,1)S(1)} %get-tuple-element.73.refs_2_), custom_call_target="tpu_custom_call" | custom-call | flops 500000000 | tf_op jit(solution)/shard_map/pallas_call | solution.py:210
  30.2 2.7 %collective-permute-start.18 = (f32[8,512]{1,0:T(8,128)S(1)}, f32[8,512]{1,0:T(8,128)S(1)}, u32[]{:S(2)}, u32[]{:S(2)}) collective-permute-start(f32[8,512]{1,0:T(8,128)S(1)} %shard_map.165.refs_4_.refs_0_), channel_id=1, source_target_pairs={{0,16},{1,17},{2,18},{3,19},{4,20},{5,21},{6,22},{7,23},{8,24},{9,... | collective-permute-start | bytes 49160 | tf_op jit(solution)/shard_map/ppermute | solution.py:32
  32.9 1.5 %shard_map.167 = (f32[8,512]{1,0:T(8,128)}, bf16[256,512]{1,0:T(8,128)(2,1)S(1)}, bf16[256,512]{1,0:T(8,128)(2,1)S(1)}) custom-call(f32[8,512]{1,0:T(8,128)S(1)} %get-tuple-element.52.refs_0_, f32[1,1,4,128,512]{4,3,2,1,0:T(8,128)S(1)} %copy-done.1, f32[1,1,4,128,128]{4,3,2,1,0:T(8,128)S(1)} %copy-done.2, f32[1,1,3,128,128]{4,3,2,1,0:T(8,128)S(1)} %copy-done.3, ...), custom_call_target="tpu_custom_call" | custom-call | flops 1000000000 | tf_op jit(solution)/shard_map/pallas_call | solution.py:210
  34.4 0.4 %collective-permute-done.18.refs_1_ = f32[8,512]{1,0:T(8,128)S(1)} collective-permute-done((f32[8,512]{1,0:T(8,128)S(1)}, f32[8,512]{1,0:T(8,128)S(1)}, u32[]{:S(2)}, u32[]{:S(2)}) %collective-permute-start.18) | collective-permute-done | bytes 16416 | tf_op jit(solution)/shard_map/ppermute | solution.py:32
  34.9 1.5 %shard_map.168 = (f32[1,1,8,512]{3,2,1,0:T(8,128)}, f32[1,1,8,96]{3,2,1,0:T(8,128)}) custom-call(f32[8,512]{1,0:T(8,128)S(1)} %shard_map.165.refs_4_.refs_0_, f32[8,512]{1,0:T(8,128)S(1)} %collective-permute-done.18.refs_1_, f32[8,256]{1,0:T(8,128)S(1)} %get-tuple-element.75.refs_2_, bf16[512,256]{1,0:T(8,128)(2,1)S(1)} %get-tuple-element.76.refs_3_, ...), custom_call_target="tpu_custom_call" | custom-call | flops 2000000000 | tf_op jit(solution)/shard_map/pallas_call | solution.py:210
  (17 shorter events, 0.1 us)
Async XLA Ops:
  0.6 6.3 %copy-start.1 = (f32[1,1,4,128,512]{4,3,2,1,0:T(8,128)S(1)}, f32[1,1,4,128,512]{4,3,2,1,0:T(8,128)}, u32[]{:S(2)}) copy-start(f32[1,1,4,128,512]{4,3,2,1,0:T(8,128)} %refs_1_.7) | copy-start | bytes 3145732
  0.6 6.3 %copy-start.3 = (f32[1,1,3,128,128]{4,3,2,1,0:T(8,128)S(1)}, f32[1,1,3,128,128]{4,3,2,1,0:T(8,128)}, u32[]{:S(2)}) copy-start(f32[1,1,3,128,128]{4,3,2,1,0:T(8,128)} %refs_3_.7) | copy-start | bytes 589828
  0.7 6.3 %copy-start.2 = (f32[1,1,4,128,128]{4,3,2,1,0:T(8,128)S(1)}, f32[1,1,4,128,128]{4,3,2,1,0:T(8,128)}, u32[]{:S(2)}) copy-start(f32[1,1,4,128,128]{4,3,2,1,0:T(8,128)} %refs_2_.7) | copy-start | bytes 786436
  0.7 6.3 %copy-start.5 = (f32[1,1,8,96]{3,2,1,0:T(8,128)S(1)}, f32[1,1,8,96]{3,2,1,0:T(8,128)}, u32[]{:S(2)}) copy-start(f32[1,1,8,96]{3,2,1,0:T(8,128)} %refs_3_.4) | copy-start | bytes 9220
  0.7 6.3 %copy-start.4 = (f32[1,1,8,512]{3,2,1,0:T(8,128)S(1)}, f32[1,1,8,512]{3,2,1,0:T(8,128)}, u32[]{:S(2)}) copy-start(f32[1,1,8,512]{3,2,1,0:T(8,128)} %refs_0_.2) | copy-start | bytes 49156
  2.4 4.6 %copy-start.6 = (s32[1,1,4,128]{3,2,1,0:T(4,128)S(1)}, s32[1,1,4,128]{3,2,1,0:T(4,128)}, u32[]{:S(2)}) copy-start(s32[1,1,4,128]{3,2,1,0:T(4,128)} %refs_16_.1) | copy-start | bytes 6148
  2.4 7.2 %collective-permute-start.1 = (f32[152,128]{1,0:T(8,128)}, f32[152,128]{1,0:T(8,128)S(1)}, u32[]{:S(2)}, u32[]{:S(2)}) collective-permute-start(f32[152,128]{1,0:T(8,128)} %get-tuple-element.45), channel_id=1, source_target_pairs={{0,8},{1,9},{2,10},{3,11},{4,12},{5,13},{6,14},{7,15},{8,0},{9,1},... | collective-permute-start | bytes 233480 | tf_op jit(solution)/shard_map/ppermute | solution.py:32
  5.5 3.6 %copy-start = (f32[280,128]{1,0:T(8,128)S(1)}, f32[280,128]{1,0:T(8,128)}, u32[]{:S(2)}) copy-start(f32[280,128]{1,0:T(8,128)} %get-tuple-element.46.refs_0_) | copy-start | bytes 430084
  5.5 5.4 %collective-permute-start.4 = (f32[280,128]{1,0:T(8,128)}, f32[280,128]{1,0:T(8,128)S(1)}, u32[]{:S(2)}, u32[]{:S(2)}) collective-permute-start(f32[280,128]{1,0:T(8,128)} %get-tuple-element.46.refs_0_), channel_id=1, source_target_pairs={{0,1},{1,0},{2,3},{3,2},{4,5},{5,4},{6,7},{7,6},{8,9},{9,8},{10,11... | collective-permute-start | bytes 430088 | tf_op jit(solution)/shard_map/ppermute | solution.py:32
  9.1 1.2 %collective-permute-start = (f32[8,1152]{1,0:T(8,128)S(1)}, f32[8,1152]{1,0:T(8,128)S(1)}, u32[]{:S(2)}, u32[]{:S(2)}) collective-permute-start(f32[8,1152]{1,0:T(8,128)S(1)} %get-tuple-element.44.refs_0_), channel_id=1, source_target_pairs={{0,4},{1,5},{2,6},{3,7},{4,0},{5,1},{6,2},{7,3},{8,12},{9,13},{10,... | collective-permute-start | bytes 110600 | tf_op jit(solution)/shard_map/ppermute | solution.py:32
  9.1 4.2 %collective-permute-start.3 = (f32[280,128]{1,0:T(8,128)S(1)}, f32[280,128]{1,0:T(8,128)S(1)}, u32[]{:S(2)}, u32[]{:S(2)}) collective-permute-start(f32[280,128]{1,0:T(8,128)S(1)} %copy-done), channel_id=1, source_target_pairs={{0,4},{1,5},{2,6},{3,7},{4,0},{5,1},{6,2},{7,3},{8,12},{9,13},{10,... | collective-permute-start | bytes 430088 | tf_op jit(solution)/shard_map/ppermute | solution.py:32
  10.9 4.0 %collective-permute-start.5 = (f32[280,128]{1,0:T(8,128)S(1)}, f32[280,128]{1,0:T(8,128)S(1)}, u32[]{:S(2)}, u32[]{:S(2)}) collective-permute-start(f32[280,128]{1,0:T(8,128)S(1)} %shard_map.144.refs_2_.refs_4_.refs_1_), channel_id=1, source_target_pairs={{0,4},{1,5},{2,6},{3,7},{4,0},{5,1},{6,2},{7,3},{8,12},{9,13},{10,... | collective-permute-start | bytes 430088 | tf_op jit(solution)/shard_map/ppermute | solution.py:32
  11.0 4.1 %collective-permute-start.2 = (f32[8,1152]{1,0:T(8,128)S(1)}, f32[8,1152]{1,0:T(8,128)S(1)}, u32[]{:S(2)}, u32[]{:S(2)}) collective-permute-start(f32[8,1152]{1,0:T(8,128)S(1)} %shard_map.143.refs_1_.refs_0_.refs_2_), channel_id=1, source_target_pairs={{0,1},{1,0},{2,3},{3,2},{4,5},{5,4},{6,7},{7,6},{8,9},{9,8},{10,11... | collective-permute-start | bytes 110600 | tf_op jit(solution)/shard_map/ppermute | solution.py:32
  12.6 7.0 %collective-permute-start.7 = (f32[152,128]{1,0:T(8,128)S(1)}, f32[152,128]{1,0:T(8,128)S(1)}, u32[]{:S(2)}, u32[]{:S(2)}) collective-permute-start(f32[152,128]{1,0:T(8,128)S(1)} %shard_map.142.refs_2_.refs_0_), channel_id=1, source_target_pairs={{0,4},{1,5},{2,6},{3,7},{4,0},{5,1},{6,2},{7,3},{8,12},{9,13},{10,... | collective-permute-start | bytes 233480 | tf_op jit(solution)/shard_map/ppermute | solution.py:32
  12.7 4.6 %collective-permute-start.8 = (f32[152,128]{1,0:T(8,128)S(1)}, f32[152,128]{1,0:T(8,128)S(1)}, u32[]{:S(2)}, u32[]{:S(2)}) collective-permute-start(f32[152,128]{1,0:T(8,128)S(1)} %shard_map.147), channel_id=1, source_target_pairs={{0,1},{1,0},{2,3},{3,2},{4,5},{5,4},{6,7},{7,6},{8,9},{9,8},{10,11... | collective-permute-start | bytes 233480 | tf_op jit(solution)/shard_map/ppermute | solution.py:32
  13.3 5.7 %collective-permute-start.11 = (f32[240,128]{1,0:T(8,128)S(1)}, f32[240,128]{1,0:T(8,128)S(1)}, u32[]{:S(2)}, u32[]{:S(2)}) collective-permute-start(f32[240,128]{1,0:T(8,128)S(1)} %shard_map.153), channel_id=1, source_target_pairs={{0,2},{1,3},{2,0},{3,1},{4,6},{5,7},{6,4},{7,5},{8,10},{9,11},{10,... | collective-permute-start | bytes 368648 | tf_op jit(solution)/shard_map/ppermute | solution.py:32
  15.4 4.4 %collective-permute-start.6 = (f32[8,1024]{1,0:T(8,128)S(1)}, f32[8,1024]{1,0:T(8,128)S(1)}, u32[]{:S(2)}, u32[]{:S(2)}) collective-permute-start(f32[8,1024]{1,0:T(8,128)S(1)} %get-tuple-element.51.refs_4_.refs_0_.refs_2_), channel_id=1, source_target_pairs={{0,8},{1,9},{2,10},{3,11},{4,12},{5,13},{6,14},{7,15},{8,0},{9,1},... | collective-permute-start | bytes 98312 | tf_op jit(solution)/shard_map/ppermute | solution.py:32
  17.4 2.2 %collective-permute-start.9 = (f32[152,128]{1,0:T(8,128)S(1)}, f32[152,128]{1,0:T(8,128)S(1)}, u32[]{:S(2)}, u32[]{:S(2)}) collective-permute-start(f32[152,128]{1,0:T(8,128)S(1)} %shard_map.149.refs_6_.refs_1_), channel_id=1, source_target_pairs={{0,4},{1,5},{2,6},{3,7},{4,0},{5,1},{6,2},{7,3},{8,12},{9,13},{10,... | collective-permute-start | bytes 233480 | tf_op jit(solution)/shard_map/ppermute | solution.py:32
  17.4 4.3 %collective-permute-start.13 = (f32[112,128]{1,0:T(8,128)S(1)}, f32[112,128]{1,0:T(8,128)S(1)}, u32[]{:S(2)}, u32[]{:S(2)}) collective-permute-start(f32[112,128]{1,0:T(8,128)S(1)} %shard_map.156), channel_id=1, source_target_pairs={{0,2},{1,3},{2,0},{3,1},{4,6},{5,7},{6,4},{7,5},{8,10},{9,11},{10,... | collective-permute-start | bytes 172040 | tf_op jit(solution)/shard_map/ppermute | solution.py:32
  19.0 4.3 %collective-permute-start.12 = (f32[240,128]{1,0:T(8,128)S(1)}, f32[240,128]{1,0:T(8,128)S(1)}, u32[]{:S(2)}, u32[]{:S(2)}) collective-permute-start(f32[240,128]{1,0:T(8,128)S(1)} %shard_map.154.refs_8_.refs_2_.refs_4_), channel_id=1, source_target_pairs={{0,4},{1,5},{2,6},{3,7},{4,0},{5,1},{6,2},{7,3},{8,12},{9,13},{10,... | collective-permute-start | bytes 368648 | tf_op jit(solution)/shard_map/ppermute | solution.py:32
  20.3 4.0 %collective-permute-start.10 = (f32[8,768]{1,0:T(8,128)S(1)}, f32[8,768]{1,0:T(8,128)S(1)}, u32[]{:S(2)}, u32[]{:S(2)}) collective-permute-start(f32[8,768]{1,0:T(8,128)S(1)} %get-tuple-element.60.refs_10_.refs_1_.refs_2_.refs_0_.refs_3_), channel_id=1, source_target_pairs={{0,2},{1,3},{2,0},{3,1},{4,6},{5,7},{6,4},{7,5},{8,10},{9,11},{10,... | collective-permute-start | bytes 73736 | tf_op jit(solution)/shard_map/ppermute | solution.py:32
  21.8 2.2 %collective-permute-start.14 = (f32[112,128]{1,0:T(8,128)S(1)}, f32[112,128]{1,0:T(8,128)S(1)}, u32[]{:S(2)}, u32[]{:S(2)}) collective-permute-start(f32[112,128]{1,0:T(8,128)S(1)} %shard_map.157.refs_0_), channel_id=1, source_target_pairs={{0,4},{1,5},{2,6},{3,7},{4,0},{5,1},{6,2},{7,3},{8,12},{9,13},{10,... | collective-permute-start | bytes 172040 | tf_op jit(solution)/shard_map/ppermute | solution.py:32
  22.1 6.0 %collective-permute-start.16 = (f32[256,128]{1,0:T(8,128)S(1)}, f32[256,128]{1,0:T(8,128)S(1)}, u32[]{:S(2)}, u32[]{:S(2)}) collective-permute-start(f32[256,128]{1,0:T(8,128)S(1)} %shard_map.162), channel_id=1, source_target_pairs={{0,8},{1,9},{2,10},{3,11},{4,12},{5,13},{6,14},{7,15},{8,0},{9,1},... | collective-permute-start | bytes 393224 | tf_op jit(solution)/shard_map/ppermute | solution.py:32
  24.7 4.7 %collective-permute-start.15 = (f32[8,512]{1,0:T(8,128)S(1)}, f32[8,512]{1,0:T(8,128)S(1)}, u32[]{:S(2)}, u32[]{:S(2)}) collective-permute-start(f32[8,512]{1,0:T(8,128)S(1)} %get-tuple-element.71.refs_0_.refs_1_), channel_id=1, source_target_pairs={{0,16},{1,17},{2,18},{3,19},{4,20},{5,21},{6,22},{7,23},{8,24},{9,... | collective-permute-start | bytes 49160 | tf_op jit(solution)/shard_map/ppermute | solution.py:32
  28.2 1.4 %collective-permute-start.17 = (f32[256,128]{1,0:T(8,128)S(1)}, f32[256,128]{1,0:T(8,128)S(1)}, u32[]{:S(2)}, u32[]{:S(2)}) collective-permute-start(f32[256,128]{1,0:T(8,128)S(1)} %shard_map.163.refs_6_), channel_id=1, source_target_pairs={{0,4},{1,5},{2,6},{3,7},{4,0},{5,1},{6,2},{7,3},{8,12},{9,13},{10,... | collective-permute-start | bytes 393224 | tf_op jit(solution)/shard_map/ppermute | solution.py:32
  30.2 4.7 %collective-permute-start.18 = (f32[8,512]{1,0:T(8,128)S(1)}, f32[8,512]{1,0:T(8,128)S(1)}, u32[]{:S(2)}, u32[]{:S(2)}) collective-permute-start(f32[8,512]{1,0:T(8,128)S(1)} %shard_map.165.refs_4_.refs_0_), channel_id=1, source_target_pairs={{0,16},{1,17},{2,18},{3,19},{4,20},{5,21},{6,22},{7,23},{8,24},{9,... | collective-permute-start | bytes 49160 | tf_op jit(solution)/shard_map/ppermute | solution.py:32

commit v4 on v3

--- a/solution.py
+++ b/solution.py
@@ -11,7 +11,6 @@
 LANES = 128
 GATHER_BYTES = 8 * 2**20
 VMEM_BYTES = 24 * 2**20
-WHOLE_VMEM_BYTES = 60 * 2**20
 FLOPS_A_MICROSECOND = 1_000_000_000
 ARRIVE_US = 0.1
 SOLVE_US = 2.0
@@ -202,7 +201,11 @@
 
 
 def vmem_call(body, outs, *operands, microseconds, after=(), space=pltpu.VMEM, scratch=(), limit=VMEM_BYTES):
-    out_shape = [jax.ShapeDtypeStruct(shape, dtype) for shape, dtype in outs]
+    if space is pltpu.HBM:
+        out_shape = [pltpu.VMEM(shape, dtype) for shape, dtype in outs]
+        operands = [pltpu.with_memory_space_constraint(operand, pltpu.HBM) for operand in operands]
+    else:
+        out_shape = [jax.ShapeDtypeStruct(shape, dtype) for shape, dtype in outs]
 
     def kernel(*refs):
         body(*refs[: len(operands)], *refs[len(operands) + len(after) :])
@@ -291,9 +294,11 @@
         forward[:, counter * block : (counter + 1) * block] = earlier
     whole = forward[...]
     own = times(sep_rhs[0, 0], [one_hot(own_targets(sizes, owned, taken), sum(sizes))], True)
+    terms = times(whole, halves(coupling[0, 0].reshape(-1, whole.shape[1])), True)
+    width = coupling.shape[3]
     at = 0
     for section in range(4):
-        term = times(whole, halves(coupling[0, 0, section]), True)
+        term = terms[:, section * width : (section + 1) * width]
         spread = times(term, [one_hot(places[0, 0, section : section + 1, :], sizes[section])], True)
         sums[:, at : at + sizes[section]] = own[:, at : at + sizes[section]] - spread
         at += sizes[section]
@@ -388,22 +393,29 @@
         d_high[:, columns], d_low[:, columns] = halves(later[rhs_count:])
 
 
+def pick_body(sizes, owned, taken, places, picks, owns):
+    at = 0
+    for section in range(4):
+        picks[at : at + sizes[section], :] = one_hot(places[0, 0, section : section + 1, :], sizes[section])
+        at += sizes[section]
+    owns[...] = one_hot(own_targets(sizes, owned, taken), at)
+
+
 def backward_body(
-    sizes, owned, taken, mine, theirs, u1, n1h, n1l, u2, n2h, n2l, u3, n3h, n3l,
-    base, d1h, d1l, d2h, d2l, places, leaf, sep,
+    sizes, mine, theirs, u1, n1h, n1l, u2, n2h, n2l, u3, n3h, n3l, base, d1h, d1l, d2h, d2l, picks, owns, leaf, sep
 ):
     solved = [mine[...] + theirs[...]]
     for known, n_high, n_low in ((u1, n1h, n1l), (u2, n2h, n2l), (u3, n3h, n3l)):
         solved.append(known[...] - times(solved[-1], [n_high[...], n_low[...]], False))
-    picked = [
-        times(solved[section], [one_hot(places[0, 0, section : section + 1, :], sizes[section])], False)
-        for section in range(4)
-    ]
+    picked = []
+    at = 0
+    for section in range(4):
+        picked.append(times(solved[section], [picks[at : at + sizes[section], :]], False))
+        at += sizes[section]
     first = times(jnp.concatenate(picked[:2], axis=1), [d1h[...], d1l[...]], False)
     second = times(jnp.concatenate(picked[2:], axis=1), [d2h[...], d2l[...]], False)
     leaf[0, 0] = base[...] - first - second
-    everything = jnp.concatenate(solved, axis=1)
-    sep[0, 0] = times(everything, [one_hot(own_targets(sizes, owned, taken), sum(sizes))], False)
+    sep[0, 0] = times(jnp.concatenate(solved, axis=1), [owns[...]], False)
 
 
 def gathered(
@@ -439,7 +451,7 @@
         functools.partial(pack_body, starts, part),
         [((height, LANES), jnp.float32), ((part[1] - part[0], LANES), jnp.float32)],
         factor_one, factor_two, factor_three, factor_four, link_two, link_three, link_four, interface,
-        microseconds=1.0, space=pltpu.HBM, limit=WHOLE_VMEM_BYTES,
+        microseconds=1.0, space=pltpu.HBM,
         scratch=[pltpu.VMEM(factor.shape, jnp.float32) for factor in factors[:3]]
         + [pltpu.VMEM(interface.shape[2:], jnp.int32), pltpu.SemaphoreType.DMA((8,))],
     )
@@ -505,12 +517,15 @@
             [((rhs_count, sums.shape[1] - size), jnp.float32), ((rhs_count, size), jnp.float32)],
             sums, theirs, *flat, microseconds=ELIM_US, after=after,
         )
-        folded = vmem_call(
-            functools.partial(fold_body, len(tables)),
+        return sums, (found, *flat)
+
+    def fold(section, pieces, after):
+        size, above = sizes[section], sizes[section - 1]
+        return vmem_call(
+            functools.partial(fold_body, (len(pieces) - 1) // 4),
             [((rhs_count, size), jnp.float32)] + [((above, size), jnp.bfloat16)] * 2,
-            found, *flat, microseconds=FOLD_US,
+            *pieces, microseconds=FOLD_US, after=after,
         )
-        return sums, folded
 
     def solve(sections, after):
         return vmem_call(
@@ -542,39 +557,49 @@
     following, near_at = message(choose([both[0], by_inner], (0, 1)), (sums,))
     near = from_partner(following, axes, second)
     table = level(3, both)
-    sums, folded_four = eliminate(3, sums, theirs, [table], ())
+    sums, four_level = eliminate(3, sums, theirs, [table], ())
 
     theirs = from_partner(sums, axes, third)
     solved_first = solve((0, 1), (sums,))
     by_two = arrive(two, two_at, (solved_first[0],), X2_US)
-    by_near = arrive(near, near_at, (solved_first[0],), NEAR_US)
     following, last_at = message(choose([by_third, by_two], (1,)), (sums,), Y2_US)
+    by_near = arrive(near, near_at, (following,), NEAR_US)
     last = from_partner(following, axes, second)
     table = level(2, both)
-    sums, folded_three = eliminate(2, sums, theirs, [table], (folded_four[0],))
+    sums, three_level = eliminate(2, sums, theirs, [table], ())
 
     theirs = from_partner(sums, axes, second)
     following, top_at = message(choose([both[0], by_inner, by_near], (0,)), (sums,), F1_US)
     from_third = from_partner(following, axes, third)
     early = len(both)
-    arrive(last, last_at, (sums,), LAST_US)
-    tables = [level(1, both[:early], (sums,)), level(1, both[early:], (sums,))]
-    sums, folded_two = eliminate(1, sums, theirs, tables, (folded_three[0],))
+    table = level(1, both[:early], (sums,))
+    arrive(last, last_at, (table[0],), LAST_US)
+    folded_three = fold(2, three_level, (sums,))
+    folded_four = fold(3, four_level, (sums,))
+    late = (folded_three[0], folded_four[0])
+    sums, two_level = eliminate(1, sums, theirs, [table, level(1, both[early:])], late)
 
     theirs = from_partner(sums, axes, first)
+    folded_two = fold(1, two_level, (sums,))
     arrive(from_third, top_at, (sums,), F1C_US)
     (sums,) = vmem_call(
-        add_body, [((rhs_count, sizes[0]), jnp.float32)], sums, theirs, microseconds=SUM_US
+        add_body, [((rhs_count, sizes[0]), jnp.float32)], sums, theirs, microseconds=SUM_US,
+        after=(folded_two[0],),
     )
     (partial,) = vmem_call(
         top_body, [((rhs_count, sizes[0]), jnp.float32)], sums, *level(0, both, (sums,)), microseconds=0.5
     )
     theirs = from_partner(partial, axes, first)
     solved_second = solve((2, 3), (partial,))
+    picks = vmem_call(
+        functools.partial(pick_body, sizes, owned, taken),
+        [((total, interface.shape[3]), jnp.bfloat16), ((total, sum(owned)), jnp.bfloat16)],
+        interface, microseconds=0.3, after=(partial,),
+    )
     leaf, sep = vmem_call(
-        functools.partial(backward_body, sizes, owned, taken),
+        functools.partial(backward_body, sizes),
         [(rhs_leaf.shape, jnp.float32), (sep_rhs.shape, jnp.float32)],
-        partial, theirs, *folded_two, *folded_three, *folded_four, *solved_first, *solved_second[1:], interface,
+        partial, theirs, *folded_two, *folded_three, *folded_four, *solved_first, *solved_second[1:], *picks,
         microseconds=2.0,
     )
     return (leaf, sep)

time: 36.6 us -> 35.8 us (0.978)
  Pallas kernels: 12.4 us -> 11.2 us
    pallas_call x29 -> x30, Pallas kernels: 12.4 us -> 11.2 us  [vmem_call(): pl.pallas_call(kernel, out_shape=out_shape, in_specs=[pl.BlockSpec(memory...]
  transfers between devices with their start and end apart: 19 -> 19, of which waited for: 7 -> 7; matrix products, arithmetic and copies ran while one was open for 0% -> 0% of each run, Pallas kernels for 24% -> 23%
where the time goes in v4:
time: 35.8 us; the launch traced here: 35.5 us
  starting transfers between devices  19.2 us (54%)
  Pallas kernels  11.2 us (31%)
  waiting for transfers between devices  4.15 us (12%)
  between operations  0.92 us (3%)
    ppermute x19, starting transfers between devices, from_partner(): lax.ppermute(value, axis, [(i, i ^ 1 << distance) for i in range(lax.axis...  19.2 us
    pallas_call x30, Pallas kernels, vmem_call(): pl.pallas_call(kernel, out_shape=out_shape, in_specs=[pl.BlockSpec(memory...  11.2 us
    ppermute x19, waiting for transfers between devices, from_partner(): lax.ppermute(value, axis, [(i, i ^ 1 << distance) for i in range(lax.axis...  4.15 us
  transfers between devices with their start and end apart: 19, of which 7 were waited for; matrix products, arithmetic and copies ran while one was open for 0% of the time, Pallas kernels for 23%

profile of v4, /device:TPU:0, one launch (start us, length us, event | category | flops | bytes accessed | tf_op | source)
XLA Modules:
  0.0 35.5 jit_solution(17526481200561349208)
XLA Ops:
  0.6 0.0 copy-start.3
  0.6 0.0 copy-start.1
  0.7 0.0 copy-start.2
  0.7 0.0 copy-start.4
  0.7 0.0 copy-start
  0.7 1.0 %shard_map.141 = (f32[280,128]{1,0:T(8,128)S(1)}, f32[152,128]{1,0:T(8,128)S(1)}) custom-call(f32[1,1,16,512]{3,2,1,0:T(8,128)} %refs_0_.4, f32[1,1,16,256]{3,2,1,0:T(8,128)} %refs_1_.5, f32[1,1,32,256]{3,2,1,0:T(8,128)} %refs_2_.5, f32[1,1,32,128]{3,2,1,0:T(8,128)} %refs_3_.5, f32[1,1,16,128]{3,2,1,0:T(8,128)} %refs_4_.3, f32[1,1,32,128]{3,2,1,0:T(8,128)} %refs_5_.3, ...), custom_call_target="tpu_custom_call" | custom-call | flops 1000000000 | tf_op jit(solution)/shard_map/pallas_call | solution.py:213
  1.7 0.0 copy-start.5
  1.7 3.1 %collective-permute-start.1 = (f32[152,128]{1,0:T(8,128)S(1)}, f32[152,128]{1,0:T(8,128)S(1)}, u32[]{:S(2)}, u32[]{:S(2)}) collective-permute-start(f32[152,128]{1,0:T(8,128)S(1)} %get-tuple-element.47), channel_id=1, source_target_pairs={{0,8},{1,9},{2,10},{3,11},{4,12},{5,13},{6,14},{7,15},{8,0},{9,1},... | collective-permute-start | bytes 233480 | tf_op jit(solution)/shard_map/ppermute | solution.py:31
  4.8 1.5 %collective-permute-start.4 = (f32[280,128]{1,0:T(8,128)S(1)}, f32[280,128]{1,0:T(8,128)S(1)}, u32[]{:S(2)}, u32[]{:S(2)}) collective-permute-start(f32[280,128]{1,0:T(8,128)S(1)} %get-tuple-element.48.refs_0_), channel_id=1, source_target_pairs={{0,1},{1,0},{2,3},{3,2},{4,5},{5,4},{6,7},{7,6},{8,9},{9,8},{10,11... | collective-permute-start | bytes 430088 | tf_op jit(solution)/shard_map/ppermute | solution.py:31
  6.3 0.0 copy-done.3
  6.3 0.0 copy-done.2
  6.3 1.5 %shard_map.140 = (f32[8,512]{1,0:T(8,128)S(1)}, f32[8,1152]{1,0:T(8,128)S(1)}) custom-call(f32[1,1,8,512]{3,2,1,0:T(8,128)S(1)} %copy-done.3, f32[1,1,4,128,128]{4,3,2,1,0:T(8,128)S(1)} %copy-done.1, f32[1,1,3,128,128]{4,3,2,1,0:T(8,128)S(1)} %copy-done.2, f32[1,1,8,96]{3,2,1,0:T(8,128)S(1)} %copy-done.4, s32[1,1,4,128]{3,2,1,0:T(4,128)S(1)} %copy-done.5, ...), custom_call_target="tpu_custom_call" | custom-call | flops 2000000000 | tf_op jit(solution)/shard_map/pallas_call | solution.py:213
  7.8 0.1 collective-permute-start
  7.8 0.5 %collective-permute-start.3 = (f32[280,128]{1,0:T(8,128)S(1)}, f32[280,128]{1,0:T(8,128)S(1)}, u32[]{:S(2)}, u32[]{:S(2)}) collective-permute-start(f32[280,128]{1,0:T(8,128)S(1)} %get-tuple-element.48.refs_0_), channel_id=1, source_target_pairs={{0,4},{1,5},{2,6},{3,7},{4,0},{5,1},{6,2},{7,3},{8,12},{9,13},{10,... | collective-permute-start | bytes 430088 | tf_op jit(solution)/shard_map/ppermute | solution.py:31
  8.3 0.0 collective-permute-done.1.refs_0_
  8.4 0.7 %collective-permute-done.refs_1_ = f32[8,1152]{1,0:T(8,128)S(1)} collective-permute-done((f32[8,1152]{1,0:T(8,128)S(1)}, f32[8,1152]{1,0:T(8,128)S(1)}, u32[]{:S(2)}, u32[]{:S(2)}) %collective-permute-start) | collective-permute-done | bytes 36896 | tf_op jit(solution)/shard_map/ppermute | solution.py:31
  9.1 1.0 %collective-permute-done.4.refs_0_ = f32[280,128]{1,0:T(8,128)S(1)} collective-permute-done((f32[280,128]{1,0:T(8,128)S(1)}, f32[280,128]{1,0:T(8,128)S(1)}, u32[]{:S(2)}, u32[]{:S(2)}) %collective-permute-start.4) | collective-permute-done | bytes 143392 | tf_op jit(solution)/shard_map/ppermute | solution.py:31
  10.0 0.1 collective-permute-start.5
  10.1 1.6 %collective-permute-start.2 = (f32[8,1152]{1,0:T(8,128)S(1)}, f32[8,1152]{1,0:T(8,128)S(1)}, u32[]{:S(2)}, u32[]{:S(2)}) collective-permute-start(f32[8,1152]{1,0:T(8,128)S(1)} %shard_map.143.refs_1_.refs_0_.refs_2_), channel_id=1, source_target_pairs={{0,1},{1,0},{2,3},{3,2},{4,5},{5,4},{6,7},{7,6},{8,9},{9,8},{10,11... | collective-permute-start | bytes 110600 | tf_op jit(solution)/shard_map/ppermute | solution.py:31
  11.7 0.2 collective-permute-start.7
  11.8 0.5 %collective-permute-start.8 = (f32[152,128]{1,0:T(8,128)S(1)}, f32[152,128]{1,0:T(8,128)S(1)}, u32[]{:S(2)}, u32[]{:S(2)}) collective-permute-start(f32[152,128]{1,0:T(8,128)S(1)} %shard_map.147), channel_id=1, source_target_pairs={{0,1},{1,0},{2,3},{3,2},{4,5},{5,4},{6,7},{7,6},{8,9},{9,8},{10,11... | collective-permute-start | bytes 233480 | tf_op jit(solution)/shard_map/ppermute | solution.py:31
  12.4 0.0 collective-permute-done.3.refs_1_
  12.4 1.6 %collective-permute-start.11 = (f32[240,128]{1,0:T(8,128)S(1)}, f32[240,128]{1,0:T(8,128)S(1)}, u32[]{:S(2)}, u32[]{:S(2)}) collective-permute-start(f32[240,128]{1,0:T(8,128)S(1)} %shard_map.152), channel_id=1, source_target_pairs={{0,2},{1,3},{2,0},{3,1},{4,6},{5,7},{6,4},{7,5},{8,10},{9,11},{10,... | collective-permute-start | bytes 368648 | tf_op jit(solution)/shard_map/ppermute | solution.py:31
  14.0 0.0 collective-permute-done.5.refs_3_.refs_5_
  14.0 0.2 shard_map.145
  14.2 0.0 collective-permute-done.2.refs_1_
  14.2 0.3 shard_map.146
  14.6 0.5 %collective-permute-start.6 = (f32[8,1024]{1,0:T(8,128)S(1)}, f32[8,1024]{1,0:T(8,128)S(1)}, u32[]{:S(2)}, u32[]{:S(2)}) collective-permute-start(f32[8,1024]{1,0:T(8,128)S(1)} %get-tuple-element.53.refs_4_.refs_0_.refs_2_), channel_id=1, source_target_pairs={{0,8},{1,9},{2,10},{3,11},{4,12},{5,13},{6,14},{7,15},{8,0},{9,1},... | collective-permute-start | bytes 98312 | tf_op jit(solution)/shard_map/ppermute | solution.py:31
  15.0 1.0 %shard_map.148 = (f32[8,512]{1,0:T(8,128)S(1)}, bf16[256,512]{1,0:T(8,128)(2,1)S(1)}, bf16[256,512]{1,0:T(8,128)(2,1)S(1)}) custom-call(f32[8,512]{1,0:T(8,128)S(1)} %get-tuple-element.54.refs_0_, f32[1,1,4,128,512]{4,3,2,1,0:T(8,128)S(1)} %copy-done, f32[1,1,4,128,128]{4,3,2,1,0:T(8,128)S(1)} %copy-done.1, f32[1,1,3,128,128]{4,3,2,1,0:T(8,128)S(1)} %copy-done.2, ...), custom_call_target="tpu_custom_call" | custom-call | flops 1000000000 | tf_op jit(solution)/shard_map/pallas_call | solution.py:213
  16.0 0.4 %collective-permute-done.8.refs_0_ = f32[152,128]{1,0:T(8,128)S(1)} collective-permute-done((f32[152,128]{1,0:T(8,128)S(1)}, f32[152,128]{1,0:T(8,128)S(1)}, u32[]{:S(2)}, u32[]{:S(2)}) %collective-permute-start.8) | collective-permute-done | bytes 77856 | tf_op jit(solution)/shard_map/ppermute | solution.py:31
  16.5 0.0 collective-permute-start.9
  16.5 1.6 %collective-permute-start.13 = (f32[112,128]{1,0:T(8,128)S(1)}, f32[112,128]{1,0:T(8,128)S(1)}, u32[]{:S(2)}, u32[]{:S(2)}) collective-permute-start(f32[112,128]{1,0:T(8,128)S(1)} %shard_map.153.refs_1_), channel_id=1, source_target_pairs={{0,2},{1,3},{2,0},{3,1},{4,6},{5,7},{6,4},{7,5},{8,10},{9,11},{10,... | collective-permute-start | bytes 172040 | tf_op jit(solution)/shard_map/ppermute | solution.py:31
  18.1 0.0 collective-permute-done.11.refs_0_
  18.1 0.2 collective-permute-start.12
  18.3 0.0 collective-permute-done.7.refs_3_
  18.3 0.0 collective-permute-done.9.refs_7_
  18.3 0.3 shard_map.150
  18.6 0.0 collective-permute-done.6.refs_1_
  18.6 0.4 %shard_map.151 = (f32[8,768]{1,0:T(8,128)S(1)}, f32[8,256]{1,0:T(8,128)S(1)}) custom-call(f32[8,1024]{1,0:T(8,128)S(1)} %get-tuple-element.53.refs_4_.refs_0_.refs_2_, f32[8,1024]{1,0:T(8,128)S(1)} %collective-permute-done.6.refs_1_, bf16[256,256]{1,0:T(8,128)(2,1)S(1)} %get-tuple-element.56.refs_2_.refs_1_, ...), custom_call_target="tpu_custom_call" | custom-call | flops 5000000000 | tf_op jit(solution)/shard_map/pallas_call | solution.py:213
  19.0 1.3 %collective-permute-start.10 = (f32[8,768]{1,0:T(8,128)S(1)}, f32[8,768]{1,0:T(8,128)S(1)}, u32[]{:S(2)}, u32[]{:S(2)}) collective-permute-start(f32[8,768]{1,0:T(8,128)S(1)} %get-tuple-element.60.refs_10_.refs_5_.refs_0_.refs_3_), channel_id=1, source_target_pairs={{0,2},{1,3},{2,0},{3,1},{4,6},{5,7},{6,4},{7,5},{8,10},{9,11},{10,... | collective-permute-start | bytes 73736 | tf_op jit(solution)/shard_map/ppermute | solution.py:31
  20.3 0.0 collective-permute-done.12.refs_9_.refs_5_
  20.3 0.6 %shard_map.155 = (bf16[192,256]{1,0:T(8,128)(2,1)S(1)}, bf16[192,256]{1,0:T(8,128)(2,1)S(1)}, bf16[192,512]{1,0:T(8,128)(2,1)S(1)}, bf16[192,512]{1,0:T(8,128)(2,1)S(1)}) custom-call(f32[280,128]{1,0:T(8,128)S(1)} %get-tuple-element.48.refs_0_, f32[280,128]{1,0:T(8,128)S(1)} %collective-permute-done.3.refs_1_, f32[152,128]{1,0:T(8,128)S(1)} %shard_map.142.refs_2_.refs_0_, ...), custom_call_target="tpu_custom_call" | custom-call | flops 400000000 | tf_op jit(solution)/shard_map/pallas_call | solution.py:213
  20.9 0.0 collective-permute-done.13.refs_0_
  21.0 0.1 collective-permute-start.14
  21.1 0.4 shard_map.158
  21.4 1.0 %collective-permute-start.16 = (f32[256,128]{1,0:T(8,128)S(1)}, f32[256,128]{1,0:T(8,128)S(1)}, u32[]{:S(2)}, u32[]{:S(2)}) collective-permute-start(f32[256,128]{1,0:T(8,128)S(1)} %shard_map.163), channel_id=1, source_target_pairs={{0,8},{1,9},{2,10},{3,11},{4,12},{5,13},{6,14},{7,15},{8,0},{9,1},... | collective-permute-start | bytes 393224 | tf_op jit(solution)/shard_map/ppermute | solution.py:31
  22.5 0.3 shard_map.159
  22.8 0.0 collective-permute-done.14.refs_1_
  22.8 0.3 shard_map.157
  23.0 0.0 collective-permute-done.10.refs_1_
  23.1 0.4 %shard_map.160 = (f32[8,512]{1,0:T(8,128)S(1)}, f32[8,256]{1,0:T(8,128)S(1)}) custom-call(f32[8,768]{1,0:T(8,128)S(1)} %get-tuple-element.60.refs_10_.refs_5_.refs_0_.refs_3_, f32[8,768]{1,0:T(8,128)S(1)} %collective-permute-done.10.refs_1_, bf16[192,256]{1,0:T(8,128)(2,1)S(1)} %get-tuple-element.61.refs_1_.refs_2_, ...), custom_call_target="tpu_custom_call" | custom-call | flops 5000000000 | tf_op jit(solution)/shard_map/pallas_call | solution.py:213
  23.5 2.7 %collective-permute-start.15 = (f32[8,512]{1,0:T(8,128)S(1)}, f32[8,512]{1,0:T(8,128)S(1)}, u32[]{:S(2)}, u32[]{:S(2)}) collective-permute-start(f32[8,512]{1,0:T(8,128)S(1)} %get-tuple-element.73.refs_9_.refs_0_.refs_1_), channel_id=1, source_target_pairs={{0,16},{1,17},{2,18},{3,19},{4,20},{5,21},{6,22},{7,23},{8,24},{9,... | collective-permute-start | bytes 49160 | tf_op jit(solution)/shard_map/ppermute | solution.py:31
  26.2 0.8 %shard_map.161 = (f32[8,256]{1,0:T(8,128)S(1)}, bf16[512,256]{1,0:T(8,128)(2,1)S(1)}, bf16[512,256]{1,0:T(8,128)(2,1)S(1)}) custom-call(f32[8,256]{1,0:T(8,128)S(1)} %get-tuple-element.74.refs_0_, bf16[192,256]{1,0:T(8,128)(2,1)S(1)} %get-tuple-element.61.refs_1_.refs_2_, bf16[192,256]{1,0:T(8,128)(2,1)S(1)} %get-tuple-element.62.refs_3_.refs_2_, ...), custom_call_target="tpu_custom_call" | custom-call | flops 500000000 | tf_op jit(solution)/shard_map/pallas_call | solution.py:213
  26.9 0.4 %collective-permute-done.16.refs_0_ = f32[256,128]{1,0:T(8,128)S(1)} collective-permute-done((f32[256,128]{1,0:T(8,128)S(1)}, f32[256,128]{1,0:T(8,128)S(1)}, u32[]{:S(2)}, u32[]{:S(2)}) %collective-permute-start.16) | collective-permute-done | bytes 131104 | tf_op jit(solution)/shard_map/ppermute | solution.py:31
  27.4 0.1 collective-permute-start.17
  27.5 0.7 %collective-permute-done.15.refs_1_ = f32[8,512]{1,0:T(8,128)S(1)} collective-permute-done((f32[8,512]{1,0:T(8,128)S(1)}, f32[8,512]{1,0:T(8,128)S(1)}, u32[]{:S(2)}, u32[]{:S(2)}) %collective-permute-start.15) | collective-permute-done | bytes 16416 | tf_op jit(solution)/shard_map/ppermute | solution.py:31
  28.2 0.6 %collective-permute-done.17.refs_7_ = f32[256,128]{1,0:T(8,128)S(1)} collective-permute-done((f32[256,128]{1,0:T(8,128)S(1)}, f32[256,128]{1,0:T(8,128)S(1)}, u32[]{:S(2)}, u32[]{:S(2)}) %collective-permute-start.17) | collective-permute-done | bytes 131104 | tf_op jit(solution)/shard_map/ppermute | solution.py:31
  28.8 0.1 shard_map.165
  28.9 0.5 %shard_map.166.refs_4_.refs_1_.refs_0_ = f32[8,512]{1,0:T(8,128)S(1)} custom-call(f32[8,512]{1,0:T(8,128)S(1)} %shard_map.162.refs_8_.refs_0_, bf16[256,512]{1,0:T(8,128)(2,1)S(1)} %get-tuple-element.76.refs_1_, bf16[256,512]{1,0:T(8,128)(2,1)S(1)} %get-tuple-element.77.refs_2_), custom_call_target="tpu_custom_call" | custom-call | flops 500000000 | tf_op jit(solution)/shard_map/pallas_call | solution.py:213
  29.4 2.8 %collective-permute-start.18 = (f32[8,512]{1,0:T(8,128)S(1)}, f32[8,512]{1,0:T(8,128)S(1)}, u32[]{:S(2)}, u32[]{:S(2)}) collective-permute-start(f32[8,512]{1,0:T(8,128)S(1)} %shard_map.166.refs_4_.refs_1_.refs_0_), channel_id=1, source_target_pairs={{0,16},{1,17},{2,18},{3,19},{4,20},{5,21},{6,22},{7,23},{8,24},{9,... | collective-permute-start | bytes 49160 | tf_op jit(solution)/shard_map/ppermute | solution.py:31
  32.2 1.5 %shard_map.167 = (f32[8,512]{1,0:T(8,128)}, bf16[256,512]{1,0:T(8,128)(2,1)S(1)}, bf16[256,512]{1,0:T(8,128)(2,1)S(1)}) custom-call(f32[8,512]{1,0:T(8,128)S(1)} %get-tuple-element.54.refs_0_, f32[1,1,4,128,512]{4,3,2,1,0:T(8,128)S(1)} %copy-done, f32[1,1,4,128,128]{4,3,2,1,0:T(8,128)S(1)} %copy-done.1, f32[1,1,3,128,128]{4,3,2,1,0:T(8,128)S(1)} %copy-done.2, ...), custom_call_target="tpu_custom_call" | custom-call | flops 1000000000 | tf_op jit(solution)/shard_map/pallas_call | solution.py:213
  33.7 0.1 shard_map.168
  33.8 0.2 collective-permute-done.18.refs_1_
  34.1 1.5 %shard_map.169 = (f32[1,1,8,512]{3,2,1,0:T(8,128)}, f32[1,1,8,96]{3,2,1,0:T(8,128)}) custom-call(f32[8,512]{1,0:T(8,128)S(1)} %shard_map.166.refs_4_.refs_1_.refs_0_, f32[8,512]{1,0:T(8,128)S(1)} %collective-permute-done.18.refs_1_, f32[8,256]{1,0:T(8,128)S(1)} %get-tuple-element.75.refs_2_, bf16[512,256]{1,0:T(8,128)(2,1)S(1)} %get-tuple-element.78.refs_3_, ...), custom_call_target="tpu_custom_call" | custom-call | flops 2000000000 | tf_op jit(solution)/shard_map/pallas_call | solution.py:213
  (16 shorter events, 0.1 us)
Async XLA Ops:
  0.6 5.7 %copy-start.3 = (f32[1,1,8,512]{3,2,1,0:T(8,128)S(1)}, f32[1,1,8,512]{3,2,1,0:T(8,128)}, u32[]{:S(2)}) copy-start(f32[1,1,8,512]{3,2,1,0:T(8,128)} %refs_0_.3) | copy-start | bytes 49156
  0.6 5.7 %copy-start.1 = (f32[1,1,4,128,128]{4,3,2,1,0:T(8,128)S(1)}, f32[1,1,4,128,128]{4,3,2,1,0:T(8,128)}, u32[]{:S(2)}) copy-start(f32[1,1,4,128,128]{4,3,2,1,0:T(8,128)} %refs_2_.7) | copy-start | bytes 786436
  0.7 5.6 %copy-start.2 = (f32[1,1,3,128,128]{4,3,2,1,0:T(8,128)S(1)}, f32[1,1,3,128,128]{4,3,2,1,0:T(8,128)}, u32[]{:S(2)}) copy-start(f32[1,1,3,128,128]{4,3,2,1,0:T(8,128)} %refs_3_.7) | copy-start | bytes 589828
  0.7 5.6 %copy-start.4 = (f32[1,1,8,96]{3,2,1,0:T(8,128)S(1)}, f32[1,1,8,96]{3,2,1,0:T(8,128)}, u32[]{:S(2)}) copy-start(f32[1,1,8,96]{3,2,1,0:T(8,128)} %refs_3_.4) | copy-start | bytes 9220
  0.7 5.6 %copy-start = (f32[1,1,4,128,512]{4,3,2,1,0:T(8,128)S(1)}, f32[1,1,4,128,512]{4,3,2,1,0:T(8,128)}, u32[]{:S(2)}) copy-start(f32[1,1,4,128,512]{4,3,2,1,0:T(8,128)} %refs_1_.7) | copy-start | bytes 3145732
  1.7 4.6 %copy-start.5 = (s32[1,1,4,128]{3,2,1,0:T(4,128)S(1)}, s32[1,1,4,128]{3,2,1,0:T(4,128)}, u32[]{:S(2)}) copy-start(s32[1,1,4,128]{3,2,1,0:T(4,128)} %refs_0_.5) | copy-start | bytes 6148
  1.7 6.6 %collective-permute-start.1 = (f32[152,128]{1,0:T(8,128)S(1)}, f32[152,128]{1,0:T(8,128)S(1)}, u32[]{:S(2)}, u32[]{:S(2)}) collective-permute-start(f32[152,128]{1,0:T(8,128)S(1)} %get-tuple-element.47), channel_id=1, source_target_pairs={{0,8},{1,9},{2,10},{3,11},{4,12},{5,13},{6,14},{7,15},{8,0},{9,1},... | collective-permute-start | bytes 233480 | tf_op jit(solution)/shard_map/ppermute | solution.py:31
  4.8 5.2 %collective-permute-start.4 = (f32[280,128]{1,0:T(8,128)S(1)}, f32[280,128]{1,0:T(8,128)S(1)}, u32[]{:S(2)}, u32[]{:S(2)}) collective-permute-start(f32[280,128]{1,0:T(8,128)S(1)} %get-tuple-element.48.refs_0_), channel_id=1, source_target_pairs={{0,1},{1,0},{2,3},{3,2},{4,5},{5,4},{6,7},{7,6},{8,9},{9,8},{10,11... | collective-permute-start | bytes 430088 | tf_op jit(solution)/shard_map/ppermute | solution.py:31
  7.8 1.3 %collective-permute-start = (f32[8,1152]{1,0:T(8,128)S(1)}, f32[8,1152]{1,0:T(8,128)S(1)}, u32[]{:S(2)}, u32[]{:S(2)}) collective-permute-start(f32[8,1152]{1,0:T(8,128)S(1)} %get-tuple-element.46.refs_0_), channel_id=1, source_target_pairs={{0,4},{1,5},{2,6},{3,7},{4,0},{5,1},{6,2},{7,3},{8,12},{9,13},{10,... | collective-permute-start | bytes 110600 | tf_op jit(solution)/shard_map/ppermute | solution.py:31
  7.8 4.5 %collective-permute-start.3 = (f32[280,128]{1,0:T(8,128)S(1)}, f32[280,128]{1,0:T(8,128)S(1)}, u32[]{:S(2)}, u32[]{:S(2)}) collective-permute-start(f32[280,128]{1,0:T(8,128)S(1)} %get-tuple-element.48.refs_0_), channel_id=1, source_target_pairs={{0,4},{1,5},{2,6},{3,7},{4,0},{5,1},{6,2},{7,3},{8,12},{9,13},{10,... | collective-permute-start | bytes 430088 | tf_op jit(solution)/shard_map/ppermute | solution.py:31
  10.0 4.0 %collective-permute-start.5 = (f32[280,128]{1,0:T(8,128)S(1)}, f32[280,128]{1,0:T(8,128)S(1)}, u32[]{:S(2)}, u32[]{:S(2)}) collective-permute-start(f32[280,128]{1,0:T(8,128)S(1)} %shard_map.144.refs_2_.refs_4_.refs_1_), channel_id=1, source_target_pairs={{0,4},{1,5},{2,6},{3,7},{4,0},{5,1},{6,2},{7,3},{8,12},{9,13},{10,... | collective-permute-start | bytes 430088 | tf_op jit(solution)/shard_map/ppermute | solution.py:31
  10.1 4.1 %collective-permute-start.2 = (f32[8,1152]{1,0:T(8,128)S(1)}, f32[8,1152]{1,0:T(8,128)S(1)}, u32[]{:S(2)}, u32[]{:S(2)}) collective-permute-start(f32[8,1152]{1,0:T(8,128)S(1)} %shard_map.143.refs_1_.refs_0_.refs_2_), channel_id=1, source_target_pairs={{0,1},{1,0},{2,3},{3,2},{4,5},{5,4},{6,7},{7,6},{8,9},{9,8},{10,11... | collective-permute-start | bytes 110600 | tf_op jit(solution)/shard_map/ppermute | solution.py:31
  11.7 6.6 %collective-permute-start.7 = (f32[152,128]{1,0:T(8,128)S(1)}, f32[152,128]{1,0:T(8,128)S(1)}, u32[]{:S(2)}, u32[]{:S(2)}) collective-permute-start(f32[152,128]{1,0:T(8,128)S(1)} %shard_map.142.refs_2_.refs_0_), channel_id=1, source_target_pairs={{0,4},{1,5},{2,6},{3,7},{4,0},{5,1},{6,2},{7,3},{8,12},{9,13},{10,... | collective-permute-start | bytes 233480 | tf_op jit(solution)/shard_map/ppermute | solution.py:31
  11.8 4.6 %collective-permute-start.8 = (f32[152,128]{1,0:T(8,128)S(1)}, f32[152,128]{1,0:T(8,128)S(1)}, u32[]{:S(2)}, u32[]{:S(2)}) collective-permute-start(f32[152,128]{1,0:T(8,128)S(1)} %shard_map.147), channel_id=1, source_target_pairs={{0,1},{1,0},{2,3},{3,2},{4,5},{5,4},{6,7},{7,6},{8,9},{9,8},{10,11... | collective-permute-start | bytes 233480 | tf_op jit(solution)/shard_map/ppermute | solution.py:31
  12.4 5.7 %collective-permute-start.11 = (f32[240,128]{1,0:T(8,128)S(1)}, f32[240,128]{1,0:T(8,128)S(1)}, u32[]{:S(2)}, u32[]{:S(2)}) collective-permute-start(f32[240,128]{1,0:T(8,128)S(1)} %shard_map.152), channel_id=1, source_target_pairs={{0,2},{1,3},{2,0},{3,1},{4,6},{5,7},{6,4},{7,5},{8,10},{9,11},{10,... | collective-permute-start | bytes 368648 | tf_op jit(solution)/shard_map/ppermute | solution.py:31
  14.6 4.1 %collective-permute-start.6 = (f32[8,1024]{1,0:T(8,128)S(1)}, f32[8,1024]{1,0:T(8,128)S(1)}, u32[]{:S(2)}, u32[]{:S(2)}) collective-permute-start(f32[8,1024]{1,0:T(8,128)S(1)} %get-tuple-element.53.refs_4_.refs_0_.refs_2_), channel_id=1, source_target_pairs={{0,8},{1,9},{2,10},{3,11},{4,12},{5,13},{6,14},{7,15},{8,0},{9,1},... | collective-permute-start | bytes 98312 | tf_op jit(solution)/shard_map/ppermute | solution.py:31
  16.5 1.9 %collective-permute-start.9 = (f32[152,128]{1,0:T(8,128)S(1)}, f32[152,128]{1,0:T(8,128)S(1)}, u32[]{:S(2)}, u32[]{:S(2)}) collective-permute-start(f32[152,128]{1,0:T(8,128)S(1)} %shard_map.149.refs_6_.refs_1_), channel_id=1, source_target_pairs={{0,4},{1,5},{2,6},{3,7},{4,0},{5,1},{6,2},{7,3},{8,12},{9,13},{10,... | collective-permute-start | bytes 233480 | tf_op jit(solution)/shard_map/ppermute | solution.py:31
  16.5 4.5 %collective-permute-start.13 = (f32[112,128]{1,0:T(8,128)S(1)}, f32[112,128]{1,0:T(8,128)S(1)}, u32[]{:S(2)}, u32[]{:S(2)}) collective-permute-start(f32[112,128]{1,0:T(8,128)S(1)} %shard_map.153.refs_1_), channel_id=1, source_target_pairs={{0,2},{1,3},{2,0},{3,1},{4,6},{5,7},{6,4},{7,5},{8,10},{9,11},{10,... | collective-permute-start | bytes 172040 | tf_op jit(solution)/shard_map/ppermute | solution.py:31
  18.1 2.2 %collective-permute-start.12 = (f32[240,128]{1,0:T(8,128)S(1)}, f32[240,128]{1,0:T(8,128)S(1)}, u32[]{:S(2)}, u32[]{:S(2)}) collective-permute-start(f32[240,128]{1,0:T(8,128)S(1)} %shard_map.154.refs_8_.refs_2_.refs_4_), channel_id=1, source_target_pairs={{0,4},{1,5},{2,6},{3,7},{4,0},{5,1},{6,2},{7,3},{8,12},{9,13},{10,... | collective-permute-start | bytes 368648 | tf_op jit(solution)/shard_map/ppermute | solution.py:31
  19.0 4.0 %collective-permute-start.10 = (f32[8,768]{1,0:T(8,128)S(1)}, f32[8,768]{1,0:T(8,128)S(1)}, u32[]{:S(2)}, u32[]{:S(2)}) collective-permute-start(f32[8,768]{1,0:T(8,128)S(1)} %get-tuple-element.60.refs_10_.refs_5_.refs_0_.refs_3_), channel_id=1, source_target_pairs={{0,2},{1,3},{2,0},{3,1},{4,6},{5,7},{6,4},{7,5},{8,10},{9,11},{10,... | collective-permute-start | bytes 73736 | tf_op jit(solution)/shard_map/ppermute | solution.py:31
  21.0 1.8 %collective-permute-start.14 = (f32[112,128]{1,0:T(8,128)S(1)}, f32[112,128]{1,0:T(8,128)S(1)}, u32[]{:S(2)}, u32[]{:S(2)}) collective-permute-start(f32[112,128]{1,0:T(8,128)S(1)} %shard_map.156.refs_0_), channel_id=1, source_target_pairs={{0,4},{1,5},{2,6},{3,7},{4,0},{5,1},{6,2},{7,3},{8,12},{9,13},{10,... | collective-permute-start | bytes 172040 | tf_op jit(solution)/shard_map/ppermute | solution.py:31
  21.4 6.0 %collective-permute-start.16 = (f32[256,128]{1,0:T(8,128)S(1)}, f32[256,128]{1,0:T(8,128)S(1)}, u32[]{:S(2)}, u32[]{:S(2)}) collective-permute-start(f32[256,128]{1,0:T(8,128)S(1)} %shard_map.163), channel_id=1, source_target_pairs={{0,8},{1,9},{2,10},{3,11},{4,12},{5,13},{6,14},{7,15},{8,0},{9,1},... | collective-permute-start | bytes 393224 | tf_op jit(solution)/shard_map/ppermute | solution.py:31
  23.5 4.7 %collective-permute-start.15 = (f32[8,512]{1,0:T(8,128)S(1)}, f32[8,512]{1,0:T(8,128)S(1)}, u32[]{:S(2)}, u32[]{:S(2)}) collective-permute-start(f32[8,512]{1,0:T(8,128)S(1)} %get-tuple-element.73.refs_9_.refs_0_.refs_1_), channel_id=1, source_target_pairs={{0,16},{1,17},{2,18},{3,19},{4,20},{5,21},{6,22},{7,23},{8,24},{9,... | collective-permute-start | bytes 49160 | tf_op jit(solution)/shard_map/ppermute | solution.py:31
  27.4 1.4 %collective-permute-start.17 = (f32[256,128]{1,0:T(8,128)S(1)}, f32[256,128]{1,0:T(8,128)S(1)}, u32[]{:S(2)}, u32[]{:S(2)}) collective-permute-start(f32[256,128]{1,0:T(8,128)S(1)} %shard_map.164.refs_6_), channel_id=1, source_target_pairs={{0,4},{1,5},{2,6},{3,7},{4,0},{5,1},{6,2},{7,3},{8,12},{9,13},{10,... | collective-permute-start | bytes 393224 | tf_op jit(solution)/shard_map/ppermute | solution.py:31
  29.4 4.7 %collective-permute-start.18 = (f32[8,512]{1,0:T(8,128)S(1)}, f32[8,512]{1,0:T(8,128)S(1)}, u32[]{:S(2)}, u32[]{:S(2)}) collective-permute-start(f32[8,512]{1,0:T(8,128)S(1)} %shard_map.166.refs_4_.refs_1_.refs_0_), channel_id=1, source_target_pairs={{0,16},{1,17},{2,18},{3,19},{4,20},{5,21},{6,22},{7,23},{8,24},{9,... | collective-permute-start | bytes 49160 | tf_op jit(solution)/shard_map/ppermute | solution.py:31

commit v5 on v4

--- a/solution.py
+++ b/solution.py
@@ -377,11 +377,14 @@
     n_high[...], n_low[...] = halves(folded)
 
 
-def leaf_body(sections, forward, coupling, inverse, lower, base, d_high, d_low):
+def leaf_body(sections, forward, coupling, inverse, lower, *outs):
     count, block = inverse.shape[2], inverse.shape[3]
-    rhs_count = forward.shape[0]
+    d_high, d_low = outs[-2:]
     rows = [coupling[0, 0, section] for section in sections]
-    rows = jnp.concatenate([forward[...]] + rows, axis=0)
+    if len(outs) == 3:
+        rows = [forward[...]] + rows
+    rows = jnp.concatenate(rows, axis=0)
+    first = rows.shape[0] - d_high.shape[0]
     later = None
     for counter in reversed(range(count)):
         current = rows[:, counter * block : (counter + 1) * block]
@@ -389,8 +392,9 @@
             current = current - wide_times(later, lower[0, 0, counter])
         later = wide_times(current, inverse[0, 0, counter])
         columns = slice(counter * block, (counter + 1) * block)
-        base[:, columns] = later[:rhs_count]
-        d_high[:, columns], d_low[:, columns] = halves(later[rhs_count:])
+        if first:
+            outs[0][:, columns] = later[:first]
+        d_high[:, columns], d_low[:, columns] = halves(later[first:])
 
 
 def pick_body(sizes, owned, taken, places, picks, owns):
@@ -404,18 +408,22 @@
 def backward_body(
     sizes, mine, theirs, u1, n1h, n1l, u2, n2h, n2l, u3, n3h, n3l, base, d1h, d1l, d2h, d2l, picks, owns, leaf, sep
 ):
+    starts = [sum(sizes[:section]) for section in range(4)]
+
+    def pick(section):
+        return times(solved[section], [picks[starts[section] : starts[section] + sizes[section], :]], False)
+
     solved = [mine[...] + theirs[...]]
-    for known, n_high, n_low in ((u1, n1h, n1l), (u2, n2h, n2l), (u3, n3h, n3l)):
-        solved.append(known[...] - times(solved[-1], [n_high[...], n_low[...]], False))
-    picked = []
-    at = 0
-    for section in range(4):
-        picked.append(times(solved[section], [picks[at : at + sizes[section], :]], False))
-        at += sizes[section]
-    first = times(jnp.concatenate(picked[:2], axis=1), [d1h[...], d1l[...]], False)
-    second = times(jnp.concatenate(picked[2:], axis=1), [d2h[...], d2l[...]], False)
-    leaf[0, 0] = base[...] - first - second
-    sep[0, 0] = times(jnp.concatenate(solved, axis=1), [owns[...]], False)
+    solved.append(u1[...] - times(solved[0], [n1h[...], n1l[...]], False))
+    picked = [pick(0)]
+    solved.append(u2[...] - times(solved[1], [n2h[...], n2l[...]], False))
+    picked.append(pick(1))
+    solved.append(u3[...] - times(solved[2], [n3h[...], n3l[...]], False))
+    first = base[...] - times(jnp.concatenate(picked, axis=1), [d1h[...], d1l[...]], False)
+    owned = times(jnp.concatenate(solved[:3], axis=1), [owns[: starts[3], :]], False)
+    picked = jnp.concatenate([pick(2), pick(3)], axis=1)
+    leaf[0, 0] = first - times(picked, [d2h[...], d2l[...]], False)
+    sep[0, 0] = owned + times(solved[3], [owns[starts[3] :, :]], False)
 
 
 def gathered(
@@ -527,11 +535,12 @@
             *pieces, microseconds=FOLD_US, after=after,
         )
 
-    def solve(sections, after):
+    def solve(sections, with_forward, after):
+        rows = len(sections) * LANES
         return vmem_call(
             functools.partial(leaf_body, sections),
-            [((rhs_count, rhs_leaf.shape[3]), jnp.float32)]
-            + [((len(sections) * LANES, rhs_leaf.shape[3]), jnp.bfloat16)] * 2,
+            [((rhs_count, rhs_leaf.shape[3]), jnp.float32)] * with_forward
+            + [((rows, rhs_leaf.shape[3]), jnp.bfloat16)] * 2,
             forward, coupling, leaf_inv, leaf_sub, microseconds=LEAF_US, after=after,
         )
 
@@ -560,7 +569,7 @@
     sums, four_level = eliminate(3, sums, theirs, [table], ())
 
     theirs = from_partner(sums, axes, third)
-    solved_first = solve((0, 1), (sums,))
+    solved_first = solve((0, 1), True, (sums,))
     by_two = arrive(two, two_at, (solved_first[0],), X2_US)
     following, last_at = message(choose([by_third, by_two], (1,)), (sums,), Y2_US)
     by_near = arrive(near, near_at, (following,), NEAR_US)
@@ -575,8 +584,7 @@
     table = level(1, both[:early], (sums,))
     arrive(last, last_at, (table[0],), LAST_US)
     folded_three = fold(2, three_level, (sums,))
-    folded_four = fold(3, four_level, (sums,))
-    late = (folded_three[0], folded_four[0])
+    late = (folded_three[0],)
     sums, two_level = eliminate(1, sums, theirs, [table, level(1, both[early:])], late)
 
     theirs = from_partner(sums, axes, first)
@@ -590,7 +598,8 @@
         top_body, [((rhs_count, sizes[0]), jnp.float32)], sums, *level(0, both, (sums,)), microseconds=0.5
     )
     theirs = from_partner(partial, axes, first)
-    solved_second = solve((2, 3), (partial,))
+    solved_second = solve((2, 3), False, (partial,))
+    folded_four = fold(3, four_level, (partial,))
     picks = vmem_call(
         functools.partial(pick_body, sizes, owned, taken),
         [((total, interface.shape[3]), jnp.bfloat16), ((total, sum(owned)), jnp.bfloat16)],
@@ -599,7 +608,7 @@
     leaf, sep = vmem_call(
         functools.partial(backward_body, sizes),
         [(rhs_leaf.shape, jnp.float32), (sep_rhs.shape, jnp.float32)],
-        partial, theirs, *folded_two, *folded_three, *folded_four, *solved_first, *solved_second[1:], *picks,
+        partial, theirs, *folded_two, *folded_three, *folded_four, *solved_first, *solved_second, *picks,
         microseconds=2.0,
     )
     return (leaf, sep)

time: 35.8 us -> 35.3 us (0.986)
  Pallas kernels: 11.2 us -> 10.6 us
    pallas_call x30, Pallas kernels: 11.2 us -> 10.6 us  [vmem_call(): pl.pallas_call(kernel, out_shape=out_shape, in_specs=[pl.BlockSpec(memory...]
  transfers between devices with their start and end apart: 19 -> 19, of which waited for: 7 -> 8; matrix products, arithmetic and copies ran while one was open for 0% -> 0% of each run, Pallas kernels for 23% -> 22%
where the time goes in v5:
time: 35.3 us; the launch traced here: 35.1 us
  starting transfers between devices  19.3 us (55%)
  Pallas kernels  10.6 us (30%)
  waiting for transfers between devices  4.26 us (12%)
  between operations  0.91 us (3%)
    ppermute x19, starting transfers between devices, from_partner(): lax.ppermute(value, axis, [(i, i ^ 1 << distance) for i in range(lax.axis...  19.3 us
    pallas_call x30, Pallas kernels, vmem_call(): pl.pallas_call(kernel, out_shape=out_shape, in_specs=[pl.BlockSpec(memory...  10.6 us
    ppermute x19, waiting for transfers between devices, from_partner(): lax.ppermute(value, axis, [(i, i ^ 1 << distance) for i in range(lax.axis...  4.26 us
  transfers between devices with their start and end apart: 19, of which 8 were waited for; matrix products, arithmetic and copies ran while one was open for 0% of the time, Pallas kernels for 22%

profile of v5, /device:TPU:0, one launch (start us, length us, event | category | flops | bytes accessed | tf_op | source)
XLA Modules:
  0.0 35.1 jit_solution(6160096950996215539)
XLA Ops:
  0.6 0.0 copy-start.3
  0.6 0.0 copy-start.1
  0.7 0.0 copy-start.2
  0.7 0.0 copy-start.4
  0.7 0.0 copy-start
  0.7 1.0 %shard_map.141 = (f32[280,128]{1,0:T(8,128)S(1)}, f32[152,128]{1,0:T(8,128)S(1)}) custom-call(f32[1,1,16,512]{3,2,1,0:T(8,128)} %refs_0_.4, f32[1,1,16,256]{3,2,1,0:T(8,128)} %refs_1_.5, f32[1,1,32,256]{3,2,1,0:T(8,128)} %refs_2_.5, f32[1,1,32,128]{3,2,1,0:T(8,128)} %refs_3_.5, f32[1,1,16,128]{3,2,1,0:T(8,128)} %refs_4_.3, f32[1,1,32,128]{3,2,1,0:T(8,128)} %refs_5_.3, ...), custom_call_target="tpu_custom_call" | custom-call | flops 1000000000 | tf_op jit(solution)/shard_map/pallas_call | solution.py:213
  1.7 0.0 copy-start.5
  1.7 3.1 %collective-permute-start.1 = (f32[152,128]{1,0:T(8,128)S(1)}, f32[152,128]{1,0:T(8,128)S(1)}, u32[]{:S(2)}, u32[]{:S(2)}) collective-permute-start(f32[152,128]{1,0:T(8,128)S(1)} %get-tuple-element.47), channel_id=1, source_target_pairs={{0,8},{1,9},{2,10},{3,11},{4,12},{5,13},{6,14},{7,15},{8,0},{9,1},... | collective-permute-start | bytes 233480 | tf_op jit(solution)/shard_map/ppermute | solution.py:31
  4.8 1.5 %collective-permute-start.4 = (f32[280,128]{1,0:T(8,128)S(1)}, f32[280,128]{1,0:T(8,128)S(1)}, u32[]{:S(2)}, u32[]{:S(2)}) collective-permute-start(f32[280,128]{1,0:T(8,128)S(1)} %get-tuple-element.48.refs_0_), channel_id=1, source_target_pairs={{0,1},{1,0},{2,3},{3,2},{4,5},{5,4},{6,7},{7,6},{8,9},{9,8},{10,11... | collective-permute-start | bytes 430088 | tf_op jit(solution)/shard_map/ppermute | solution.py:31
  6.3 0.0 copy-done.4
  6.3 0.0 copy-done
  6.3 1.5 %shard_map.140 = (f32[8,512]{1,0:T(8,128)S(1)}, f32[8,1152]{1,0:T(8,128)S(1)}) custom-call(f32[1,1,8,512]{3,2,1,0:T(8,128)S(1)} %copy-done.3, f32[1,1,4,128,128]{4,3,2,1,0:T(8,128)S(1)} %copy-done.1, f32[1,1,3,128,128]{4,3,2,1,0:T(8,128)S(1)} %copy-done.2, f32[1,1,8,96]{3,2,1,0:T(8,128)S(1)} %copy-done.4, s32[1,1,4,128]{3,2,1,0:T(4,128)S(1)} %copy-done.5, ...), custom_call_target="tpu_custom_call" | custom-call | flops 2000000000 | tf_op jit(solution)/shard_map/pallas_call | solution.py:213
  7.8 0.1 collective-permute-start
  7.8 0.5 %collective-permute-start.3 = (f32[280,128]{1,0:T(8,128)S(1)}, f32[280,128]{1,0:T(8,128)S(1)}, u32[]{:S(2)}, u32[]{:S(2)}) collective-permute-start(f32[280,128]{1,0:T(8,128)S(1)} %get-tuple-element.48.refs_0_), channel_id=1, source_target_pairs={{0,4},{1,5},{2,6},{3,7},{4,0},{5,1},{6,2},{7,3},{8,12},{9,13},{10,... | collective-permute-start | bytes 430088 | tf_op jit(solution)/shard_map/ppermute | solution.py:31
  8.3 0.0 collective-permute-done.1.refs_0_
  8.4 0.7 %collective-permute-done.refs_1_ = f32[8,1152]{1,0:T(8,128)S(1)} collective-permute-done((f32[8,1152]{1,0:T(8,128)S(1)}, f32[8,1152]{1,0:T(8,128)S(1)}, u32[]{:S(2)}, u32[]{:S(2)}) %collective-permute-start) | collective-permute-done | bytes 36896 | tf_op jit(solution)/shard_map/ppermute | solution.py:31
  9.1 1.0 %collective-permute-done.4.refs_0_ = f32[280,128]{1,0:T(8,128)S(1)} collective-permute-done((f32[280,128]{1,0:T(8,128)S(1)}, f32[280,128]{1,0:T(8,128)S(1)}, u32[]{:S(2)}, u32[]{:S(2)}) %collective-permute-start.4) | collective-permute-done | bytes 143392 | tf_op jit(solution)/shard_map/ppermute | solution.py:31
  10.0 0.1 collective-permute-start.5
  10.1 1.6 %collective-permute-start.2 = (f32[8,1152]{1,0:T(8,128)S(1)}, f32[8,1152]{1,0:T(8,128)S(1)}, u32[]{:S(2)}, u32[]{:S(2)}) collective-permute-start(f32[8,1152]{1,0:T(8,128)S(1)} %shard_map.143.refs_1_.refs_0_.refs_2_), channel_id=1, source_target_pairs={{0,1},{1,0},{2,3},{3,2},{4,5},{5,4},{6,7},{7,6},{8,9},{9,8},{10,11... | collective-permute-start | bytes 110600 | tf_op jit(solution)/shard_map/ppermute | solution.py:31
  11.7 0.2 collective-permute-start.7
  11.8 0.5 %collective-permute-start.8 = (f32[152,128]{1,0:T(8,128)S(1)}, f32[152,128]{1,0:T(8,128)S(1)}, u32[]{:S(2)}, u32[]{:S(2)}) collective-permute-start(f32[152,128]{1,0:T(8,128)S(1)} %shard_map.147), channel_id=1, source_target_pairs={{0,1},{1,0},{2,3},{3,2},{4,5},{5,4},{6,7},{7,6},{8,9},{9,8},{10,11... | collective-permute-start | bytes 233480 | tf_op jit(solution)/shard_map/ppermute | solution.py:31
  12.4 0.0 collective-permute-done.3.refs_1_
  12.4 1.6 %collective-permute-start.11 = (f32[240,128]{1,0:T(8,128)S(1)}, f32[240,128]{1,0:T(8,128)S(1)}, u32[]{:S(2)}, u32[]{:S(2)}) collective-permute-start(f32[240,128]{1,0:T(8,128)S(1)} %shard_map.152), channel_id=1, source_target_pairs={{0,2},{1,3},{2,0},{3,1},{4,6},{5,7},{6,4},{7,5},{8,10},{9,11},{10,... | collective-permute-start | bytes 368648 | tf_op jit(solution)/shard_map/ppermute | solution.py:31
  14.0 0.0 collective-permute-done.5.refs_3_.refs_5_
  14.0 0.2 shard_map.145
  14.2 0.0 collective-permute-done.2.refs_1_
  14.2 0.3 shard_map.146
  14.6 0.5 %collective-permute-start.6 = (f32[8,1024]{1,0:T(8,128)S(1)}, f32[8,1024]{1,0:T(8,128)S(1)}, u32[]{:S(2)}, u32[]{:S(2)}) collective-permute-start(f32[8,1024]{1,0:T(8,128)S(1)} %get-tuple-element.53.refs_4_.refs_0_.refs_2_), channel_id=1, source_target_pairs={{0,8},{1,9},{2,10},{3,11},{4,12},{5,13},{6,14},{7,15},{8,0},{9,1},... | collective-permute-start | bytes 98312 | tf_op jit(solution)/shard_map/ppermute | solution.py:31
  15.0 1.0 %shard_map.148 = (f32[8,512]{1,0:T(8,128)S(1)}, bf16[256,512]{1,0:T(8,128)(2,1)S(1)}, bf16[256,512]{1,0:T(8,128)(2,1)S(1)}) custom-call(f32[8,512]{1,0:T(8,128)S(1)} %get-tuple-element.54.refs_0_, f32[1,1,4,128,512]{4,3,2,1,0:T(8,128)S(1)} %copy-done, f32[1,1,4,128,128]{4,3,2,1,0:T(8,128)S(1)} %copy-done.1, f32[1,1,3,128,128]{4,3,2,1,0:T(8,128)S(1)} %copy-done.2, ...), custom_call_target="tpu_custom_call" | custom-call | flops 1000000000 | tf_op jit(solution)/shard_map/pallas_call | solution.py:213
  16.0 0.4 %collective-permute-done.8.refs_0_ = f32[152,128]{1,0:T(8,128)S(1)} collective-permute-done((f32[152,128]{1,0:T(8,128)S(1)}, f32[152,128]{1,0:T(8,128)S(1)}, u32[]{:S(2)}, u32[]{:S(2)}) %collective-permute-start.8) | collective-permute-done | bytes 77856 | tf_op jit(solution)/shard_map/ppermute | solution.py:31
  16.5 0.0 collective-permute-start.9
  16.5 1.6 %collective-permute-start.13 = (f32[112,128]{1,0:T(8,128)S(1)}, f32[112,128]{1,0:T(8,128)S(1)}, u32[]{:S(2)}, u32[]{:S(2)}) collective-permute-start(f32[112,128]{1,0:T(8,128)S(1)} %shard_map.153.refs_1_), channel_id=1, source_target_pairs={{0,2},{1,3},{2,0},{3,1},{4,6},{5,7},{6,4},{7,5},{8,10},{9,11},{10,... | collective-permute-start | bytes 172040 | tf_op jit(solution)/shard_map/ppermute | solution.py:31
  18.1 0.0 collective-permute-done.11.refs_0_
  18.1 0.2 collective-permute-start.12
  18.3 0.0 collective-permute-done.7.refs_3_
  18.3 0.0 collective-permute-done.9.refs_7_
  18.3 0.3 shard_map.150
  18.6 0.0 collective-permute-done.6.refs_1_
  18.6 0.4 %shard_map.151 = (f32[8,768]{1,0:T(8,128)S(1)}, f32[8,256]{1,0:T(8,128)S(1)}) custom-call(f32[8,1024]{1,0:T(8,128)S(1)} %get-tuple-element.53.refs_4_.refs_0_.refs_2_, f32[8,1024]{1,0:T(8,128)S(1)} %collective-permute-done.6.refs_1_, bf16[256,256]{1,0:T(8,128)(2,1)S(1)} %get-tuple-element.56.refs_2_.refs_1_, ...), custom_call_target="tpu_custom_call" | custom-call | flops 5000000000 | tf_op jit(solution)/shard_map/pallas_call | solution.py:213
  19.0 1.3 %collective-permute-start.10 = (f32[8,768]{1,0:T(8,128)S(1)}, f32[8,768]{1,0:T(8,128)S(1)}, u32[]{:S(2)}, u32[]{:S(2)}) collective-permute-start(f32[8,768]{1,0:T(8,128)S(1)} %get-tuple-element.60.refs_10_.refs_5_.refs_0_.refs_3_), channel_id=1, source_target_pairs={{0,2},{1,3},{2,0},{3,1},{4,6},{5,7},{6,4},{7,5},{8,10},{9,11},{10,... | collective-permute-start | bytes 73736 | tf_op jit(solution)/shard_map/ppermute | solution.py:31
  20.3 0.0 collective-permute-done.12.refs_9_.refs_5_
  20.3 0.6 %shard_map.155 = (bf16[192,256]{1,0:T(8,128)(2,1)S(1)}, bf16[192,256]{1,0:T(8,128)(2,1)S(1)}, bf16[192,512]{1,0:T(8,128)(2,1)S(1)}, bf16[192,512]{1,0:T(8,128)(2,1)S(1)}) custom-call(f32[280,128]{1,0:T(8,128)S(1)} %get-tuple-element.48.refs_0_, f32[280,128]{1,0:T(8,128)S(1)} %collective-permute-done.3.refs_1_, f32[152,128]{1,0:T(8,128)S(1)} %shard_map.142.refs_2_.refs_0_, ...), custom_call_target="tpu_custom_call" | custom-call | flops 400000000 | tf_op jit(solution)/shard_map/pallas_call | solution.py:213
  20.9 0.0 collective-permute-done.13.refs_0_
  20.9 0.1 collective-permute-start.14
  21.1 1.1 %collective-permute-start.16 = (f32[256,128]{1,0:T(8,128)S(1)}, f32[256,128]{1,0:T(8,128)S(1)}, u32[]{:S(2)}, u32[]{:S(2)}) collective-permute-start(f32[256,128]{1,0:T(8,128)S(1)} %shard_map.162), channel_id=1, source_target_pairs={{0,8},{1,9},{2,10},{3,11},{4,12},{5,13},{6,14},{7,15},{8,0},{9,1},... | collective-permute-start | bytes 393224 | tf_op jit(solution)/shard_map/ppermute | solution.py:31
  22.1 0.3 shard_map.158
  22.5 0.0 collective-permute-done.14.refs_1_
  22.5 0.3 shard_map.157
  22.8 0.1 collective-permute-done.10.refs_1_
  22.9 0.4 %shard_map.159 = (f32[8,512]{1,0:T(8,128)S(1)}, f32[8,256]{1,0:T(8,128)S(1)}) custom-call(f32[8,768]{1,0:T(8,128)S(1)} %get-tuple-element.60.refs_10_.refs_5_.refs_0_.refs_3_, f32[8,768]{1,0:T(8,128)S(1)} %collective-permute-done.10.refs_1_, bf16[192,256]{1,0:T(8,128)(2,1)S(1)} %get-tuple-element.61.refs_1_.refs_2_, ...), custom_call_target="tpu_custom_call" | custom-call | flops 5000000000 | tf_op jit(solution)/shard_map/pallas_call | solution.py:213
  23.3 2.7 %collective-permute-start.15 = (f32[8,512]{1,0:T(8,128)S(1)}, f32[8,512]{1,0:T(8,128)S(1)}, u32[]{:S(2)}, u32[]{:S(2)}) collective-permute-start(f32[8,512]{1,0:T(8,128)S(1)} %get-tuple-element.71.refs_9_.refs_0_.refs_1_), channel_id=1, source_target_pairs={{0,16},{1,17},{2,18},{3,19},{4,20},{5,21},{6,22},{7,23},{8,24},{9,... | collective-permute-start | bytes 49160 | tf_op jit(solution)/shard_map/ppermute | solution.py:31
  26.0 0.8 %shard_map.160 = (f32[8,256]{1,0:T(8,128)S(1)}, bf16[512,256]{1,0:T(8,128)(2,1)S(1)}, bf16[512,256]{1,0:T(8,128)(2,1)S(1)}) custom-call(f32[8,256]{1,0:T(8,128)S(1)} %get-tuple-element.72.refs_0_, bf16[192,256]{1,0:T(8,128)(2,1)S(1)} %get-tuple-element.61.refs_1_.refs_2_, bf16[192,256]{1,0:T(8,128)(2,1)S(1)} %get-tuple-element.62.refs_3_.refs_2_, ...), custom_call_target="tpu_custom_call" | custom-call | flops 500000000 | tf_op jit(solution)/shard_map/pallas_call | solution.py:213
  26.8 0.2 collective-permute-done.16.refs_0_
  27.0 0.1 collective-permute-start.17
  27.1 0.9 %collective-permute-done.15.refs_1_ = f32[8,512]{1,0:T(8,128)S(1)} collective-permute-done((f32[8,512]{1,0:T(8,128)S(1)}, f32[8,512]{1,0:T(8,128)S(1)}, u32[]{:S(2)}, u32[]{:S(2)}) %collective-permute-start.15) | collective-permute-done | bytes 16416 | tf_op jit(solution)/shard_map/ppermute | solution.py:31
  28.0 0.4 %collective-permute-done.17.refs_7_ = f32[256,128]{1,0:T(8,128)S(1)} collective-permute-done((f32[256,128]{1,0:T(8,128)S(1)}, f32[256,128]{1,0:T(8,128)S(1)}, u32[]{:S(2)}, u32[]{:S(2)}) %collective-permute-start.17) | collective-permute-done | bytes 131104 | tf_op jit(solution)/shard_map/ppermute | solution.py:31
  28.4 0.1 shard_map.164
  28.5 0.5 %shard_map.165.refs_5_.refs_4_.refs_1_.refs_0_ = f32[8,512]{1,0:T(8,128)S(1)} custom-call(f32[8,512]{1,0:T(8,128)S(1)} %shard_map.161.refs_8_.refs_0_, bf16[256,512]{1,0:T(8,128)(2,1)S(1)} %get-tuple-element.74.refs_1_, bf16[256,512]{1,0:T(8,128)(2,1)S(1)} %get-tuple-element.75.refs_2_), custom_call_target="tpu_custom_call" | custom-call | flops 500000000 | tf_op jit(solution)/shard_map/pallas_call | solution.py:213
  29.0 2.8 %collective-permute-start.18 = (f32[8,512]{1,0:T(8,128)S(1)}, f32[8,512]{1,0:T(8,128)S(1)}, u32[]{:S(2)}, u32[]{:S(2)}) collective-permute-start(f32[8,512]{1,0:T(8,128)S(1)} %shard_map.165.refs_5_.refs_4_.refs_1_.refs_0_), channel_id=1, source_target_pairs={{0,16},{1,17},{2,18},{3,19},{4,20},{5,21},{6,22},{7,23},{8,24},{9,... | collective-permute-start | bytes 49160 | tf_op jit(solution)/shard_map/ppermute | solution.py:31
  31.8 1.0 %shard_map.167 = (bf16[256,512]{1,0:T(8,128)(2,1)S(1)}, bf16[256,512]{1,0:T(8,128)(2,1)S(1)}) custom-call(f32[8,512]{1,0:T(8,128)S(1)} %get-tuple-element.54.refs_0_, f32[1,1,4,128,512]{4,3,2,1,0:T(8,128)S(1)} %copy-done, f32[1,1,4,128,128]{4,3,2,1,0:T(8,128)S(1)} %copy-done.1, f32[1,1,3,128,128]{4,3,2,1,0:T(8,128)S(1)} %copy-done.2, ...), custom_call_target="tpu_custom_call" | custom-call | flops 1000000000 | tf_op jit(solution)/shard_map/pallas_call | solution.py:213
  32.8 0.3 shard_map.166
  33.1 0.1 shard_map.168
  33.2 0.5 %collective-permute-done.18.refs_1_ = f32[8,512]{1,0:T(8,128)S(1)} collective-permute-done((f32[8,512]{1,0:T(8,128)S(1)}, f32[8,512]{1,0:T(8,128)S(1)}, u32[]{:S(2)}, u32[]{:S(2)}) %collective-permute-start.18) | collective-permute-done | bytes 16416 | tf_op jit(solution)/shard_map/ppermute | solution.py:31
  33.7 1.4 %shard_map.169 = (f32[1,1,8,512]{3,2,1,0:T(8,128)}, f32[1,1,8,96]{3,2,1,0:T(8,128)}) custom-call(f32[8,512]{1,0:T(8,128)S(1)} %shard_map.165.refs_5_.refs_4_.refs_1_.refs_0_, f32[8,512]{1,0:T(8,128)S(1)} %collective-permute-done.18.refs_1_, f32[8,256]{1,0:T(8,128)S(1)} %get-tuple-element.73.refs_2_, bf16[512,256]{1,0:T(8,128)(2,1)S(1)} %get-tuple-element.76.refs_3_, ...), custom_call_target="tpu_custom_call" | custom-call | flops 2000000000 | tf_op jit(solution)/shard_map/pallas_call | solution.py:213
  (16 shorter events, 0.1 us)
Async XLA Ops:
  0.6 5.7 %copy-start.3 = (f32[1,1,8,512]{3,2,1,0:T(8,128)S(1)}, f32[1,1,8,512]{3,2,1,0:T(8,128)}, u32[]{:S(2)}) copy-start(f32[1,1,8,512]{3,2,1,0:T(8,128)} %refs_0_.3) | copy-start | bytes 49156
  0.6 5.7 %copy-start.1 = (f32[1,1,4,128,128]{4,3,2,1,0:T(8,128)S(1)}, f32[1,1,4,128,128]{4,3,2,1,0:T(8,128)}, u32[]{:S(2)}) copy-start(f32[1,1,4,128,128]{4,3,2,1,0:T(8,128)} %refs_2_.7) | copy-start | bytes 786436
  0.7 5.6 %copy-start.2 = (f32[1,1,3,128,128]{4,3,2,1,0:T(8,128)S(1)}, f32[1,1,3,128,128]{4,3,2,1,0:T(8,128)}, u32[]{:S(2)}) copy-start(f32[1,1,3,128,128]{4,3,2,1,0:T(8,128)} %refs_3_.7) | copy-start | bytes 589828
  0.7 5.6 %copy-start.4 = (f32[1,1,8,96]{3,2,1,0:T(8,128)S(1)}, f32[1,1,8,96]{3,2,1,0:T(8,128)}, u32[]{:S(2)}) copy-start(f32[1,1,8,96]{3,2,1,0:T(8,128)} %refs_3_.4) | copy-start | bytes 9220
  0.7 5.6 %copy-start = (f32[1,1,4,128,512]{4,3,2,1,0:T(8,128)S(1)}, f32[1,1,4,128,512]{4,3,2,1,0:T(8,128)}, u32[]{:S(2)}) copy-start(f32[1,1,4,128,512]{4,3,2,1,0:T(8,128)} %refs_1_.7) | copy-start | bytes 3145732
  1.7 4.6 %copy-start.5 = (s32[1,1,4,128]{3,2,1,0:T(4,128)S(1)}, s32[1,1,4,128]{3,2,1,0:T(4,128)}, u32[]{:S(2)}) copy-start(s32[1,1,4,128]{3,2,1,0:T(4,128)} %refs_0_.5) | copy-start | bytes 6148
  1.7 6.6 %collective-permute-start.1 = (f32[152,128]{1,0:T(8,128)S(1)}, f32[152,128]{1,0:T(8,128)S(1)}, u32[]{:S(2)}, u32[]{:S(2)}) collective-permute-start(f32[152,128]{1,0:T(8,128)S(1)} %get-tuple-element.47), channel_id=1, source_target_pairs={{0,8},{1,9},{2,10},{3,11},{4,12},{5,13},{6,14},{7,15},{8,0},{9,1},... | collective-permute-start | bytes 233480 | tf_op jit(solution)/shard_map/ppermute | solution.py:31
  4.8 5.2 %collective-permute-start.4 = (f32[280,128]{1,0:T(8,128)S(1)}, f32[280,128]{1,0:T(8,128)S(1)}, u32[]{:S(2)}, u32[]{:S(2)}) collective-permute-start(f32[280,128]{1,0:T(8,128)S(1)} %get-tuple-element.48.refs_0_), channel_id=1, source_target_pairs={{0,1},{1,0},{2,3},{3,2},{4,5},{5,4},{6,7},{7,6},{8,9},{9,8},{10,11... | collective-permute-start | bytes 430088 | tf_op jit(solution)/shard_map/ppermute | solution.py:31
  7.8 1.3 %collective-permute-start = (f32[8,1152]{1,0:T(8,128)S(1)}, f32[8,1152]{1,0:T(8,128)S(1)}, u32[]{:S(2)}, u32[]{:S(2)}) collective-permute-start(f32[8,1152]{1,0:T(8,128)S(1)} %get-tuple-element.46.refs_0_), channel_id=1, source_target_pairs={{0,4},{1,5},{2,6},{3,7},{4,0},{5,1},{6,2},{7,3},{8,12},{9,13},{10,... | collective-permute-start | bytes 110600 | tf_op jit(solution)/shard_map/ppermute | solution.py:31
  7.8 4.5 %collective-permute-start.3 = (f32[280,128]{1,0:T(8,128)S(1)}, f32[280,128]{1,0:T(8,128)S(1)}, u32[]{:S(2)}, u32[]{:S(2)}) collective-permute-start(f32[280,128]{1,0:T(8,128)S(1)} %get-tuple-element.48.refs_0_), channel_id=1, source_target_pairs={{0,4},{1,5},{2,6},{3,7},{4,0},{5,1},{6,2},{7,3},{8,12},{9,13},{10,... | collective-permute-start | bytes 430088 | tf_op jit(solution)/shard_map/ppermute | solution.py:31
  10.0 4.0 %collective-permute-start.5 = (f32[280,128]{1,0:T(8,128)S(1)}, f32[280,128]{1,0:T(8,128)S(1)}, u32[]{:S(2)}, u32[]{:S(2)}) collective-permute-start(f32[280,128]{1,0:T(8,128)S(1)} %shard_map.144.refs_2_.refs_4_.refs_1_), channel_id=1, source_target_pairs={{0,4},{1,5},{2,6},{3,7},{4,0},{5,1},{6,2},{7,3},{8,12},{9,13},{10,... | collective-permute-start | bytes 430088 | tf_op jit(solution)/shard_map/ppermute | solution.py:31
  10.1 4.1 %collective-permute-start.2 = (f32[8,1152]{1,0:T(8,128)S(1)}, f32[8,1152]{1,0:T(8,128)S(1)}, u32[]{:S(2)}, u32[]{:S(2)}) collective-permute-start(f32[8,1152]{1,0:T(8,128)S(1)} %shard_map.143.refs_1_.refs_0_.refs_2_), channel_id=1, source_target_pairs={{0,1},{1,0},{2,3},{3,2},{4,5},{5,4},{6,7},{7,6},{8,9},{9,8},{10,11... | collective-permute-start | bytes 110600 | tf_op jit(solution)/shard_map/ppermute | solution.py:31
  11.7 6.6 %collective-permute-start.7 = (f32[152,128]{1,0:T(8,128)S(1)}, f32[152,128]{1,0:T(8,128)S(1)}, u32[]{:S(2)}, u32[]{:S(2)}) collective-permute-start(f32[152,128]{1,0:T(8,128)S(1)} %shard_map.142.refs_2_.refs_0_), channel_id=1, source_target_pairs={{0,4},{1,5},{2,6},{3,7},{4,0},{5,1},{6,2},{7,3},{8,12},{9,13},{10,... | collective-permute-start | bytes 233480 | tf_op jit(solution)/shard_map/ppermute | solution.py:31
  11.8 4.6 %collective-permute-start.8 = (f32[152,128]{1,0:T(8,128)S(1)}, f32[152,128]{1,0:T(8,128)S(1)}, u32[]{:S(2)}, u32[]{:S(2)}) collective-permute-start(f32[152,128]{1,0:T(8,128)S(1)} %shard_map.147), channel_id=1, source_target_pairs={{0,1},{1,0},{2,3},{3,2},{4,5},{5,4},{6,7},{7,6},{8,9},{9,8},{10,11... | collective-permute-start | bytes 233480 | tf_op jit(solution)/shard_map/ppermute | solution.py:31
  12.4 5.7 %collective-permute-start.11 = (f32[240,128]{1,0:T(8,128)S(1)}, f32[240,128]{1,0:T(8,128)S(1)}, u32[]{:S(2)}, u32[]{:S(2)}) collective-permute-start(f32[240,128]{1,0:T(8,128)S(1)} %shard_map.152), channel_id=1, source_target_pairs={{0,2},{1,3},{2,0},{3,1},{4,6},{5,7},{6,4},{7,5},{8,10},{9,11},{10,... | collective-permute-start | bytes 368648 | tf_op jit(solution)/shard_map/ppermute | solution.py:31
  14.6 4.1 %collective-permute-start.6 = (f32[8,1024]{1,0:T(8,128)S(1)}, f32[8,1024]{1,0:T(8,128)S(1)}, u32[]{:S(2)}, u32[]{:S(2)}) collective-permute-start(f32[8,1024]{1,0:T(8,128)S(1)} %get-tuple-element.53.refs_4_.refs_0_.refs_2_), channel_id=1, source_target_pairs={{0,8},{1,9},{2,10},{3,11},{4,12},{5,13},{6,14},{7,15},{8,0},{9,1},... | collective-permute-start | bytes 98312 | tf_op jit(solution)/shard_map/ppermute | solution.py:31
  16.5 1.9 %collective-permute-start.9 = (f32[152,128]{1,0:T(8,128)S(1)}, f32[152,128]{1,0:T(8,128)S(1)}, u32[]{:S(2)}, u32[]{:S(2)}) collective-permute-start(f32[152,128]{1,0:T(8,128)S(1)} %shard_map.149.refs_6_.refs_1_), channel_id=1, source_target_pairs={{0,4},{1,5},{2,6},{3,7},{4,0},{5,1},{6,2},{7,3},{8,12},{9,13},{10,... | collective-permute-start | bytes 233480 | tf_op jit(solution)/shard_map/ppermute | solution.py:31
  16.5 4.4 %collective-permute-start.13 = (f32[112,128]{1,0:T(8,128)S(1)}, f32[112,128]{1,0:T(8,128)S(1)}, u32[]{:S(2)}, u32[]{:S(2)}) collective-permute-start(f32[112,128]{1,0:T(8,128)S(1)} %shard_map.153.refs_1_), channel_id=1, source_target_pairs={{0,2},{1,3},{2,0},{3,1},{4,6},{5,7},{6,4},{7,5},{8,10},{9,11},{10,... | collective-permute-start | bytes 172040 | tf_op jit(solution)/shard_map/ppermute | solution.py:31
  18.1 2.2 %collective-permute-start.12 = (f32[240,128]{1,0:T(8,128)S(1)}, f32[240,128]{1,0:T(8,128)S(1)}, u32[]{:S(2)}, u32[]{:S(2)}) collective-permute-start(f32[240,128]{1,0:T(8,128)S(1)} %shard_map.154.refs_8_.refs_2_.refs_4_), channel_id=1, source_target_pairs={{0,4},{1,5},{2,6},{3,7},{4,0},{5,1},{6,2},{7,3},{8,12},{9,13},{10,... | collective-permute-start | bytes 368648 | tf_op jit(solution)/shard_map/ppermute | solution.py:31
  19.0 3.8 %collective-permute-start.10 = (f32[8,768]{1,0:T(8,128)S(1)}, f32[8,768]{1,0:T(8,128)S(1)}, u32[]{:S(2)}, u32[]{:S(2)}) collective-permute-start(f32[8,768]{1,0:T(8,128)S(1)} %get-tuple-element.60.refs_10_.refs_5_.refs_0_.refs_3_), channel_id=1, source_target_pairs={{0,2},{1,3},{2,0},{3,1},{4,6},{5,7},{6,4},{7,5},{8,10},{9,11},{10,... | collective-permute-start | bytes 73736 | tf_op jit(solution)/shard_map/ppermute | solution.py:31
  20.9 1.5 %collective-permute-start.14 = (f32[112,128]{1,0:T(8,128)S(1)}, f32[112,128]{1,0:T(8,128)S(1)}, u32[]{:S(2)}, u32[]{:S(2)}) collective-permute-start(f32[112,128]{1,0:T(8,128)S(1)} %shard_map.156.refs_0_), channel_id=1, source_target_pairs={{0,4},{1,5},{2,6},{3,7},{4,0},{5,1},{6,2},{7,3},{8,12},{9,13},{10,... | collective-permute-start | bytes 172040 | tf_op jit(solution)/shard_map/ppermute | solution.py:31
  21.1 5.9 %collective-permute-start.16 = (f32[256,128]{1,0:T(8,128)S(1)}, f32[256,128]{1,0:T(8,128)S(1)}, u32[]{:S(2)}, u32[]{:S(2)}) collective-permute-start(f32[256,128]{1,0:T(8,128)S(1)} %shard_map.162), channel_id=1, source_target_pairs={{0,8},{1,9},{2,10},{3,11},{4,12},{5,13},{6,14},{7,15},{8,0},{9,1},... | collective-permute-start | bytes 393224 | tf_op jit(solution)/shard_map/ppermute | solution.py:31
  23.3 4.7 %collective-permute-start.15 = (f32[8,512]{1,0:T(8,128)S(1)}, f32[8,512]{1,0:T(8,128)S(1)}, u32[]{:S(2)}, u32[]{:S(2)}) collective-permute-start(f32[8,512]{1,0:T(8,128)S(1)} %get-tuple-element.71.refs_9_.refs_0_.refs_1_), channel_id=1, source_target_pairs={{0,16},{1,17},{2,18},{3,19},{4,20},{5,21},{6,22},{7,23},{8,24},{9,... | collective-permute-start | bytes 49160 | tf_op jit(solution)/shard_map/ppermute | solution.py:31
  27.0 1.4 %collective-permute-start.17 = (f32[256,128]{1,0:T(8,128)S(1)}, f32[256,128]{1,0:T(8,128)S(1)}, u32[]{:S(2)}, u32[]{:S(2)}) collective-permute-start(f32[256,128]{1,0:T(8,128)S(1)} %shard_map.163.refs_6_), channel_id=1, source_target_pairs={{0,4},{1,5},{2,6},{3,7},{4,0},{5,1},{6,2},{7,3},{8,12},{9,13},{10,... | collective-permute-start | bytes 393224 | tf_op jit(solution)/shard_map/ppermute | solution.py:31
  29.0 4.7 %collective-permute-start.18 = (f32[8,512]{1,0:T(8,128)S(1)}, f32[8,512]{1,0:T(8,128)S(1)}, u32[]{:S(2)}, u32[]{:S(2)}) collective-permute-start(f32[8,512]{1,0:T(8,128)S(1)} %shard_map.165.refs_5_.refs_4_.refs_1_.refs_0_), channel_id=1, source_target_pairs={{0,16},{1,17},{2,18},{3,19},{4,20},{5,21},{6,22},{7,23},{8,24},{9,... | collective-permute-start | bytes 49160 | tf_op jit(solution)/shard_map/ppermute | solution.py:31

commit v6 on v5

--- a/solution.py
+++ b/solution.py
@@ -285,12 +285,18 @@
 
 def forward_body(sizes, owned, taken, rhs, inverse, lower, sep_rhs, places, coupling, forward, sums):
     count, block = inverse.shape[2], inverse.shape[3]
+    alone, steps = [], [None]
+    for counter in range(count):
+        pieces = halves(inverse[0, 0, counter])
+        alone.append(times(rhs[0, 0, :, counter * block : (counter + 1) * block], pieces, False))
+        if counter > 0:
+            steps.append(halves(times(lower[0, 0, counter - 1], pieces, False)))
     earlier = None
     for counter in range(count):
-        current = rhs[0, 0, :, counter * block : (counter + 1) * block]
+        current = alone[counter]
         if counter > 0:
-            current = current - times(earlier, halves(lower[0, 0, counter - 1]), False)
-        earlier = times(current, halves(inverse[0, 0, counter]), False)
+            current = current - times(earlier, steps[counter], False)
+        earlier = current
         forward[:, counter * block : (counter + 1) * block] = earlier
     whole = forward[...]
     own = times(sep_rhs[0, 0], [one_hot(own_targets(sizes, owned, taken), sum(sizes))], True)
@@ -342,6 +348,11 @@
 def top_body(total, f_high, f_low, partial):
     pieces = [f_high[...], f_low[...]]
     partial[...] = times(times(total[...], pieces, True), pieces, False)
+
+
+def last_top_body(total, earlier, f_high, f_low, partial):
+    pieces = [f_high[...], f_low[...]]
+    partial[...] = earlier[...] + times(times(total[...], pieces, True), pieces, False)
 
 
 def join_body(moves, *refs):
@@ -590,12 +601,17 @@
     theirs = from_partner(sums, axes, first)
     folded_two = fold(1, two_level, (sums,))
     arrive(from_third, top_at, (sums,), F1C_US)
+    table = level(0, both[:-2], (sums,))
     (sums,) = vmem_call(
         add_body, [((rhs_count, sizes[0]), jnp.float32)], sums, theirs, microseconds=SUM_US,
-        after=(folded_two[0],),
+        after=(folded_two[0], table[0]),
+    )
+    (near_part,) = vmem_call(
+        top_body, [((rhs_count, sizes[0]), jnp.float32)], sums, *table, microseconds=0.4
     )
     (partial,) = vmem_call(
-        top_body, [((rhs_count, sizes[0]), jnp.float32)], sums, *level(0, both, (sums,)), microseconds=0.5
+        last_top_body, [((rhs_count, sizes[0]), jnp.float32)],
+        sums, near_part, *level(0, both[-2:], (near_part,)), microseconds=0.4,
     )
     theirs = from_partner(partial, axes, first)
     solved_second = solve((2, 3), False, (partial,))

time: 35.3 us -> 35.3 us (level)
    pallas_call x30 -> x32, Pallas kernels: 10.6 us -> 10.5 us  [vmem_call(): pl.pallas_call(kernel, out_shape=out_shape, in_specs=[pl.BlockSpec(memory...]
  transfers between devices with their start and end apart: 19 -> 19, of which waited for: 8 -> 7; matrix products, arithmetic and copies ran while one was open for 0% -> 0% of each run, Pallas kernels for 22% -> 22%
where the time goes in v6:
time: 35.3 us; the launch traced here: 35 us
  starting transfers between devices  19.3 us (55%)
  Pallas kernels  10.5 us (30%)
  waiting for transfers between devices  4.29 us (12%)
  between operations  0.93 us (3%)
    ppermute x19, starting transfers between devices, from_partner(): lax.ppermute(value, axis, [(i, i ^ 1 << distance) for i in range(lax.axis...  19.3 us
    pallas_call x32, Pallas kernels, vmem_call(): pl.pallas_call(kernel, out_shape=out_shape, in_specs=[pl.BlockSpec(memory...  10.5 us
    ppermute x19, waiting for transfers between devices, from_partner(): lax.ppermute(value, axis, [(i, i ^ 1 << distance) for i in range(lax.axis...  4.29 us
  transfers between devices with their start and end apart: 19, of which 7 were waited for; matrix products, arithmetic and copies ran while one was open for 0% of the time, Pallas kernels for 22%

profile of v6, /device:TPU:0, one launch (start us, length us, event | category | flops | bytes accessed | tf_op | source)
XLA Modules:
  0.0 35.0 jit_solution(11601907539793731593)
XLA Ops:
  0.6 0.0 copy-start
  0.6 0.0 copy-start.2
  0.7 0.0 copy-start.1
  0.7 0.0 copy-start.4
  0.7 1.0 %shard_map.141 = (f32[280,128]{1,0:T(8,128)S(1)}, f32[152,128]{1,0:T(8,128)S(1)}) custom-call(f32[1,1,16,512]{3,2,1,0:T(8,128)} %refs_0_.4, f32[1,1,16,256]{3,2,1,0:T(8,128)} %refs_1_.5, f32[1,1,32,256]{3,2,1,0:T(8,128)} %refs_2_.5, f32[1,1,32,128]{3,2,1,0:T(8,128)} %refs_3_.5, f32[1,1,16,128]{3,2,1,0:T(8,128)} %refs_4_.3, f32[1,1,32,128]{3,2,1,0:T(8,128)} %refs_5_.3, ...), custom_call_target="tpu_custom_call" | custom-call | flops 1000000000 | tf_op jit(solution)/shard_map/pallas_call | solution.py:213
  1.7 0.0 copy-start.5
  1.7 3.1 %collective-permute-start.1 = (f32[152,128]{1,0:T(8,128)S(1)}, f32[152,128]{1,0:T(8,128)S(1)}, u32[]{:S(2)}, u32[]{:S(2)}) collective-permute-start(f32[152,128]{1,0:T(8,128)S(1)} %get-tuple-element.49), channel_id=1, source_target_pairs={{0,8},{1,9},{2,10},{3,11},{4,12},{5,13},{6,14},{7,15},{8,0},{9,1},... | collective-permute-start | bytes 233480 | tf_op jit(solution)/shard_map/ppermute | solution.py:31
  4.8 1.5 %collective-permute-start.4 = (f32[280,128]{1,0:T(8,128)S(1)}, f32[280,128]{1,0:T(8,128)S(1)}, u32[]{:S(2)}, u32[]{:S(2)}) collective-permute-start(f32[280,128]{1,0:T(8,128)S(1)} %get-tuple-element.50.refs_0_), channel_id=1, source_target_pairs={{0,1},{1,0},{2,3},{3,2},{4,5},{5,4},{6,7},{7,6},{8,9},{9,8},{10,11... | collective-permute-start | bytes 430088 | tf_op jit(solution)/shard_map/ppermute | solution.py:31
  6.3 0.0 copy-done
  6.3 0.0 copy-done.3
  6.3 0.0 copy-done.5
  6.3 1.1 %shard_map.140 = (f32[8,512]{1,0:T(8,128)S(1)}, f32[8,1152]{1,0:T(8,128)S(1)}) custom-call(f32[1,1,8,512]{3,2,1,0:T(8,128)S(1)} %copy-done.3, f32[1,1,4,128,128]{4,3,2,1,0:T(8,128)S(1)} %copy-done.1, f32[1,1,3,128,128]{4,3,2,1,0:T(8,128)S(1)} %copy-done.2, f32[1,1,8,96]{3,2,1,0:T(8,128)S(1)} %copy-done.4, s32[1,1,4,128]{3,2,1,0:T(4,128)S(1)} %copy-done.5, ...), custom_call_target="tpu_custom_call" | custom-call | flops 2000000000 | tf_op jit(solution)/shard_map/pallas_call | solution.py:213
  7.4 0.1 collective-permute-start
  7.5 0.5 %collective-permute-start.3 = (f32[280,128]{1,0:T(8,128)S(1)}, f32[280,128]{1,0:T(8,128)S(1)}, u32[]{:S(2)}, u32[]{:S(2)}) collective-permute-start(f32[280,128]{1,0:T(8,128)S(1)} %get-tuple-element.50.refs_0_), channel_id=1, source_target_pairs={{0,4},{1,5},{2,6},{3,7},{4,0},{5,1},{6,2},{7,3},{8,12},{9,13},{10,... | collective-permute-start | bytes 430088 | tf_op jit(solution)/shard_map/ppermute | solution.py:31
  8.0 0.0 collective-permute-done.1.refs_0_
  8.0 0.7 %collective-permute-done.refs_1_ = f32[8,1152]{1,0:T(8,128)S(1)} collective-permute-done((f32[8,1152]{1,0:T(8,128)S(1)}, f32[8,1152]{1,0:T(8,128)S(1)}, u32[]{:S(2)}, u32[]{:S(2)}) %collective-permute-start) | collective-permute-done | bytes 36896 | tf_op jit(solution)/shard_map/ppermute | solution.py:31
  8.7 1.3 %collective-permute-done.4.refs_0_ = f32[280,128]{1,0:T(8,128)S(1)} collective-permute-done((f32[280,128]{1,0:T(8,128)S(1)}, f32[280,128]{1,0:T(8,128)S(1)}, u32[]{:S(2)}, u32[]{:S(2)}) %collective-permute-start.4) | collective-permute-done | bytes 143392 | tf_op jit(solution)/shard_map/ppermute | solution.py:31
  10.0 0.1 collective-permute-start.5
  10.1 1.6 %collective-permute-start.2 = (f32[8,1152]{1,0:T(8,128)S(1)}, f32[8,1152]{1,0:T(8,128)S(1)}, u32[]{:S(2)}, u32[]{:S(2)}) collective-permute-start(f32[8,1152]{1,0:T(8,128)S(1)} %shard_map.143.refs_1_.refs_0_.refs_2_), channel_id=1, source_target_pairs={{0,1},{1,0},{2,3},{3,2},{4,5},{5,4},{6,7},{7,6},{8,9},{9,8},{10,11... | collective-permute-start | bytes 110600 | tf_op jit(solution)/shard_map/ppermute | solution.py:31
  11.7 0.2 collective-permute-start.7
  11.8 0.5 %collective-permute-start.8 = (f32[152,128]{1,0:T(8,128)S(1)}, f32[152,128]{1,0:T(8,128)S(1)}, u32[]{:S(2)}, u32[]{:S(2)}) collective-permute-start(f32[152,128]{1,0:T(8,128)S(1)} %shard_map.147), channel_id=1, source_target_pairs={{0,1},{1,0},{2,3},{3,2},{4,5},{5,4},{6,7},{7,6},{8,9},{9,8},{10,11... | collective-permute-start | bytes 233480 | tf_op jit(solution)/shard_map/ppermute | solution.py:31
  12.4 0.0 collective-permute-done.3.refs_1_
  12.4 1.6 %collective-permute-start.11 = (f32[240,128]{1,0:T(8,128)S(1)}, f32[240,128]{1,0:T(8,128)S(1)}, u32[]{:S(2)}, u32[]{:S(2)}) collective-permute-start(f32[240,128]{1,0:T(8,128)S(1)} %shard_map.152), channel_id=1, source_target_pairs={{0,2},{1,3},{2,0},{3,1},{4,6},{5,7},{6,4},{7,5},{8,10},{9,11},{10,... | collective-permute-start | bytes 368648 | tf_op jit(solution)/shard_map/ppermute | solution.py:31
  14.0 0.0 collective-permute-done.5.refs_3_.refs_5_
  14.0 0.2 shard_map.145
  14.2 0.0 collective-permute-done.2.refs_1_
  14.2 0.3 shard_map.146
  14.6 0.5 %collective-permute-start.6 = (f32[8,1024]{1,0:T(8,128)S(1)}, f32[8,1024]{1,0:T(8,128)S(1)}, u32[]{:S(2)}, u32[]{:S(2)}) collective-permute-start(f32[8,1024]{1,0:T(8,128)S(1)} %get-tuple-element.55.refs_4_.refs_0_.refs_2_), channel_id=1, source_target_pairs={{0,8},{1,9},{2,10},{3,11},{4,12},{5,13},{6,14},{7,15},{8,0},{9,1},... | collective-permute-start | bytes 98312 | tf_op jit(solution)/shard_map/ppermute | solution.py:31
  15.0 1.0 %shard_map.148 = (f32[8,512]{1,0:T(8,128)S(1)}, bf16[256,512]{1,0:T(8,128)(2,1)S(1)}, bf16[256,512]{1,0:T(8,128)(2,1)S(1)}) custom-call(f32[8,512]{1,0:T(8,128)S(1)} %get-tuple-element.56.refs_0_, f32[1,1,4,128,512]{4,3,2,1,0:T(8,128)S(1)} %copy-done, f32[1,1,4,128,128]{4,3,2,1,0:T(8,128)S(1)} %copy-done.1, f32[1,1,3,128,128]{4,3,2,1,0:T(8,128)S(1)} %copy-done.2, ...), custom_call_target="tpu_custom_call" | custom-call | flops 1000000000 | tf_op jit(solution)/shard_map/pallas_call | solution.py:213
  16.0 0.4 %collective-permute-done.8.refs_0_ = f32[152,128]{1,0:T(8,128)S(1)} collective-permute-done((f32[152,128]{1,0:T(8,128)S(1)}, f32[152,128]{1,0:T(8,128)S(1)}, u32[]{:S(2)}, u32[]{:S(2)}) %collective-permute-start.8) | collective-permute-done | bytes 77856 | tf_op jit(solution)/shard_map/ppermute | solution.py:31
  16.5 0.1 collective-permute-start.9
  16.5 1.6 %collective-permute-start.13 = (f32[112,128]{1,0:T(8,128)S(1)}, f32[112,128]{1,0:T(8,128)S(1)}, u32[]{:S(2)}, u32[]{:S(2)}) collective-permute-start(f32[112,128]{1,0:T(8,128)S(1)} %shard_map.153.refs_1_), channel_id=1, source_target_pairs={{0,2},{1,3},{2,0},{3,1},{4,6},{5,7},{6,4},{7,5},{8,10},{9,11},{10,... | collective-permute-start | bytes 172040 | tf_op jit(solution)/shard_map/ppermute | solution.py:31
  18.1 0.0 collective-permute-done.11.refs_0_
  18.1 0.2 collective-permute-start.12
  18.4 0.0 collective-permute-done.7.refs_3_
  18.4 0.0 collective-permute-done.9.refs_7_
  18.4 0.3 shard_map.150
  18.7 0.0 collective-permute-done.6.refs_1_
  18.7 0.4 %shard_map.151 = (f32[8,768]{1,0:T(8,128)S(1)}, f32[8,256]{1,0:T(8,128)S(1)}) custom-call(f32[8,1024]{1,0:T(8,128)S(1)} %get-tuple-element.55.refs_4_.refs_0_.refs_2_, f32[8,1024]{1,0:T(8,128)S(1)} %collective-permute-done.6.refs_1_, bf16[256,256]{1,0:T(8,128)(2,1)S(1)} %get-tuple-element.58.refs_2_.refs_1_, ...), custom_call_target="tpu_custom_call" | custom-call | flops 5000000000 | tf_op jit(solution)/shard_map/pallas_call | solution.py:213
  19.1 1.2 %collective-permute-start.10 = (f32[8,768]{1,0:T(8,128)S(1)}, f32[8,768]{1,0:T(8,128)S(1)}, u32[]{:S(2)}, u32[]{:S(2)}) collective-permute-start(f32[8,768]{1,0:T(8,128)S(1)} %get-tuple-element.62.refs_10_.refs_5_.refs_0_.refs_3_), channel_id=1, source_target_pairs={{0,2},{1,3},{2,0},{3,1},{4,6},{5,7},{6,4},{7,5},{8,10},{9,11},{10,... | collective-permute-start | bytes 73736 | tf_op jit(solution)/shard_map/ppermute | solution.py:31
  20.3 0.0 collective-permute-done.12.refs_9_.refs_5_
  20.3 0.6 %shard_map.155 = (bf16[192,256]{1,0:T(8,128)(2,1)S(1)}, bf16[192,256]{1,0:T(8,128)(2,1)S(1)}, bf16[192,512]{1,0:T(8,128)(2,1)S(1)}, bf16[192,512]{1,0:T(8,128)(2,1)S(1)}) custom-call(f32[280,128]{1,0:T(8,128)S(1)} %get-tuple-element.50.refs_0_, f32[280,128]{1,0:T(8,128)S(1)} %collective-permute-done.3.refs_1_, f32[152,128]{1,0:T(8,128)S(1)} %shard_map.142.refs_2_.refs_0_, ...), custom_call_target="tpu_custom_call" | custom-call | flops 400000000 | tf_op jit(solution)/shard_map/pallas_call | solution.py:213
  20.9 0.0 collective-permute-done.13.refs_0_
  20.9 0.1 collective-permute-start.14
  21.1 1.1 %collective-permute-start.16 = (f32[256,128]{1,0:T(8,128)S(1)}, f32[256,128]{1,0:T(8,128)S(1)}, u32[]{:S(2)}, u32[]{:S(2)}) collective-permute-start(f32[256,128]{1,0:T(8,128)S(1)} %shard_map.164), channel_id=1, source_target_pairs={{0,8},{1,9},{2,10},{3,11},{4,12},{5,13},{6,14},{7,15},{8,0},{9,1},... | collective-permute-start | bytes 393224 | tf_op jit(solution)/shard_map/ppermute | solution.py:31
  22.1 0.3 shard_map.158
  22.5 0.0 collective-permute-done.14.refs_1_
  22.5 0.3 shard_map.157
  22.8 0.2 collective-permute-done.10.refs_1_
  23.0 0.4 %shard_map.159 = (f32[8,512]{1,0:T(8,128)S(1)}, f32[8,256]{1,0:T(8,128)S(1)}) custom-call(f32[8,768]{1,0:T(8,128)S(1)} %get-tuple-element.62.refs_10_.refs_5_.refs_0_.refs_3_, f32[8,768]{1,0:T(8,128)S(1)} %collective-permute-done.10.refs_1_, bf16[192,256]{1,0:T(8,128)(2,1)S(1)} %get-tuple-element.63.refs_1_.refs_2_, ...), custom_call_target="tpu_custom_call" | custom-call | flops 5000000000 | tf_op jit(solution)/shard_map/pallas_call | solution.py:213
  23.4 2.7 %collective-permute-start.15 = (f32[8,512]{1,0:T(8,128)S(1)}, f32[8,512]{1,0:T(8,128)S(1)}, u32[]{:S(2)}, u32[]{:S(2)}) collective-permute-start(f32[8,512]{1,0:T(8,128)S(1)} %get-tuple-element.73.refs_9_.refs_6_.refs_0_.refs_1_), channel_id=1, source_target_pairs={{0,16},{1,17},{2,18},{3,19},{4,20},{5,21},{6,22},{7,23},{8,24},{9,... | collective-permute-start | bytes 49160 | tf_op jit(solution)/shard_map/ppermute | solution.py:31
  26.0 0.8 %shard_map.160 = (f32[8,256]{1,0:T(8,128)S(1)}, bf16[512,256]{1,0:T(8,128)(2,1)S(1)}, bf16[512,256]{1,0:T(8,128)(2,1)S(1)}) custom-call(f32[8,256]{1,0:T(8,128)S(1)} %get-tuple-element.74.refs_0_, bf16[192,256]{1,0:T(8,128)(2,1)S(1)} %get-tuple-element.63.refs_1_.refs_2_, bf16[192,256]{1,0:T(8,128)(2,1)S(1)} %get-tuple-element.64.refs_3_.refs_2_, ...), custom_call_target="tpu_custom_call" | custom-call | flops 500000000 | tf_op jit(solution)/shard_map/pallas_call | solution.py:213
  26.9 0.1 collective-permute-done.16.refs_0_
  27.0 0.1 collective-permute-start.17
  27.1 1.0 %collective-permute-done.15.refs_1_ = f32[8,512]{1,0:T(8,128)S(1)} collective-permute-done((f32[8,512]{1,0:T(8,128)S(1)}, f32[8,512]{1,0:T(8,128)S(1)}, u32[]{:S(2)}, u32[]{:S(2)}) %collective-permute-start.15) | collective-permute-done | bytes 16416 | tf_op jit(solution)/shard_map/ppermute | solution.py:31
  28.1 0.4 %shard_map.163.refs_2_.refs_1_ = f32[8,512]{1,0:T(8,128)S(1)} custom-call(f32[8,512]{1,0:T(8,128)S(1)} %shard_map.162.refs_0_, bf16[128,512]{1,0:T(8,128)(2,1)S(1)} %get-tuple-element.76.refs_3_.refs_1_, bf16[128,512]{1,0:T(8,128)(2,1)S(1)} %get-tuple-element.77.refs_2_), custom_call_target="tpu_custom_call" | custom-call | flops 400000000 | tf_op jit(solution)/shard_map/pallas_call | solution.py:213
  28.5 0.0 collective-permute-done.17.refs_1_
  28.5 0.4 %shard_map.167.refs_5_.refs_4_.refs_1_.refs_0_ = f32[8,512]{1,0:T(8,128)S(1)} custom-call(f32[8,512]{1,0:T(8,128)S(1)} %shard_map.162.refs_0_, f32[8,512]{1,0:T(8,128)S(1)} %shard_map.163.refs_2_.refs_1_, bf16[128,512]{1,0:T(8,128)(2,1)S(1)} %get-tuple-element.78.refs_2_, bf16[128,512]{1,0:T(8,128)(2,1)S(1)} %get-tuple-element.79.refs_3_), custom_call_target="tpu_custom_call" | custom-call | flops 400000000 | tf_op jit(solution)/shard_map/pallas_call | solution.py:213
  28.9 2.8 %collective-permute-start.18 = (f32[8,512]{1,0:T(8,128)S(1)}, f32[8,512]{1,0:T(8,128)S(1)}, u32[]{:S(2)}, u32[]{:S(2)}) collective-permute-start(f32[8,512]{1,0:T(8,128)S(1)} %shard_map.167.refs_5_.refs_4_.refs_1_.refs_0_), channel_id=1, source_target_pairs={{0,16},{1,17},{2,18},{3,19},{4,20},{5,21},{6,22},{7,23},{8,24},{9,... | collective-permute-start | bytes 49160 | tf_op jit(solution)/shard_map/ppermute | solution.py:31
  31.7 1.0 %shard_map.169 = (bf16[256,512]{1,0:T(8,128)(2,1)S(1)}, bf16[256,512]{1,0:T(8,128)(2,1)S(1)}) custom-call(f32[8,512]{1,0:T(8,128)S(1)} %get-tuple-element.56.refs_0_, f32[1,1,4,128,512]{4,3,2,1,0:T(8,128)S(1)} %copy-done, f32[1,1,4,128,128]{4,3,2,1,0:T(8,128)S(1)} %copy-done.1, f32[1,1,3,128,128]{4,3,2,1,0:T(8,128)S(1)} %copy-done.2, ...), custom_call_target="tpu_custom_call" | custom-call | flops 1000000000 | tf_op jit(solution)/shard_map/pallas_call | solution.py:213
  32.7 0.3 shard_map.168
  32.9 0.1 shard_map.170
  33.1 0.5 %collective-permute-done.18.refs_1_ = f32[8,512]{1,0:T(8,128)S(1)} collective-permute-done((f32[8,512]{1,0:T(8,128)S(1)}, f32[8,512]{1,0:T(8,128)S(1)}, u32[]{:S(2)}, u32[]{:S(2)}) %collective-permute-start.18) | collective-permute-done | bytes 16416 | tf_op jit(solution)/shard_map/ppermute | solution.py:31
  33.6 1.4 %shard_map.171 = (f32[1,1,8,512]{3,2,1,0:T(8,128)}, f32[1,1,8,96]{3,2,1,0:T(8,128)}) custom-call(f32[8,512]{1,0:T(8,128)S(1)} %shard_map.167.refs_5_.refs_4_.refs_1_.refs_0_, f32[8,512]{1,0:T(8,128)S(1)} %collective-permute-done.18.refs_1_, f32[8,256]{1,0:T(8,128)S(1)} %get-tuple-element.75.refs_2_, bf16[512,256]{1,0:T(8,128)(2,1)S(1)} %get-tuple-element.80.refs_3_, ...), custom_call_target="tpu_custom_call" | custom-call | flops 2000000000 | tf_op jit(solution)/shard_map/pallas_call | solution.py:213
  (18 shorter events, 0.2 us)
Async XLA Ops:
  0.6 5.7 %copy-start = (f32[1,1,4,128,512]{4,3,2,1,0:T(8,128)S(1)}, f32[1,1,4,128,512]{4,3,2,1,0:T(8,128)}, u32[]{:S(2)}) copy-start(f32[1,1,4,128,512]{4,3,2,1,0:T(8,128)} %refs_1_.7) | copy-start | bytes 3145732
  0.6 5.6 %copy-start.2 = (f32[1,1,3,128,128]{4,3,2,1,0:T(8,128)S(1)}, f32[1,1,3,128,128]{4,3,2,1,0:T(8,128)}, u32[]{:S(2)}) copy-start(f32[1,1,3,128,128]{4,3,2,1,0:T(8,128)} %refs_3_.7) | copy-start | bytes 589828
  0.7 5.6 %copy-start.1 = (f32[1,1,4,128,128]{4,3,2,1,0:T(8,128)S(1)}, f32[1,1,4,128,128]{4,3,2,1,0:T(8,128)}, u32[]{:S(2)}) copy-start(f32[1,1,4,128,128]{4,3,2,1,0:T(8,128)} %refs_2_.7) | copy-start | bytes 786436
  0.7 5.6 %copy-start.4 = (f32[1,1,8,96]{3,2,1,0:T(8,128)S(1)}, f32[1,1,8,96]{3,2,1,0:T(8,128)}, u32[]{:S(2)}) copy-start(f32[1,1,8,96]{3,2,1,0:T(8,128)} %refs_3_.4) | copy-start | bytes 9220
  0.7 5.6 %copy-start.3 = (f32[1,1,8,512]{3,2,1,0:T(8,128)S(1)}, f32[1,1,8,512]{3,2,1,0:T(8,128)}, u32[]{:S(2)}) copy-start(f32[1,1,8,512]{3,2,1,0:T(8,128)} %refs_0_.3) | copy-start | bytes 49156
  1.7 4.6 %copy-start.5 = (s32[1,1,4,128]{3,2,1,0:T(4,128)S(1)}, s32[1,1,4,128]{3,2,1,0:T(4,128)}, u32[]{:S(2)}) copy-start(s32[1,1,4,128]{3,2,1,0:T(4,128)} %refs_0_.5) | copy-start | bytes 6148
  1.7 6.3 %collective-permute-start.1 = (f32[152,128]{1,0:T(8,128)S(1)}, f32[152,128]{1,0:T(8,128)S(1)}, u32[]{:S(2)}, u32[]{:S(2)}) collective-permute-start(f32[152,128]{1,0:T(8,128)S(1)} %get-tuple-element.49), channel_id=1, source_target_pairs={{0,8},{1,9},{2,10},{3,11},{4,12},{5,13},{6,14},{7,15},{8,0},{9,1},... | collective-permute-start | bytes 233480 | tf_op jit(solution)/shard_map/ppermute | solution.py:31
  4.8 5.2 %collective-permute-start.4 = (f32[280,128]{1,0:T(8,128)S(1)}, f32[280,128]{1,0:T(8,128)S(1)}, u32[]{:S(2)}, u32[]{:S(2)}) collective-permute-start(f32[280,128]{1,0:T(8,128)S(1)} %get-tuple-element.50.refs_0_), channel_id=1, source_target_pairs={{0,1},{1,0},{2,3},{3,2},{4,5},{5,4},{6,7},{7,6},{8,9},{9,8},{10,11... | collective-permute-start | bytes 430088 | tf_op jit(solution)/shard_map/ppermute | solution.py:31
  7.4 1.3 %collective-permute-start = (f32[8,1152]{1,0:T(8,128)S(1)}, f32[8,1152]{1,0:T(8,128)S(1)}, u32[]{:S(2)}, u32[]{:S(2)}) collective-permute-start(f32[8,1152]{1,0:T(8,128)S(1)} %get-tuple-element.48.refs_0_), channel_id=1, source_target_pairs={{0,4},{1,5},{2,6},{3,7},{4,0},{5,1},{6,2},{7,3},{8,12},{9,13},{10,... | collective-permute-start | bytes 110600 | tf_op jit(solution)/shard_map/ppermute | solution.py:31
  7.5 4.9 %collective-permute-start.3 = (f32[280,128]{1,0:T(8,128)S(1)}, f32[280,128]{1,0:T(8,128)S(1)}, u32[]{:S(2)}, u32[]{:S(2)}) collective-permute-start(f32[280,128]{1,0:T(8,128)S(1)} %get-tuple-element.50.refs_0_), channel_id=1, source_target_pairs={{0,4},{1,5},{2,6},{3,7},{4,0},{5,1},{6,2},{7,3},{8,12},{9,13},{10,... | collective-permute-start | bytes 430088 | tf_op jit(solution)/shard_map/ppermute | solution.py:31
  10.0 4.0 %collective-permute-start.5 = (f32[280,128]{1,0:T(8,128)S(1)}, f32[280,128]{1,0:T(8,128)S(1)}, u32[]{:S(2)}, u32[]{:S(2)}) collective-permute-start(f32[280,128]{1,0:T(8,128)S(1)} %shard_map.144.refs_2_.refs_4_.refs_1_), channel_id=1, source_target_pairs={{0,4},{1,5},{2,6},{3,7},{4,0},{5,1},{6,2},{7,3},{8,12},{9,13},{10,... | collective-permute-start | bytes 430088 | tf_op jit(solution)/shard_map/ppermute | solution.py:31
  10.1 4.1 %collective-permute-start.2 = (f32[8,1152]{1,0:T(8,128)S(1)}, f32[8,1152]{1,0:T(8,128)S(1)}, u32[]{:S(2)}, u32[]{:S(2)}) collective-permute-start(f32[8,1152]{1,0:T(8,128)S(1)} %shard_map.143.refs_1_.refs_0_.refs_2_), channel_id=1, source_target_pairs={{0,1},{1,0},{2,3},{3,2},{4,5},{5,4},{6,7},{7,6},{8,9},{9,8},{10,11... | collective-permute-start | bytes 110600 | tf_op jit(solution)/shard_map/ppermute | solution.py:31
  11.7 6.7 %collective-permute-start.7 = (f32[152,128]{1,0:T(8,128)S(1)}, f32[152,128]{1,0:T(8,128)S(1)}, u32[]{:S(2)}, u32[]{:S(2)}) collective-permute-start(f32[152,128]{1,0:T(8,128)S(1)} %shard_map.142.refs_2_.refs_0_), channel_id=1, source_target_pairs={{0,4},{1,5},{2,6},{3,7},{4,0},{5,1},{6,2},{7,3},{8,12},{9,13},{10,... | collective-permute-start | bytes 233480 | tf_op jit(solution)/shard_map/ppermute | solution.py:31
  11.8 4.6 %collective-permute-start.8 = (f32[152,128]{1,0:T(8,128)S(1)}, f32[152,128]{1,0:T(8,128)S(1)}, u32[]{:S(2)}, u32[]{:S(2)}) collective-permute-start(f32[152,128]{1,0:T(8,128)S(1)} %shard_map.147), channel_id=1, source_target_pairs={{0,1},{1,0},{2,3},{3,2},{4,5},{5,4},{6,7},{7,6},{8,9},{9,8},{10,11... | collective-permute-start | bytes 233480 | tf_op jit(solution)/shard_map/ppermute | solution.py:31
  12.4 5.7 %collective-permute-start.11 = (f32[240,128]{1,0:T(8,128)S(1)}, f32[240,128]{1,0:T(8,128)S(1)}, u32[]{:S(2)}, u32[]{:S(2)}) collective-permute-start(f32[240,128]{1,0:T(8,128)S(1)} %shard_map.152), channel_id=1, source_target_pairs={{0,2},{1,3},{2,0},{3,1},{4,6},{5,7},{6,4},{7,5},{8,10},{9,11},{10,... | collective-permute-start | bytes 368648 | tf_op jit(solution)/shard_map/ppermute | solution.py:31
  14.6 4.1 %collective-permute-start.6 = (f32[8,1024]{1,0:T(8,128)S(1)}, f32[8,1024]{1,0:T(8,128)S(1)}, u32[]{:S(2)}, u32[]{:S(2)}) collective-permute-start(f32[8,1024]{1,0:T(8,128)S(1)} %get-tuple-element.55.refs_4_.refs_0_.refs_2_), channel_id=1, source_target_pairs={{0,8},{1,9},{2,10},{3,11},{4,12},{5,13},{6,14},{7,15},{8,0},{9,1},... | collective-permute-start | bytes 98312 | tf_op jit(solution)/shard_map/ppermute | solution.py:31
  16.5 1.9 %collective-permute-start.9 = (f32[152,128]{1,0:T(8,128)S(1)}, f32[152,128]{1,0:T(8,128)S(1)}, u32[]{:S(2)}, u32[]{:S(2)}) collective-permute-start(f32[152,128]{1,0:T(8,128)S(1)} %shard_map.149.refs_6_.refs_1_), channel_id=1, source_target_pairs={{0,4},{1,5},{2,6},{3,7},{4,0},{5,1},{6,2},{7,3},{8,12},{9,13},{10,... | collective-permute-start | bytes 233480 | tf_op jit(solution)/shard_map/ppermute | solution.py:31
  16.5 4.4 %collective-permute-start.13 = (f32[112,128]{1,0:T(8,128)S(1)}, f32[112,128]{1,0:T(8,128)S(1)}, u32[]{:S(2)}, u32[]{:S(2)}) collective-permute-start(f32[112,128]{1,0:T(8,128)S(1)} %shard_map.153.refs_1_), channel_id=1, source_target_pairs={{0,2},{1,3},{2,0},{3,1},{4,6},{5,7},{6,4},{7,5},{8,10},{9,11},{10,... | collective-permute-start | bytes 172040 | tf_op jit(solution)/shard_map/ppermute | solution.py:31
  18.1 2.2 %collective-permute-start.12 = (f32[240,128]{1,0:T(8,128)S(1)}, f32[240,128]{1,0:T(8,128)S(1)}, u32[]{:S(2)}, u32[]{:S(2)}) collective-permute-start(f32[240,128]{1,0:T(8,128)S(1)} %shard_map.154.refs_8_.refs_4_.refs_2_), channel_id=1, source_target_pairs={{0,4},{1,5},{2,6},{3,7},{4,0},{5,1},{6,2},{7,3},{8,12},{9,13},{10,... | collective-permute-start | bytes 368648 | tf_op jit(solution)/shard_map/ppermute | solution.py:31
  19.1 3.8 %collective-permute-start.10 = (f32[8,768]{1,0:T(8,128)S(1)}, f32[8,768]{1,0:T(8,128)S(1)}, u32[]{:S(2)}, u32[]{:S(2)}) collective-permute-start(f32[8,768]{1,0:T(8,128)S(1)} %get-tuple-element.62.refs_10_.refs_5_.refs_0_.refs_3_), channel_id=1, source_target_pairs={{0,2},{1,3},{2,0},{3,1},{4,6},{5,7},{6,4},{7,5},{8,10},{9,11},{10,... | collective-permute-start | bytes 73736 | tf_op jit(solution)/shard_map/ppermute | solution.py:31
  20.9 1.6 %collective-permute-start.14 = (f32[112,128]{1,0:T(8,128)S(1)}, f32[112,128]{1,0:T(8,128)S(1)}, u32[]{:S(2)}, u32[]{:S(2)}) collective-permute-start(f32[112,128]{1,0:T(8,128)S(1)} %shard_map.156.refs_0_), channel_id=1, source_target_pairs={{0,4},{1,5},{2,6},{3,7},{4,0},{5,1},{6,2},{7,3},{8,12},{9,13},{10,... | collective-permute-start | bytes 172040 | tf_op jit(solution)/shard_map/ppermute | solution.py:31
  21.1 5.9 %collective-permute-start.16 = (f32[256,128]{1,0:T(8,128)S(1)}, f32[256,128]{1,0:T(8,128)S(1)}, u32[]{:S(2)}, u32[]{:S(2)}) collective-permute-start(f32[256,128]{1,0:T(8,128)S(1)} %shard_map.164), channel_id=1, source_target_pairs={{0,8},{1,9},{2,10},{3,11},{4,12},{5,13},{6,14},{7,15},{8,0},{9,1},... | collective-permute-start | bytes 393224 | tf_op jit(solution)/shard_map/ppermute | solution.py:31
  23.4 4.7 %collective-permute-start.15 = (f32[8,512]{1,0:T(8,128)S(1)}, f32[8,512]{1,0:T(8,128)S(1)}, u32[]{:S(2)}, u32[]{:S(2)}) collective-permute-start(f32[8,512]{1,0:T(8,128)S(1)} %get-tuple-element.73.refs_9_.refs_6_.refs_0_.refs_1_), channel_id=1, source_target_pairs={{0,16},{1,17},{2,18},{3,19},{4,20},{5,21},{6,22},{7,23},{8,24},{9,... | collective-permute-start | bytes 49160 | tf_op jit(solution)/shard_map/ppermute | solution.py:31
  27.0 1.5 %collective-permute-start.17 = (f32[256,128]{1,0:T(8,128)S(1)}, f32[256,128]{1,0:T(8,128)S(1)}, u32[]{:S(2)}, u32[]{:S(2)}) collective-permute-start(f32[256,128]{1,0:T(8,128)S(1)} %shard_map.165.refs_0_), channel_id=1, source_target_pairs={{0,4},{1,5},{2,6},{3,7},{4,0},{5,1},{6,2},{7,3},{8,12},{9,13},{10,... | collective-permute-start | bytes 393224 | tf_op jit(solution)/shard_map/ppermute | solution.py:31
  28.9 4.7 %collective-permute-start.18 = (f32[8,512]{1,0:T(8,128)S(1)}, f32[8,512]{1,0:T(8,128)S(1)}, u32[]{:S(2)}, u32[]{:S(2)}) collective-permute-start(f32[8,512]{1,0:T(8,128)S(1)} %shard_map.167.refs_5_.refs_4_.refs_1_.refs_0_), channel_id=1, source_target_pairs={{0,16},{1,17},{2,18},{3,19},{4,20},{5,21},{6,22},{7,23},{8,24},{9,... | collective-permute-start | bytes 49160 | tf_op jit(solution)/shard_map/ppermute | solution.py:31
